TPU v7x, 32 devices: a whole 2x2x4 slice. The times are simulated.
32 devices in a mesh: req: 8 (over y, x, core), head: 4 (over z).
Axes of the slice: x: 2, y: 2, z: 4, core: 2. Of those that a mesh axis runs over, the one named last changes fastest.
Arguments:
- tokens: bfloat16 [1024, 1536], P(('req', 'head')), may hold values from -6 to 6
- pre_gain: float32 [1536], replicated, may hold values from 0.1 to 1.9
- inner_weight: bfloat16 [1536, 2, 3072], P(None, None, 'head')
- shared_weight: bfloat16 [1536, 304], replicated, may hold values from -0.15625 to 0.15625
- conv_inner: float32 [4, 3072], P(None, 'head'), may hold values from -0.5 to 0.5
- conv_inner_bias: float32 [3072], P('head'), may hold values from -0.5 to 0.5
- conv_shared: float32 [4, 256], replicated, may hold values from -0.5 to 0.5
- conv_shared_bias: float32 [256], replicated, may hold values from -0.5 to 0.5
- step_bias: float32 [48], P('head'), may hold values from -4 to 0
- decay_log: float32 [48], P('head'), may hold values from 0 to 2.77
- skip_gain: float32 [48], P('head'), may hold values from 0.5 to 1.5
- gate_gain: float32 [3072], P('head'), may hold values from 0.1 to 1.9
- out_weight: bfloat16 [3072, 1536], P('head'), may hold values from -0.109375 to 0.109375
- states: bfloat16 [256, 48, 64, 128], P('req', 'head'), may hold values from -1.1953125 to 1.1953125
- edge_inner: bfloat16 [256, 3, 3072], P('req', None, 'head'), may hold values from -6 to 6
- edge_shared: bfloat16 [256, 3, 256], P('req'), may hold values from -6 to 6
- counts: int32 [256], P('req'), may hold values from 1 to 4, as said below
- mig_ids: int32 [8], replicated, may hold values from 0 to 255, as said below
- mig_dest: int32 [8], replicated, may hold values from 0 to 255, as said below
- reorder: int32 [256], replicated, may hold values from 0 to 255, as said below
Outputs:
- hidden_out: bfloat16 [1024, 1536], P(('req', 'head'))
- states_out: bfloat16 [256, 48, 64, 128], P('req', 'head')
- edge_inner_out: bfloat16 [256, 3, 3072], P('req', None, 'head')
- edge_shared_out: bfloat16 [256, 3, 256], P('req')
Inputs may be any that keep to these rules, and one draw needn't show every extreme that they name: counts: each slot's token rows are r * 4 to r * 4 + 3 of tokens; the first counts[r] of them are real. mig_ids: distinct old slots listed by owner: entry i is one of the slots i * 32 to (i + 1) * 32 - 1, those held by index i of req. mig_dest: a reordering of the slots in mig_ids. reorder: a permutation of all slots. The 32 new slots j with j // 32 = d take at most 4 values reorder[j] of any one block of 32 slots, and exactly 4 of some block.
All inputs are finite; a program needn't handle non-finite values.
Results may differ from a plain program's by a relative error of at most 0.013.
Values may be sent and summed in bfloat16 or wider, within the bound.
No kernel may reach another device: no remote copies, remote signals or barrier semaphores. Data moves between devices by JAX's collectives and lax.ppermute only.
A program may use at most 128 MiB of HBM per device.

v0:
```python
import jax
import jax.numpy as jnp
from jax import lax
from jax.sharding import PartitionSpec as P

EPS = 1e-05


def advance(carried, step_now, inputs_now, entry_now, readout_now, decay, skip_gain):
    factor = jnp.exp(step_now * decay)
    carried = (
        carried * factor[:, :, None, None]
        + (step_now[:, :, None] * inputs_now)[:, :, :, None] * entry_now[:, None, None, :]
    )
    produced = jnp.einsum("khpn,kn->khp", carried, readout_now, precision=lax.Precision.HIGHEST)
    return (carried, produced + skip_gain[None, :, None] * inputs_now)


def depthwise(edge, fresh, weight, offset_bias):
    sequence = jnp.concatenate([edge, fresh], axis=1).astype(jnp.float32)
    window = fresh.shape[1]
    summed = sequence[:, 0:window] * weight[0]
    for offset in range(1, weight.shape[0]):
        summed = summed + sequence[:, offset : offset + window] * weight[offset]
    return jax.nn.silu(summed + offset_bias)


def new_edge(edge, fresh, counts):
    sequence = jnp.concatenate([edge, fresh], axis=1)
    keep_rows = edge.shape[1]
    result = edge
    for length in range(1, fresh.shape[1] + 1):
        result = jnp.where(
            (counts == length)[:, None, None], sequence[:, length : length + keep_rows], result
        )
    return result


def rank_rows(partner, position, capacity):
    matching = partner[:, None] == partner[None, :]
    earlier = position[None, :] < position[:, None]
    ranking = jnp.sum(jnp.logical_and(matching, earlier), axis=1)
    return partner * capacity + ranking


def pack_pages(member, send_rows, buffer_rows):
    empty = jnp.zeros((buffer_rows,) + member.shape[1:], member.dtype)
    return empty.at[send_rows].set(member)


def route_rows(anchor, first_slot, slot_count, all_slots, capacity):
    inverse = jnp.zeros(all_slots.shape, jnp.int32).at[anchor].set(all_slots)
    targets = lax.dynamic_slice_in_dim(inverse, first_slot, slot_count)
    send_rows = rank_rows(targets // slot_count, targets % slot_count, capacity)
    sources = lax.dynamic_slice_in_dim(anchor, first_slot, slot_count)
    recv_rows = rank_rows(sources // slot_count, jnp.arange(slot_count, dtype=jnp.int32), capacity)
    return (send_rows, recv_rows)


def local(
    tokens,
    pre_gain,
    inner_weight,
    shared_weight,
    conv_inner,
    conv_inner_bias,
    conv_shared,
    conv_shared_bias,
    step_bias,
    decay_log,
    skip_gain,
    gate_gain,
    out_weight,
    states,
    edge_inner,
    edge_shared,
    counts,
    mig_ids,
    mig_dest,
    reorder,
):
    slot_count = states.shape[0]
    heads_here = states.shape[1]
    head_dim = states.shape[2]
    state_dim = states.shape[3]
    inner_here = heads_here * head_dim
    groups = lax.axis_size("req")
    device = lax.axis_index("req")
    first_slot = device * slot_count
    moving = mig_ids.shape[0] // groups
    stride = (slot_count + groups - 1) // groups
    all_slots = jnp.arange(slot_count * groups, dtype=jnp.int32)
    rows_in = tokens.astype(jnp.float32)
    normed = (
        rows_in * lax.rsqrt(jnp.mean(rows_in * rows_in, axis=-1, keepdims=True) + EPS) * pre_gain
    ).astype(jnp.bfloat16)
    inner_flat = inner_weight.reshape(inner_weight.shape[0], 2 * inner_here)
    piece_rows = lax.all_gather(normed, "head", axis=0, tiled=True)
    inner_rows = jnp.dot(piece_rows, inner_flat, preferred_element_type=jnp.float32).astype(
        jnp.bfloat16
    )
    shared_rows = jnp.dot(piece_rows, shared_weight, preferred_element_type=jnp.float32).astype(
        jnp.bfloat16
    )
    projected = jnp.concatenate([inner_rows, shared_rows], axis=1)
    own_ids = lax.dynamic_slice_in_dim(mig_ids, device * moving, moving)
    local_ids = own_ids - first_slot
    arrived = (
        lax.all_gather(states[local_ids], "req", axis=0, tiled=True),
        lax.all_gather(edge_inner[local_ids], "req", axis=0, tiled=True),
        lax.all_gather(edge_shared[local_ids], "req", axis=0, tiled=True),
    )
    picked = jnp.argmax(mig_dest[None, :] == own_ids[:, None], axis=1)
    sectioned_states = states.at[local_ids].set(arrived[0][picked])
    sectioned_inner = edge_inner.at[local_ids].set(arrived[1][picked])
    sectioned_shared = edge_shared.at[local_ids].set(arrived[2][picked])
    send_rows, recv_rows = route_rows(reorder, first_slot, slot_count, all_slots, stride)
    buffer_rows = groups * stride
    received = (
        lax.all_to_all(
            pack_pages(sectioned_states, send_rows, buffer_rows),
            "req",
            split_axis=0,
            concat_axis=0,
            tiled=True,
        ),
        lax.all_to_all(
            pack_pages(sectioned_inner, send_rows, buffer_rows),
            "req",
            split_axis=0,
            concat_axis=0,
            tiled=True,
        ),
        lax.all_to_all(
            pack_pages(sectioned_shared, send_rows, buffer_rows),
            "req",
            split_axis=0,
            concat_axis=0,
            tiled=True,
        ),
    )
    moved_states = received[0][recv_rows]
    moved_inner = received[1][recv_rows]
    moved_shared = received[2][recv_rows]
    window = projected.shape[0] // slot_count
    projected = projected.reshape(slot_count, window, projected.shape[1])
    gate_part = projected[:, :, :inner_here]
    value_part = projected[:, :, inner_here : 2 * inner_here]
    fresh_shared = projected[:, :, 2 * inner_here : 2 * inner_here + 2 * state_dim]
    head_index = lax.axis_index("head")
    step_raw = lax.dynamic_slice_in_dim(
        projected[:, :, 2 * inner_here + 2 * state_dim :],
        head_index * heads_here,
        heads_here,
        axis=2,
    )
    edge_inner_out = new_edge(moved_inner, value_part, counts)
    edge_shared_out = new_edge(moved_shared, fresh_shared, counts)
    mixed_inner = depthwise(moved_inner, value_part, conv_inner, conv_inner_bias)
    mixed_shared = depthwise(moved_shared, fresh_shared, conv_shared, conv_shared_bias)
    valid = jnp.arange(window)[None, :] < counts[:, None]
    step_size = jax.nn.softplus(step_raw.astype(jnp.float32) + step_bias)
    step_size = jnp.where(valid[:, :, None], step_size, 0.0)
    decay = -jnp.exp(decay_log)
    inputs = mixed_inner.reshape(slot_count, window, heads_here, head_dim)
    entries = mixed_shared[:, :, :state_dim]
    readouts = mixed_shared[:, :, state_dim:]
    carried = moved_states.astype(jnp.float32)
    collected = []
    for position in range(window):
        carried, produced = advance(
            carried,
            step_size[:, position],
            inputs[:, position],
            entries[:, position],
            readouts[:, position],
            decay,
            skip_gain,
        )
        collected.append(produced)
    outputs = jnp.stack(collected, axis=1)
    outputs = outputs.reshape(slot_count, window, inner_here)
    gated = outputs * jax.nn.silu(gate_part.astype(jnp.float32))
    square_part = jnp.sum(gated * gated, axis=-1, keepdims=True)
    square_sum = lax.psum(square_part, "head")
    full_inner = inner_here * lax.axis_size("head")
    scaled = gated * lax.rsqrt(square_sum / full_inner + EPS) * gate_gain
    scaled = (
        jnp.where(valid[:, :, None], scaled, 0.0)
        .astype(jnp.bfloat16)
        .reshape(slot_count * window, inner_here)
    )
    mixer = lax.psum_scatter(
        jnp.dot(scaled, out_weight, preferred_element_type=jnp.float32).astype(jnp.bfloat16),
        "head",
        scatter_dimension=0,
        tiled=True,
    ).astype(jnp.float32)
    hidden_out = (rows_in + mixer).astype(jnp.bfloat16)
    return (hidden_out, carried.astype(jnp.bfloat16), edge_inner_out, edge_shared_out)


def solution(mesh):
    placed = (
        P(("req", "head"), None),
        P(),
        P(None, None, "head"),
        P(),
        P(None, "head"),
        P("head"),
        P(),
        P(),
        P("head"),
        P("head"),
        P("head"),
        P("head"),
        P("head", None),
        P("req", "head", None, None),
        P("req", None, "head"),
        P("req", None, None),
        P("req"),
        P(),
        P(),
        P(),
    )
    return jax.shard_map(
        local,
        mesh=mesh,
        in_specs=placed,
        out_specs=(
            P(("req", "head"), None),
            P("req", "head", None, None),
            P("req", None, "head"),
            P("req", None, None),
        ),
        check_vma=False,
    )
```

profile of v0, /device:TPU:2, one launch (start us, length us, event | category | flops | bytes accessed | tf_op | source)
XLA Modules:
  0.0 373.1 jit_solution(9102667032434646585)
XLA Ops:
  7.3 8.0 %copy.151 = bf16[32,12,64,128]{3,2,1,0:T(8,128)(2,1)} copy(bf16[32,12,64,128]{3,2,1,0:T(8,128)(2,1)} %param.39) | data formatting | bytes 12582912
  21.6 8.9 %all_gather.15 = bf16[8,3,256]{2,1,0:T(4,128)(2,1)S(1)} all-gather(bf16[1,3,256]{2,1,0:T(4,128)(2,1)S(1)} %copy.121), channel_id=1, replica_groups=mesh['req'=8,'head'=4] {'req'}, dimensions={0}, use_global_device_ids=true | all-gather | bytes 13824 | tf_op jit(solution)/shard_map/all_gather | solution.py:111
  34.9 4.2 %scatter_fusion.2 = bf16[32,3,256]{2,1,0:T(4,128)(2,1)} fusion(bf16[32,3,256]{2,1,0:T(4,128)(2,1)} %broadcast_in_dim.159, s32[32]{0:T(128)S(1)} %compare_select_fusion.3, bf16[32,3,256]{2,1,0:T(4,128)(2,1)S(1)} %copy.98), kind=kCustom, calls=%fused_computation.6 | custom fusion | bytes 147584 | tf_op jit(solution)/shard_map/scatter | solution.py:48
  39.2 3.8 %all-to-all-start.2 = ((bf16[32,3,256]{2,1,0:T(4,128)(2,1)}), bf16[32,3,256]{2,1,0:T(4,128)(2,1)S(1)}, u32[]{:S(2)}, u32[]{:S(2)}) async-start(bf16[32,3,256]{2,1,0:T(4,128)(2,1)} %scatter_fusion.2), calls=%async_computation.2 | async-start | bytes 131072 | tf_op jit(solution)/shard_map/all_to_all | solution.py:134
  43.0 9.1 %all_gather.14 = bf16[8,3,768]{2,1,0:T(4,128)(2,1)S(1)} all-gather(bf16[1,3,768]{2,1,0:T(4,128)(2,1)S(1)} %copy.119), channel_id=1, replica_groups=mesh['req'=8,'head'=4] {'req'}, dimensions={0}, use_global_device_ids=true | all-gather | bytes 41472 | tf_op jit(solution)/shard_map/all_gather | solution.py:110
  54.0 4.3 %scatter_fusion.1 = bf16[32,3,768]{2,1,0:T(4,128)(2,1)} fusion(bf16[32,3,768]{2,1,0:T(4,128)(2,1)} %broadcast_in_dim.158, s32[32]{0:T(128)S(1)} %compare_select_fusion.3, bf16[32,3,768]{2,1,0:T(4,128)(2,1)S(1)} %copy.93), kind=kCustom, calls=%fused_computation.5 | custom fusion | bytes 442496 | tf_op jit(solution)/shard_map/scatter | solution.py:48
  58.3 3.8 %all-to-all-start.1 = ((bf16[32,3,768]{2,1,0:T(4,128)(2,1)}), bf16[32,3,768]{2,1,0:T(4,128)(2,1)S(1)}, u32[]{:S(2)}, u32[]{:S(2)}) async-start(bf16[32,3,768]{2,1,0:T(4,128)(2,1)} %scatter_fusion.1), calls=%async_computation.1 | async-start | bytes 393216 | tf_op jit(solution)/shard_map/all_to_all | solution.py:127
  62.8 2.3 fusion.33
  65.2 4.3 %broadcast_in_dim.83 = bf16[32,12,64,128]{3,2,1,0:T(8,128)(2,1)} broadcast(bf16[]{:T(256)} %constant.132.clone.1), dimensions={} | broadcast | bytes 6291458 | tf_op jit(solution)/shard_map/broadcast_in_dim | solution.py:47
  69.5 19.8 %scatter_fusion = bf16[32,12,64,128]{3,2,1,0:T(8,128)(2,1)} fusion(bf16[32,12,64,128]{3,2,1,0:T(8,128)(2,1)} %broadcast_in_dim.83, s32[32]{0:T(128)S(1)} %compare_select_fusion.3, bf16[32,12,64,128]{3,2,1,0:T(8,128)(2,1)} %fusion.33), kind=kCustom, calls=%fused_computation.4 | custom fusion | bytes 18874496 | tf_op jit(solution)/shard_map/scatter | solution.py:48
  89.3 4.8 %all-to-all-start = ((bf16[32,12,64,128]{3,2,1,0:T(8,128)(2,1)}), bf16[32,12,64,128]{3,2,1,0:T(8,128)(2,1)}, u32[]{:S(2)}, u32[]{:S(2)}) async-start(bf16[32,12,64,128]{3,2,1,0:T(8,128)(2,1)} %scatter_fusion), calls=%async_computation | async-start | bytes 12582912 | tf_op jit(solution)/shard_map/all_to_all | solution.py:120
  94.0 15.2 %all_gather.13 = bf16[128,1536]{1,0:T(8,128)(2,1)S(1)} all-gather(bf16[32,1536]{1,0:T(8,128)(2,1)S(1)} %fusion.31), channel_id=1, replica_groups=mesh['req'=8,'head'=4] {'head'}, dimensions={0}, use_global_device_ids=true | all-gather | bytes 491520 | tf_op jit(solution)/shard_map/all_gather | solution.py:98
  110.9 3.3 copy.127
  131.5 2.1 fusion.36
  133.6 2.1 fusion.25
  135.6 28.6 %all-to-all-done = bf16[32,12,64,128]{3,2,1,0:T(8,128)(2,1)} async-done(((bf16[32,12,64,128]{3,2,1,0:T(8,128)(2,1)}), bf16[32,12,64,128]{3,2,1,0:T(8,128)(2,1)}, u32[]{:S(2)}, u32[]{:S(2)}) %all-to-all-start) | async-done | bytes 6291488 | tf_op jit(solution)/shard_map/all_to_all | solution.py:120
  164.2 7.0 %gather_fusion = bf16[32,12,64,128]{3,2,1,0:T(8,128)(2,1)} fusion(bf16[32,12,64,128]{3,2,1,0:T(8,128)(2,1)} %all-to-all-done, s32[1024]{0:T(1024)} %copy-done.31), kind=kCustom, calls=%fused_computation | custom fusion | bytes 12583040 | tf_op jit(solution)/shard_map/gather | solution.py:142
  171.2 32.0 %fusion = f32[32,1,12,64]{3,1,2,0:T(1,128)S(1)} fusion(bf16[32,12,64,128]{3,2,1,0:T(8,128)(2,1)} %gather_fusion, f32[32,128]{1,0:T(8,128)} %bitcast.110, f32[32,12,64]{2,1,0:T(8,128)} %get-tuple-element.136, f32[32,12]{1,0:T(8,128)S(1)} %copy-done.20, f32[32,4,256]{2,1,0:T(4,128)S(1)} %copy-done.14), kind=kOutput, calls=%fused_computation.11 | convolution fusion | flops 50331648 | bytes 6537216 | tf_op jit(solution)/shard_map/khpn,kn->khp/dot_general | solution.py:15
  203.4 32.3 %fusion.1 = f32[32,1,12,64]{3,1,2,0:T(1,128)S(1)} fusion(bf16[32,12,64,128]{3,2,1,0:T(8,128)(2,1)S(1)} %copy-done.1, f32[32,128]{1,0:T(8,128)S(1)} %bitcast.121, f32[32,12,64]{2,1,0:T(8,128)S(1)} %copy-done.10, f32[32,12]{1,0:T(8,128)S(1)} %copy-done.21, f32[32,128]{1,0:T(8,128)S(1)} %bitcast.112, f32[32,12,64]{2,1,0:T(8,128)S(1)} %copy-done.4, ...), kind=kOutput, calls=%fused_computation.12 | convolution fusion | flops 59768832 | bytes 6995968 | tf_op jit(solution)/shard_map/khpn,kn->khp/dot_general | solution.py:15
  235.7 39.1 %fusion.16 = f32[32,1,12,64]{3,1,2,0:T(1,128)S(1)} fusion(bf16[32,12,64,128]{3,2,1,0:T(8,128)(2,1)S(1)} %copy-done.1, f32[32,128]{1,0:T(8,128)S(1)} %bitcast.118, f32[32,12,64]{2,1,0:T(8,128)S(1)} %copy-done.8, f32[32,12]{1,0:T(8,128)S(1)} %copy-done.22, f32[32,128]{1,0:T(8,128)S(1)} %bitcast.122, f32[32,12,64]{2,1,0:T(8,128)S(1)} %copy-done.10, ...), kind=kOutput, calls=%fused_computation.27 | convolution fusion | flops 69206016 | bytes 7290880 | tf_op jit(solution)/shard_map/khpn,kn->khp/dot_general | solution.py:15
  274.8 42.6 %fusion.3 = f32[32,1,12,64]{3,1,2,0:T(1,128)S(1)} fusion(f32[32,128]{1,0:T(8,128)S(1)} %bitcast.116, f32[32,12,64]{2,1,0:T(8,128)S(1)} %copy-done.6, f32[32,12]{1,0:T(8,128)S(1)} %copy-done.23, bf16[32,12,64,128]{3,2,1,0:T(8,128)(2,1)S(1)} %copy-done.1, f32[32,128]{1,0:T(8,128)S(1)} %bitcast.119, f32[32,12,64]{2,1,0:T(8,128)S(1)} %copy-done.8, ...), kind=kOutput, calls=%fused_computation.14 | convolution fusion | flops 78643200 | bytes 7585792 | tf_op jit(solution)/shard_map/khpn,kn->khp/dot_general | solution.py:15
  325.4 1.9 multiply_reduce_fusion
  327.3 12.6 %psum.7 = f32[32,4,1]{0,1,2:T(4,128)} all-reduce(f32[32,4,1]{0,1,2:T(4,128)} %bitcast.124), channel_id=1, replica_groups=mesh['req'=8,'head'=4] {'head'}, use_global_device_ids=true, to_apply=%region_11.12 | all-reduce | flops 128 | bytes 1024 | tf_op jit(solution)/shard_map/psum | solution.py:185
  342.9 21.7 %fusion.2 = bf16[32,12,64,128]{3,2,1,0:T(8,128)(2,1)} fusion(f32[32,128]{1,0:T(8,128)} %bitcast.115, f32[32,12,64]{2,1,0:T(8,128)S(1)} %copy-done.7, f32[32,12]{1,0:T(8,128)} %get-tuple-element.163, f32[32,128]{1,0:T(8,128)} %bitcast.117, f32[32,12,64]{2,1,0:T(8,128)S(1)} %copy-done.9, f32[32,12]{1,0:T(8,128)} %get-tuple-element.162, ...), kind=kLoop, calls=%fused_computation.13 | loop fusion | flops 44040192 | bytes 13047808 | tf_op jit(solution)/shard_map/convert_element_type | solution.py:200
  (171 shorter events, 41.9 us)
Async XLA Ops:
  7.2 334.5 %copy-start = (bf16[768,1536]{1,0:T(8,128)(2,1)S(1)}, bf16[768,1536]{1,0:T(8,128)(2,1)}, u32[]{:S(2)}) copy-start(bf16[768,1536]{1,0:T(8,128)(2,1)} %param.38) | copy-start | bytes 7077892
  7.2 54.9 %copy-start.41 = (s32[4]{0:T(128)S(1)}, s32[4]{0:T(128)}, u32[]{:S(2)}) copy-start(s32[4]{0:T(128)} %constant.146.clone.1) | copy-start | bytes 52
  7.2 44.9 %copy-start.11 = (bf16[32,1536]{1,0:T(8,128)(2,1)S(1)}, bf16[32,1536]{1,0:T(8,128)(2,1)}, u32[]{:S(2)}) copy-start(bf16[32,1536]{1,0:T(8,128)(2,1)} %param.26) | copy-start | bytes 294916
  7.2 45.0 %copy-start.30 = (f32[1536]{0:T(1024)S(1)}, f32[1536]{0:T(1024)}, u32[]{:S(2)}) copy-start(f32[1536]{0:T(1024)} %param.27) | copy-start | bytes 18436
  7.3 55.5 %all-gather.2.cloned.1.call-start = ((), (), s32[]{:S(2)}) async-start(), calls=%async_computation.4 | async-start | bytes 1769472 | tf_op jit(solution)/shard_map/all_gather | solution.py:109
  39.2 19.1 %all-to-all-start.2 = ((bf16[32,3,256]{2,1,0:T(4,128)(2,1)}), bf16[32,3,256]{2,1,0:T(4,128)(2,1)S(1)}, u32[]{:S(2)}, u32[]{:S(2)}) async-start(bf16[32,3,256]{2,1,0:T(4,128)(2,1)} %scatter_fusion.2), calls=%async_computation.2 | async-start | bytes 131072 | tf_op jit(solution)/shard_map/all_to_all | solution.py:134
  58.3 31.0 %all-to-all-start.1 = ((bf16[32,3,768]{2,1,0:T(4,128)(2,1)}), bf16[32,3,768]{2,1,0:T(4,128)(2,1)S(1)}, u32[]{:S(2)}, u32[]{:S(2)}) async-start(bf16[32,3,768]{2,1,0:T(4,128)(2,1)} %scatter_fusion.1), calls=%async_computation.1 | async-start | bytes 393216 | tf_op jit(solution)/shard_map/all_to_all | solution.py:127
  89.3 75.0 %all-to-all-start = ((bf16[32,12,64,128]{3,2,1,0:T(8,128)(2,1)}), bf16[32,12,64,128]{3,2,1,0:T(8,128)(2,1)}, u32[]{:S(2)}, u32[]{:S(2)}) async-start(bf16[32,12,64,128]{3,2,1,0:T(8,128)(2,1)} %scatter_fusion), calls=%async_computation | async-start | bytes 12582912 | tf_op jit(solution)/shard_map/all_to_all | solution.py:120
  94.0 270.6 %reduce-scatter.2.cloned.1.call-start = ((), (), s32[]{:S(2)}) async-start(), calls=%async_computation.5 | async-start | bytes 491520 | tf_op jit(solution)/shard_map/reduce_scatter | solution.py:193
  135.6 35.6 %copy-start.14 = (f32[32,4,256]{2,1,0:T(4,128)S(1)}, f32[32,4,256]{2,1,0:T(4,128)}, u32[]{:S(2)}) copy-start(f32[32,4,256]{2,1,0:T(4,128)} %copy-done.13) | copy-start | bytes 393220
  135.6 35.6 %copy-start.20 = (f32[32,12]{1,0:T(8,128)S(1)}, f32[32,12]{1,0:T(8,128)}, u32[]{:S(2)}) copy-start(f32[32,12]{1,0:T(8,128)} %get-tuple-element.160) | copy-start | bytes 4612
  171.2 32.1 %copy-start.1 = (bf16[32,12,64,128]{3,2,1,0:T(8,128)(2,1)S(1)}, bf16[32,12,64,128]{3,2,1,0:T(8,128)(2,1)}, u32[]{:S(2)}) copy-start(bf16[32,12,64,128]{3,2,1,0:T(8,128)(2,1)} %gather_fusion) | copy-start | bytes 18874372
  171.2 32.1 %copy-start.4 = (f32[32,12,64]{2,1,0:T(8,128)S(1)}, f32[32,12,64]{2,1,0:T(8,128)}, u32[]{:S(2)}) copy-start(f32[32,12,64]{2,1,0:T(8,128)} %get-tuple-element.136) | copy-start | bytes 294916
  171.2 32.1 %copy-start.10 = (f32[32,12,64]{2,1,0:T(8,128)S(1)}, f32[32,12,64]{2,1,0:T(8,128)}, u32[]{:S(2)}) copy-start(f32[32,12,64]{2,1,0:T(8,128)} %get-tuple-element.139) | copy-start | bytes 294916
  171.2 32.1 %copy-start.21 = (f32[32,12]{1,0:T(8,128)S(1)}, f32[32,12]{1,0:T(8,128)}, u32[]{:S(2)}) copy-start(f32[32,12]{1,0:T(8,128)} %get-tuple-element.161) | copy-start | bytes 4612
  171.2 32.1 %copy-start.24 = (f32[32,1,128]{2,1,0:T(1,128)S(1)}, f32[32,1,128]{2,1,0:T(1,128)}, u32[]{:S(2)}) copy-start(f32[32,1,128]{2,1,0:T(1,128)} %get-tuple-element.144) | copy-start | bytes 49156
  171.2 32.1 %copy-start.27 = (f32[32,1,128]{2,1,0:T(1,128)S(1)}, f32[32,1,128]{2,1,0:T(1,128)}, u32[]{:S(2)}) copy-start(f32[32,1,128]{2,1,0:T(1,128)} %get-tuple-element.147) | copy-start | bytes 49156
  203.3 32.3 %copy-start.8 = (f32[32,12,64]{2,1,0:T(8,128)S(1)}, f32[32,12,64]{2,1,0:T(8,128)}, u32[]{:S(2)}) copy-start(f32[32,12,64]{2,1,0:T(8,128)} %get-tuple-element.138) | copy-start | bytes 294916
  203.3 32.3 %copy-start.22 = (f32[32,12]{1,0:T(8,128)S(1)}, f32[32,12]{1,0:T(8,128)}, u32[]{:S(2)}) copy-start(f32[32,12]{1,0:T(8,128)} %get-tuple-element.162) | copy-start | bytes 4612
  203.4 32.3 %copy-start.26 = (f32[32,1,128]{2,1,0:T(1,128)S(1)}, f32[32,1,128]{2,1,0:T(1,128)}, u32[]{:S(2)}) copy-start(f32[32,1,128]{2,1,0:T(1,128)} %get-tuple-element.146) | copy-start | bytes 49156
  235.7 39.1 %copy-start.6 = (f32[32,12,64]{2,1,0:T(8,128)S(1)}, f32[32,12,64]{2,1,0:T(8,128)}, u32[]{:S(2)}) copy-start(f32[32,12,64]{2,1,0:T(8,128)} %get-tuple-element.137) | copy-start | bytes 294916
  235.7 39.1 %copy-start.23 = (f32[32,12]{1,0:T(8,128)S(1)}, f32[32,12]{1,0:T(8,128)}, u32[]{:S(2)}) copy-start(f32[32,12]{1,0:T(8,128)} %get-tuple-element.163) | copy-start | bytes 4612
  235.7 39.1 %copy-start.25 = (f32[32,1,128]{2,1,0:T(1,128)S(1)}, f32[32,1,128]{2,1,0:T(1,128)}, u32[]{:S(2)}) copy-start(f32[32,1,128]{2,1,0:T(1,128)} %get-tuple-element.145) | copy-start | bytes 49156
  274.8 42.6 %copy-start.39 = (f32[12]{0:T(128)S(1)}, f32[12]{0:T(128)}, u32[]{:S(2)}) copy-start(f32[12]{0:T(128)} %param.36) | copy-start | bytes 148
  (25 other events, 282.0 us)
Sparse Core Ops, SparseCore 0:
  18.4 26.9 all-gather.1
  343.0 17.8 reduce-scatter.1
where the time goes:
time: 377 us; the launch traced here: 373 us
  matrix products  150 us (40%)
  local copies, waits for them, and re-layouts  71.8 us (19%)
  other arithmetic  47.4 us (13%)
  blocking collectives  45.9 us (12%)
  waiting for transfers between devices  28.7 us (8%)
  between operations  17.5 us (5%)
  starting transfers between devices  12.4 us (3%)
    dot_general x4, matrix products, advance(): jnp.einsum('khpn,kn->khp', carried, readout_now, precision=lax.Precision....  146 us
    all_to_all x1, waiting for transfers between devices, local(): lax.all_to_all(pack_pages(sectioned_states, send_rows, buffer_rows), 'req...  28.6 us
    scatter x3, local copies, waits for them, and re-layouts, pack_pages(): return empty.at[send_rows].set(member)  28.3 us
    convert_element_type x1, other arithmetic, local(): carried.astype(jnp.bfloat16)  21.7 us
    all_gather x1, blocking collectives, local(): piece_rows = lax.all_gather(normed, 'head', axis=0, tiled=True)  15.2 us
    unnamed x96, local copies, waits for them, and re-layouts  13.5 us
    psum x1, blocking collectives, local(): square_sum = lax.psum(square_part, 'head')  12.6 us
    all_gather x1, blocking collectives, local(): lax.all_gather(edge_inner[local_ids], 'req', axis=0, tiled=True)  9.14 us
  transfers between devices with their start and end apart: 5, of which 1 were waited for; matrix products, arithmetic and copies ran while one was open for 24% of the time, Pallas kernels for 0%

commit v1 on v0

v1 whole, which is shorter than its diff:
```python
import functools

import jax
import jax.numpy as jnp
from jax import lax
from jax.experimental import pallas as pl
from jax.experimental.pallas import tpu as pltpu
from jax.sharding import PartitionSpec as P

EPS = 1e-05
F32 = jnp.float32
BF16 = jnp.bfloat16
VMEM_BYTES = 16 * 1024 * 1024
HBM = pl.BlockSpec(memory_space=pl.ANY)
SMEM = pl.BlockSpec(memory_space=pltpu.SMEM)
VMEM = pl.BlockSpec(memory_space=pltpu.VMEM)


def peer_of(index, step, size):
    if size & (size - 1) == 0:
        return index ^ step
    return lax.rem(index + step, size)


def origin_of(index, step, size):
    if size & (size - 1) == 0:
        return index ^ step
    return lax.rem(index - step + size, size)


def permute(value, axis, step):
    size = lax.axis_size(axis)
    pairs = [(i, i ^ step if size & (size - 1) == 0 else (i + step) % size) for i in range(size)]
    return lax.ppermute(value, axis, pairs)


def fill_sources(count, ids_ref, dest_ref, source):
    def fill(slot, carry):
        source[slot] = slot
        return carry

    lax.fori_loop(0, count, fill, 0)

    def migrate(entry, carry):
        source[dest_ref[entry]] = ids_ref[entry]
        return carry

    lax.fori_loop(0, ids_ref.shape[0], migrate, 0)


def pack_kernel(
    groups,
    slots,
    capacity,
    edge_block,
    chunk,
    device_ref,
    ids_ref,
    dest_ref,
    reorder_ref,
    inner_ref,
    shared_ref,
    states_ref,
    out_edges,
    recv_rows,
    out_states,
    source,
    target,
    seen,
    staged,
    read_done,
    write_done,
):
    first = device_ref[0] * slots
    reads = [
        pltpu.make_async_copy(
            states_ref.at[pl.ds(part * chunk, chunk)], staged.at[pl.ds(part * chunk, chunk)], read_done.at[part]
        )
        for part in range(slots // chunk)
    ]
    for read in reads:
        read.start()
    fill_sources(groups * slots, ids_ref, dest_ref, source)

    def to_peer(peer, carry):
        def one(slot, rank):
            local = source[reorder_ref[peer * slots + slot]] - first
            mine = jnp.logical_and(local >= 0, local < slots)

            @pl.when(mine)
            def _():
                target[local] = peer * edge_block + rank

            return rank + mine.astype(jnp.int32)

        lax.fori_loop(0, slots, one, 0, unroll=4)
        return carry

    lax.fori_loop(0, groups, to_peer, 0)

    def clear(group, carry):
        seen[group] = 0
        return carry

    lax.fori_loop(0, groups, clear, 0)

    def receive(slot, carry):
        owner = lax.div(source[reorder_ref[first + slot]], slots)
        rank = seen[owner]
        recv_rows[slot] = owner * edge_block + rank
        seen[owner] = rank + 1
        return carry

    lax.fori_loop(0, slots, receive, 0)

    for part in range(slots // chunk):
        reads[part].wait()
        for slot in range(part * chunk, (part + 1) * chunk):
            place = target[slot]
            row = lax.div(place, edge_block) * capacity + lax.rem(place, edge_block)
            pltpu.make_async_copy(staged.at[slot], out_states.at[row], write_done.at[0]).start()

    keep = inner_ref.shape[0]
    rows = groups * edge_block
    lane = lax.broadcasted_iota(jnp.int32, (1, slots), 1)
    places = jnp.zeros((1, slots), jnp.int32)
    for slot in range(slots):
        places = jnp.where(lane == slot, target[slot], places)
    row = lax.broadcasted_iota(jnp.int32, (rows, slots), 0)
    width = inner_ref.shape[2]
    inner_sum = jnp.zeros((rows, width), F32)
    shared_sum = jnp.zeros((rows, shared_ref.shape[2]), F32)
    for k in range(keep):
        pick = jnp.where(row == places + k * capacity, 1.0, 0.0).astype(BF16)
        inner_sum = inner_sum + jnp.dot(pick, inner_ref[k], preferred_element_type=F32)
        shared_sum = shared_sum + jnp.dot(pick, shared_ref[k], preferred_element_type=F32)
    out_edges[:, :width] = inner_sum.astype(BF16)
    out_edges[:, width:] = shared_sum.astype(BF16)
    pltpu.make_async_copy(staged, out_states.at[pl.ds(0, slots)], write_done.at[0]).wait()


def pack(device, mig_ids, mig_dest, reorder, states, edge_inner, edge_shared, groups, capacity, edge_block):
    slots = states.shape[0]
    width = edge_inner.shape[2] + edge_shared.shape[2]
    chunk = 4
    return pl.pallas_call(
        functools.partial(pack_kernel, groups, slots, capacity, edge_block, chunk),
        out_shape=(
            jax.ShapeDtypeStruct((groups * edge_block, width), BF16),
            jax.ShapeDtypeStruct((slots,), jnp.int32),
            jax.ShapeDtypeStruct((groups * capacity,) + states.shape[1:], states.dtype),
        ),
        in_specs=[SMEM] * 4 + [VMEM] * 2 + [HBM],
        out_specs=(VMEM, SMEM, HBM),
        scratch_shapes=[
            pltpu.SMEM((groups * slots,), jnp.int32),
            pltpu.SMEM((slots,), jnp.int32),
            pltpu.SMEM((groups,), jnp.int32),
            pltpu.VMEM(states.shape, states.dtype),
            pltpu.SemaphoreType.DMA((slots // chunk,)),
            pltpu.SemaphoreType.DMA((1,)),
        ],
        compiler_params=pltpu.CompilerParams(vmem_limit_bytes=VMEM_BYTES),
        name="pack",
    )(device, mig_ids, mig_dest, reorder, edge_inner.transpose(1, 0, 2), edge_shared.transpose(1, 0, 2), states)


def shift_rows(value, by):
    by = by % value.shape[0]
    return pltpu.roll(value, by, 0) if by else value


def mix(edge, fresh, weight, bias, token):
    taps = weight.shape[0]
    summed = fresh * weight[taps - 1 : taps] + bias
    for tap in range(taps - 1):
        back = taps - 1 - tap
        moved = jnp.where(token >= back, shift_rows(fresh, back), shift_rows(edge, -tap))
        summed = summed + moved * weight[tap : tap + 1]
    return summed / (1.0 + jnp.exp(-summed))


def latest(edge, fresh, counts, token, window):
    keep = window - 1
    result = edge
    for length in range(1, window + 1):
        chosen = jnp.where(token + length < keep, shift_rows(edge, -length), shift_rows(fresh, keep - length))
        result = jnp.where(counts == length, chosen, result)
    return result


def token_kernel(
    window,
    heads,
    head_dim,
    state_dim,
    capacity,
    device_ref,
    skip_ref,
    recv_ref,
    rows_ref,
    shared_ref,
    edges_ref,
    counts_ref,
    conv_inner_ref,
    inner_bias_ref,
    conv_shared_ref,
    shared_bias_ref,
    step_bias_ref,
    decay_log_ref,
    moved_ref,
    entry_ref,
    readout_ref,
    within_ref,
    decay_ref,
    gate_ref,
    new_inner_ref,
    new_shared_ref,
):
    inner = heads * head_dim
    rows = rows_ref.shape[0]
    wide = lax.broadcasted_iota(jnp.int32, (rows, 1), 0)
    token = lax.rem(wide, window)
    counts = counts_ref[...]
    valid = token < counts

    arrived = edges_ref.shape[0]
    place = jnp.zeros((rows, 1), jnp.int32)
    for slot in range(rows // window):
        place = jnp.where(lax.div(wide, window) == slot, recv_ref[slot], place)
    pick = lax.broadcasted_iota(jnp.int32, (rows, arrived), 1) == place + token * capacity
    pick = jnp.logical_and(pick, token < window - 1)
    edges = jnp.dot(jnp.where(pick, 1.0, 0.0).astype(BF16), edges_ref[...], preferred_element_type=F32)

    gate = rows_ref[:, :inner].astype(F32)
    gate_ref[...] = jnp.where(valid, gate / (1.0 + jnp.exp(-gate)), 0.0)

    value = rows_ref[:, inner:].astype(F32)
    edge = edges[:, :inner]
    new_inner_ref[...] = latest(edge, value, counts, token, window).astype(BF16)
    mixed = mix(edge, value, conv_inner_ref[...], inner_bias_ref[...], token)

    fresh = shared_ref[:, : 2 * state_dim].astype(F32)
    edge = edges[:, inner:]
    new_shared_ref[...] = latest(edge, fresh, counts, token, window).astype(BF16)
    shared = mix(edge, fresh, conv_shared_ref[...], shared_bias_ref[...], token)
    entry = shared[:, :state_dim]
    readout = shared[:, state_dim:]
    entry_ref[...] = entry.astype(BF16)
    readout_t = readout.T.astype(BF16)
    readout_ref[...] = readout_t

    raw = shared_ref[:, 2 * state_dim :]
    all_heads = raw.shape[1]
    from_head = lax.broadcasted_iota(jnp.int32, (all_heads, rows), 0)
    to_lane = lax.broadcasted_iota(jnp.int32, (all_heads, rows), 1)
    pick = jnp.logical_and(from_head == to_lane + device_ref[1] * heads, to_lane < heads)
    raw = jnp.dot(raw, pick.astype(BF16), preferred_element_type=F32) + step_bias_ref[...]
    step = jnp.maximum(raw, 0.0) + jnp.log(1.0 + jnp.exp(-jnp.abs(raw)))
    step = jnp.where(valid, step, 0.0)
    drop = step * -jnp.exp(decay_log_ref[...])
    total = drop
    after = drop
    reach = 1
    while reach < window:
        total = total + jnp.where(token >= reach, shift_rows(total, reach), 0.0)
        after = after + jnp.where(token + reach < window, shift_rows(after, -reach), 0.0)
        reach *= 2
    after = jnp.where(token + 1 < window, shift_rows(after, -1), 0.0)
    total_t = total.T
    decay_ref[...] = jnp.exp(total_t)[: decay_ref.shape[0]]
    carry_t = (step * jnp.exp(after)).T

    slot_a = lax.div(lax.broadcasted_iota(jnp.int32, (rows, rows), 0), window)
    slot_b = lax.div(lax.broadcasted_iota(jnp.int32, (rows, rows), 1), window)
    row_a = lax.broadcasted_iota(jnp.int32, (rows, rows), 0)
    row_b = lax.broadcasted_iota(jnp.int32, (rows, rows), 1)
    causal = jnp.logical_and(slot_a == slot_b, row_a <= row_b)
    overlap = jnp.dot(entry.astype(BF16), readout_t, preferred_element_type=F32)
    overlap = jnp.where(causal, overlap, 0.0)
    for block in range(inner // rows):
        turned = mixed[:, block * rows : (block + 1) * rows].T
        for part in range(rows // head_dim):
            head = block * (rows // head_dim) + part
            mine = turned[part * head_dim : (part + 1) * head_dim]
            here = pl.ds(head * head_dim, head_dim)
            moved_ref[here, :] = (mine * carry_t[head : head + 1]).astype(BF16)
            gap = jnp.minimum(total_t[head : head + 1] - total[:, head : head + 1], 0.0)
            weight = overlap * jnp.exp(gap) * step[:, head : head + 1]
            within_ref[here, :] = skip_ref[head] * mine + jnp.dot(
                mine.astype(BF16), weight.astype(BF16), preferred_element_type=F32
            )


def token_part(
    device, skip_gain, recv_rows, rows, shared, edges, counts, conv_inner, inner_bias, conv_shared, shared_bias, step_bias, decay_log, window, heads, head_dim, state_dim, capacity
):
    count = rows.shape[0]
    inner = heads * head_dim
    padded = -(-heads // 8) * 8
    shape = jax.ShapeDtypeStruct
    return pl.pallas_call(
        functools.partial(token_kernel, window, heads, head_dim, state_dim, capacity),
        out_shape=(
            shape((inner, count), BF16),
            shape((count, state_dim), BF16),
            shape((state_dim, count), BF16),
            shape((inner, count), F32),
            shape((padded, count), F32),
            shape((count, inner), F32),
            shape((count, inner), BF16),
            shape((count, 2 * state_dim), BF16),
        ),
        in_specs=[SMEM] * 3 + [VMEM] * 10,
        out_specs=(VMEM,) * 8,
        compiler_params=pltpu.CompilerParams(vmem_limit_bytes=VMEM_BYTES),
        name="token_rows",
    )(device, skip_gain, recv_rows, rows, shared, edges, counts, conv_inner, inner_bias, conv_shared, shared_bias, step_bias, decay_log)


def state_kernel(window, batch, rows_ref, decay_smem, *refs):
    del rows_ref
    pages = refs[:batch]
    moved_ref, entry_ref, readout_ref, within_ref, decay_ref, gate_ref, gain_ref, weight_ref, out_ref, message_ref, read_sum = refs[batch:]
    step = pl.program_id(0)
    heads, head_dim, state_dim = pages[0].shape[1:]
    inner = heads * head_dim
    count = entry_ref.shape[0]
    entry = entry_ref[...]
    readout = readout_ref[...]
    row_slot = lax.div(lax.broadcasted_iota(jnp.int32, (count, state_dim), 0), window)
    lane_slot = lax.div(lax.broadcasted_iota(jnp.int32, (state_dim, count), 1), window)
    first = step * batch
    zero = jnp.zeros((), BF16)
    entries = jnp.concatenate([jnp.where(row_slot == first + q, entry, zero) for q in range(batch)], axis=1)
    readouts = jnp.concatenate([jnp.where(lane_slot == first + q, readout, zero) for q in range(batch)], axis=0)
    held = jnp.concatenate([page[0].reshape(inner, state_dim) for page in pages], axis=1)
    read = jnp.dot(held, readouts, preferred_element_type=F32)

    @pl.when(step == 0)
    def _():
        read_sum[...] = read

    @pl.when(step > 0)
    def _():
        read_sum[...] += read

    added = jnp.dot(moved_ref[...], entries, preferred_element_type=F32)
    for q in range(batch):
        lane = (first + q) * window + window - 1
        for head in range(heads):
            here = slice(head * head_dim, (head + 1) * head_dim)
            kept = pages[q][0, head].astype(F32) * decay_smem[head, lane]
            out_ref[q, head] = (kept + added[here, q * state_dim : (q + 1) * state_dim]).astype(BF16)

    @pl.when(step == pl.num_programs(0) - 1)
    def _():
        decay = decay_ref[...]
        blocks = []
        for block in range(inner // count):
            parts = []
            for part in range(count // head_dim):
                head = block * (count // head_dim) + part
                here = pl.ds(head * head_dim, head_dim)
                parts.append(read_sum[here, :] * decay[head : head + 1] + within_ref[here, :])
            blocks.append(jnp.concatenate(parts, axis=0).T)
        gated = jnp.concatenate(blocks, axis=1) * gate_ref[...]
        squares = jnp.sum(gated * gated, axis=1, keepdims=True)
        high = squares.astype(BF16)
        low = (squares - high.astype(F32)).astype(BF16)
        scaled = (gated * gain_ref[...]).astype(BF16)
        width = weight_ref.shape[1]
        message_ref[:, :width] = jnp.dot(scaled, weight_ref[...], preferred_element_type=F32).astype(BF16)
        lane = lax.broadcasted_iota(jnp.int32, (count, message_ref.shape[1] - width), 1)
        message_ref[:, width:] = jnp.where(lane == 0, high, jnp.where(lane == 1, low, zero))


def state_part(recv_rows, decay, received, moved, entry, readout, within, gate, gain, out_weight, window):
    slots = recv_rows.shape[0]
    page = received.shape[1:]
    batch = 4
    steps = slots // batch
    count, inner = gate.shape
    width = out_weight.shape[1]

    def page_spec(q):
        return pl.BlockSpec((1,) + page, lambda i, rows, q=q: (rows[i * batch + q], 0, 0, 0))

    def whole(array):
        return pl.BlockSpec(array.shape, lambda i, rows: (0,) * array.ndim)

    return pl.pallas_call(
        functools.partial(state_kernel, window, batch),
        grid_spec=pltpu.PrefetchScalarGridSpec(
            num_scalar_prefetch=1,
            grid=(steps,),
            in_specs=[pl.BlockSpec(memory_space=pltpu.SMEM)]
            + [page_spec(q) for q in range(batch)]
            + [whole(a) for a in (moved, entry, readout, within, decay, gate, gain, out_weight)],
            out_specs=(
                pl.BlockSpec((batch,) + page, lambda i, rows: (i, 0, 0, 0)),
                pl.BlockSpec((count, width + 128), lambda i, rows: (0, 0)),
            ),
            scratch_shapes=[pltpu.VMEM((inner, count), F32)],
        ),
        out_shape=(
            jax.ShapeDtypeStruct((slots,) + page, BF16),
            jax.ShapeDtypeStruct((count, width + 128), BF16),
        ),
        compiler_params=pltpu.CompilerParams(vmem_limit_bytes=VMEM_BYTES),
        name="states",
    )(recv_rows, decay, *([received] * batch), moved, entry, readout, within, decay, gate, gain, out_weight)


def local(
    tokens,
    pre_gain,
    inner_weight,
    shared_weight,
    conv_inner,
    conv_inner_bias,
    conv_shared,
    conv_shared_bias,
    step_bias,
    decay_log,
    skip_gain,
    gate_gain,
    out_weight,
    states,
    edge_inner,
    edge_shared,
    counts,
    mig_ids,
    mig_dest,
    reorder,
):
    slots, heads, head_dim, state_dim = states.shape
    inner = heads * head_dim
    groups = lax.axis_size("req")
    shares = lax.axis_size("head")
    request_index = lax.axis_index("req")
    head_index = lax.axis_index("head")
    device = jnp.stack([request_index, head_index]).astype(jnp.int32)
    own_rows = tokens.shape[0]
    window = own_rows * shares // slots
    width = tokens.shape[1]
    capacity = -(-slots // groups) + mig_ids.shape[0] // groups

    keep = edge_inner.shape[1]
    edge_block = -(-keep * capacity // 16) * 16
    send_edges, recv_rows, send_states = pack(
        device, mig_ids, mig_dest, reorder, states, edge_inner, edge_shared, groups, capacity, edge_block
    )
    exchange = functools.partial(lax.all_to_all, axis_name="req", split_axis=0, concat_axis=0, tiled=True)
    edges = exchange(send_edges)
    send_states, edges = lax.optimization_barrier((send_states, edges))
    received = exchange(send_states)

    rows_in = tokens.astype(F32)
    normed = (rows_in * lax.rsqrt(jnp.mean(rows_in * rows_in, axis=-1, keepdims=True) + EPS) * pre_gain).astype(BF16)
    all_rows = jnp.zeros((own_rows * shares, width), BF16)
    for step in range(shares):
        piece = permute(normed, "head", step) if step else normed
        start = origin_of(head_index, step, shares) * own_rows
        all_rows = lax.dynamic_update_slice_in_dim(all_rows, piece, start, 0)
    inner_flat = inner_weight.reshape(width, 2 * inner)
    inner_rows = jnp.dot(all_rows, inner_flat, preferred_element_type=F32).astype(BF16)
    shared_rows = jnp.dot(all_rows, shared_weight, preferred_element_type=F32).astype(BF16)

    lanes = slots * window

    def in_lanes(vector):
        return jnp.pad(vector, (0, lanes - heads)).reshape(1, lanes)

    moved, entry, readout, within, decay, gate, new_inner, new_shared = token_part(
        device,
        skip_gain,
        recv_rows,
        inner_rows,
        shared_rows,
        edges,
        jnp.repeat(counts, window).reshape(lanes, 1),
        conv_inner,
        conv_inner_bias.reshape(1, -1),
        conv_shared,
        conv_shared_bias.reshape(1, -1),
        in_lanes(step_bias),
        in_lanes(decay_log),
        window,
        heads,
        head_dim,
        state_dim,
        capacity,
    )
    page_rows = lax.div(recv_rows, edge_block) * capacity + lax.rem(recv_rows, edge_block)
    edge_inner_out = new_inner.reshape(slots, window, inner)[:, :keep]
    edge_shared_out = new_shared.reshape(slots, window, 2 * state_dim)[:, :keep]

    states_out, message = state_part(
        page_rows, decay, received, moved, entry, readout, within, gate, gate_gain.reshape(1, -1), out_weight, window
    )
    total = jnp.zeros((own_rows, message.shape[1]), F32)
    for step in range(shares):
        start = peer_of(head_index, step, shares) * own_rows
        piece = lax.dynamic_slice_in_dim(message, start, own_rows)
        if step:
            piece = permute(piece, "head", step)
        total = total + piece.astype(F32)
    squares = total[:, width : width + 1] + total[:, width + 1 : width + 2]
    mixer = total[:, :width] * lax.rsqrt(squares / (inner * shares) + EPS)
    hidden_out = (rows_in + mixer).astype(BF16)
    return (hidden_out, states_out, edge_inner_out, edge_shared_out)


def solution(mesh):
    placed = (
        P(("req", "head"), None),
        P(),
        P(None, None, "head"),
        P(),
        P(None, "head"),
        P("head"),
        P(),
        P(),
        P("head"),
        P("head"),
        P("head"),
        P("head"),
        P("head", None),
        P("req", "head", None, None),
        P("req", None, "head"),
        P("req", None, None),
        P("req"),
        P(),
        P(),
        P(),
    )
    return jax.shard_map(
        local,
        mesh=mesh,
        in_specs=placed,
        out_specs=(
            P(("req", "head"), None),
            P("req", "head", None, None),
            P("req", None, "head"),
            P("req", None, None),
        ),
        check_vma=False,
    )
```

time: 377 us -> 166 us (0.44)
  matrix products: 150 us -> 5.34 us
  other arithmetic: 47.4 us -> 5.02 us
  blocking collectives: 45.9 us -> 9.52 us
  local copies, waits for them, and re-layouts: 71.8 us -> 39.4 us
  waiting for transfers between devices: 28.7 us -> 59.8 us
  Pallas kernels: 0 us -> 29.8 us
  between operations: 17.5 us -> 0.92 us
    dot_general x7 -> x2, matrix products: 150 us -> 5.34 us  [the longest x1 3.31 us: local(): jnp.dot(all_rows, inner_flat, preferred_element_type=F32).astype(BF16)]
    all_gather x3 -> x0, blocking collectives: 33.2 us -> none  [the longest x1 15.2 us: local(): piece_rows = lax.all_gather(normed, 'head', axis=0, tiled=True)]
    scatter x8 -> x0, local copies, waits for them, and re-layouts: 30 us -> none  [the longest x3 28.3 us: pack_pages(): return empty.at[send_rows].set(member)]
    pallas_call x0 -> x3, Pallas kernels: none -> 29.8 us  [the longest x1 13.9 us: pack(): pl.pallas_call(functools.partial(pack_kernel, groups, slots, capacity, ed...]
    all_to_all x3 -> x1, waiting for transfers between devices: 28.6 us -> 51.4 us  [local(): received = exchange(send_states)]
    convert_element_type x6 -> x1, other arithmetic: 24.3 us -> 1.63 us  [local(): hidden_out = (rows_in + mixer).astype(BF16)]
    unnamed x96 -> x95, local copies, waits for them, and re-layouts: 13.5 us -> 29 us
    psum x1 -> x0, blocking collectives: 12.6 us -> none  [local(): square_sum = lax.psum(square_part, 'head')]
  transfers between devices with their start and end apart: 5 -> 7, of which waited for: 1 -> 3; matrix products, arithmetic and copies ran while one was open for 24% -> 15% of each run, Pallas kernels for 0% -> 1%
where the time goes in v1:
time: 166 us; the launch traced here: 165 us
  waiting for transfers between devices  59.8 us (36%)
  local copies, waits for them, and re-layouts  39.4 us (24%)
  Pallas kernels  29.8 us (18%)
  starting transfers between devices  15 us (9%)
  blocking collectives  9.52 us (6%)
  matrix products  5.34 us (3%)
  other arithmetic  5.02 us (3%)
    all_to_all x1, waiting for transfers between devices, local(): received = exchange(send_states)  51.4 us
    unnamed x95, local copies, waits for them, and re-layouts  29 us
    pallas_call x1, Pallas kernels, pack(): pl.pallas_call(functools.partial(pack_kernel, groups, slots, capacity, ed...  13.9 us
    pallas_call x1, Pallas kernels, state_part(): pl.pallas_call(functools.partial(state_kernel, window, batch), grid_spec=...  13.5 us
    all_to_all x1, blocking collectives, local(): edges = exchange(send_edges)  9.52 us
    ppermute x6, starting transfers between devices, permute(): return lax.ppermute(value, axis, pairs)  8.61 us
    ppermute x6, waiting for transfers between devices, permute(): return lax.ppermute(value, axis, pairs)  8.38 us
    all_to_all x1, starting transfers between devices, local(): received = exchange(send_states)  6.41 us
  transfers between devices with their start and end apart: 7, of which 3 were waited for; matrix products, arithmetic and copies ran while one was open for 15% of the time, Pallas kernels for 1%

profile of v1, /device:TPU:2, one launch (start us, length us, event | category | flops | bytes accessed | tf_op | source)
XLA Modules:
  0.0 164.8 jit_solution(5307409744154009883)
XLA Ops:
  0.7 2.8 %copy-done.2 = bf16[32,12,64,128]{3,2,1,0:T(8,128)(2,1)S(1)} copy-done((bf16[32,12,64,128]{3,2,1,0:T(8,128)(2,1)S(1)}, bf16[32,12,64,128]{3,2,1,0:T(8,128)(2,1)}, u32[]{:S(2)}) %copy-start.2) | copy-done | bytes 6291480
  7.3 13.9 %pack.1 = (bf16[128,1024]{1,0:T(8,128)(2,1)S(1)}, s32[32]{0:T(128)S(1)}, bf16[40,12,64,128]{3,2,1,0:T(8,128)(2,1)S(1)}) custom-call(s32[2]{0:T(128)S(1)} %pad_add_fusion.device_ref, s32[8]{0:T(128)S(1)} %copy-done.35, s32[8]{0:T(128)S(1)} %copy-done.36, s32[256]{0:T(256)S(1)} %copy-done.33, bf16[3,32,768]{2,1,0:T(8,128)(2,1)S(1)} %bitcast.21, ...), custom_call_target="tpu_custom_call" | custom-call | tf_op jit(solution)/shard_map/pack/pallas_call | solution.py:146
  21.2 3.1 %copy-done.1 = bf16[40,12,64,128]{3,2,1,0:T(8,128)(2,1)} copy-done((bf16[40,12,64,128]{3,2,1,0:T(8,128)(2,1)}, bf16[40,12,64,128]{3,2,1,0:T(8,128)(2,1)S(1)}, u32[]{:S(2)}) %copy-start.1) | copy-done | bytes 7864344
  24.2 9.5 %all_to_all.17 = bf16[8,16,1024]{2,1,0:T(8,128)(2,1)S(1)} all-to-all(bf16[8,16,1024]{2,1,0:T(8,128)(2,1)S(1)} %bitcast.20), channel_id=1, replica_groups=mesh['req'=8,'head'=4] {'req'}, dimensions={0} | all-to-all | bytes 524288 | tf_op jit(solution)/shard_map/all_to_all | solution.py:455
  33.8 6.4 %all-to-all-start.1 = ((bf16[40,12,64,128]{3,2,1,0:T(8,128)(2,1)}), bf16[40,12,64,128]{3,2,1,0:T(8,128)(2,1)}, u32[]{:S(2)}, u32[]{:S(2)}) async-start(bf16[40,12,64,128]{3,2,1,0:T(8,128)(2,1)} %copy-done.1), calls=%async_computation.1 | async-start | bytes 15728640 | tf_op jit(solution)/shard_map/all_to_all | solution.py:457
  41.9 2.6 %collective-permute-start.1 = (bf16[32,1536]{1,0:T(8,128)(2,1)}, bf16[32,1536]{1,0:T(8,128)(2,1)}, u32[]{:S(2)}, u32[]{:S(2)}) collective-permute-start(bf16[32,1536]{1,0:T(8,128)(2,1)} %get-tuple-element.35), channel_id=1, source_target_pairs={{0,2},{1,3},{2,0},{3,1},{4,6},{5,7},{6,4},{7,5},{8,10},{9,11},{10,... | collective-permute-start | bytes 294920 | tf_op jit(solution)/shard_map/ppermute | solution.py:34
  44.5 1.6 collective-permute-start
  48.3 5.5 %copy.38 = bf16[192,8,2,768]{3,1,2,0:T(8,128)(2,1)} copy(bf16[192,8,2,768]{3,2,1,0:T(2,128)(2,1)} %bitcast.25) | data formatting | bytes 9437184
  53.7 1.3 fusion.8.rows_ref
  55.0 1.3 pad_bitcast_fusion
  56.3 1.6 constant_dynamic-update-slice_fusion.2
  57.8 1.5 constant_dynamic-update-slice_fusion.1
  59.4 1.5 constant_dynamic-update-slice_fusion
  60.9 2.0 %convolution_convert_fusion.1 = bf16[128,304]{0,1:T(8,128)(2,1)} fusion(bf16[128,1536]{1,0:T(8,128)(2,1)} %constant_dynamic-update-slice_fusion, bf16[1536,304]{0,1:T(8,128)(2,1)S(1)} %copy-done), kind=kOutput, calls=%fused_computation.1 | convolution fusion | flops 119576576 | bytes 1404928 | tf_op jit(solution)/shard_map/dot_general | solution.py:468
  62.9 1.6 copy.32.shared_ref
  64.7 3.3 %convolution_convert_fusion.rows_ref = bf16[128,1536]{1,0:T(8,128)(2,1)S(1)} fusion(bf16[128,1536]{1,0:T(8,128)(2,1)} %constant_dynamic-update-slice_fusion, bf16[1536,1536]{1,0:T(8,128)(2,1)} %bitcast.24), kind=kOutput, calls=%fused_computation | convolution fusion | flops 604176384 | bytes 5505024 | tf_op jit(solution)/shard_map/dot_general | solution.py:467
  68.1 2.4 %token_rows.1 = (bf16[768,128]{1,0:T(8,128)(2,1)S(1)}, bf16[128,128]{1,0:T(8,128)(2,1)S(1)}, bf16[128,128]{1,0:T(8,128)(2,1)S(1)}, f32[768,128]{1,0:T(8,128)S(1)...) custom-call(s32[2]{0:T(128)S(1)} %copy-done.30, ...), custom_call_target="tpu_custom_call" | custom-call | tf_op jit(solution)/shard_map/token_rows/pallas_call | solution.py:302
  75.8 51.4 %all-to-all-done.1.refs_0_.refs_1_.refs_2_.refs_3_ = bf16[40,12,64,128]{3,2,1,0:T(8,128)(2,1)} async-done(((bf16[40,12,64,128]{3,2,1,0:T(8,128)(2,1)}), bf16[40,12,64,128]{3,2,1,0:T(8,128)(2,1)}, u32[]{:S(2)}, u32[]{:S(2)}) %all-to-all-start.1) | async-done | bytes 7864352 | tf_op jit(solution)/shard_map/all_to_all | solution.py:457
  133.7 13.5 %states.1 = (bf16[32,12,64,128]{3,2,1,0:T(8,128)(2,1)}, bf16[128,1664]{1,0:T(8,128)(2,1)S(1)}) custom-call(s32[32]{0:T(128)S(1)} %copy-done.40, f32[16,128]{1,0:T(8,128)S(1)} %copy-done.24, bf16[40,12,64,128]{3,2,1,0:T(8,128)(2,1)} %all-to-all-done.1.refs_0_.refs_1_.refs_2_.refs_3_, bf16[40,12,64,128]{3,2,1,0:T(8,128)(2,1)} %all-to-all-done.1.refs_0_.refs_1_.refs_2_.refs_3_, ...), custom_call_target="tpu_custom_call" | custom-call | tf_op jit(solution)/shard_map/states/pallas_call | solution.py:392
  148.0 1.6 collective-permute-start.3
  149.7 2.5 %collective-permute-start.5 = (bf16[32,1664]{1,0:T(8,128)(2,1)S(1)}, bf16[32,1664]{1,0:T(8,128)(2,1)S(1)}, u32[]{:S(2)}, u32[]{:S(2)}) collective-permute-start(bf16[32,1664]{1,0:T(8,128)(2,1)S(1)} %get-tuple-element.37), channel_id=1, source_target_pairs={{0,3},{1,2},{2,1},{3,0},{4,7},{5,6},{6,5},{7,4},{8,11},{9,10},{10,... | collective-permute-start | bytes 319496 | tf_op jit(solution)/shard_map/ppermute | solution.py:34
  153.7 4.7 %collective-permute-done.5 = bf16[32,1664]{1,0:T(8,128)(2,1)S(1)} collective-permute-done((bf16[32,1664]{1,0:T(8,128)(2,1)S(1)}, bf16[32,1664]{1,0:T(8,128)(2,1)S(1)}, u32[]{:S(2)}, u32[]{:S(2)}) %collective-permute-start.5) | collective-permute-done | bytes 106528 | tf_op jit(solution)/shard_map/ppermute | solution.py:34
  158.3 3.7 %collective-permute-done.4 = bf16[32,1664]{1,0:T(8,128)(2,1)S(1)} collective-permute-done((bf16[32,1664]{1,0:T(8,128)(2,1)S(1)}, bf16[32,1664]{1,0:T(8,128)(2,1)S(1)}, u32[]{:S(2)}, u32[]{:S(2)}) %collective-permute-start.4) | collective-permute-done | bytes 106528 | tf_op jit(solution)/shard_map/ppermute | solution.py:34
  163.2 1.6 fusion.3
  (112 shorter events, 23.0 us)
Async XLA Ops:
  0.6 60.3 %copy-start = (bf16[1536,304]{0,1:T(8,128)(2,1)S(1)}, bf16[1536,304]{0,1:T(8,128)(2,1)}, u32[]{:S(2)}) copy-start(bf16[1536,304]{0,1:T(8,128)(2,1)} %param.23) | copy-start | bytes 2801668
  0.7 33.0 %copy-start.29 = (s32[2]{0:T(128)}, s32[2]{0:T(128)S(1)}, u32[]{:S(2)}) copy-start(s32[2]{0:T(128)S(1)} %pad_add_fusion.device_ref) | copy-start | bytes 28
  24.2 9.5 %copy-start.38 = (s32[32]{0:T(128)}, s32[32]{0:T(128)S(1)}, u32[]{:S(2)}) copy-start(s32[32]{0:T(128)S(1)} %get-tuple-element.19.recv_ref) | copy-start | bytes 388
  33.8 6.5 %copy-start.41 = (bf16[32,1536]{1,0:T(8,128)(2,1)S(1)}, bf16[32,1536]{1,0:T(8,128)(2,1)}, u32[]{:S(2)}) copy-start(bf16[32,1536]{1,0:T(8,128)(2,1)} %param.20) | copy-start | bytes 294916
  33.8 7.4 %copy-start.42 = (f32[1536]{0:T(1024)S(1)}, f32[1536]{0:T(1024)}, u32[]{:S(2)}) copy-start(f32[1536]{0:T(1024)} %param.21) | copy-start | bytes 18436
  33.8 12.6 %copy-start.43 = (f32[768]{0:T(1024)S(1)}, f32[768]{0:T(1024)}, u32[]{:S(2)}) copy-start(f32[768]{0:T(1024)} %param.25) | copy-start | bytes 9220
  33.8 13.1 %copy-start.44 = (f32[768]{0:T(1024)S(1)}, f32[768]{0:T(1024)}, u32[]{:S(2)}) copy-start(f32[768]{0:T(1024)} %param.31) | copy-start | bytes 9220
  33.8 13.7 %copy-start.45 = (s32[32]{0:T(128)S(1)}, s32[32]{0:T(128)}, u32[]{:S(2)}) copy-start(s32[32]{0:T(128)} %param.36) | copy-start | bytes 388
  33.8 93.5 %all-to-all-start.1 = ((bf16[40,12,64,128]{3,2,1,0:T(8,128)(2,1)}), bf16[40,12,64,128]{3,2,1,0:T(8,128)(2,1)}, u32[]{:S(2)}, u32[]{:S(2)}) async-start(bf16[40,12,64,128]{3,2,1,0:T(8,128)(2,1)} %copy-done.1), calls=%async_computation.1 | async-start | bytes 15728640 | tf_op jit(solution)/shard_map/all_to_all | solution.py:457
  41.9 15.9 %collective-permute-start.1 = (bf16[32,1536]{1,0:T(8,128)(2,1)}, bf16[32,1536]{1,0:T(8,128)(2,1)}, u32[]{:S(2)}, u32[]{:S(2)}) collective-permute-start(bf16[32,1536]{1,0:T(8,128)(2,1)} %get-tuple-element.35), channel_id=1, source_target_pairs={{0,2},{1,3},{2,0},{3,1},{4,6},{5,7},{6,4},{7,5},{8,10},{9,11},{10,... | collective-permute-start | bytes 294920 | tf_op jit(solution)/shard_map/ppermute | solution.py:34
  44.5 11.8 %collective-permute-start = (bf16[32,1536]{1,0:T(8,128)(2,1)}, bf16[32,1536]{1,0:T(8,128)(2,1)}, u32[]{:S(2)}, u32[]{:S(2)}) collective-permute-start(bf16[32,1536]{1,0:T(8,128)(2,1)} %get-tuple-element.35), channel_id=1, source_target_pairs={{0,1},{1,0},{2,3},{3,2},{4,5},{5,4},{6,7},{7,6},{8,9},{9,8},{10,11... | collective-permute-start | bytes 294920 | tf_op jit(solution)/shard_map/ppermute | solution.py:34
  46.1 13.3 %collective-permute-start.2 = (bf16[32,1536]{1,0:T(8,128)(2,1)}, bf16[32,1536]{1,0:T(8,128)(2,1)}, u32[]{:S(2)}, u32[]{:S(2)}) collective-permute-start(bf16[32,1536]{1,0:T(8,128)(2,1)} %get-tuple-element.35), channel_id=1, source_target_pairs={{0,3},{1,2},{2,1},{3,0},{4,7},{5,6},{6,5},{7,4},{8,11},{9,10},{10,... | collective-permute-start | bytes 294920 | tf_op jit(solution)/shard_map/ppermute | solution.py:34
  53.7 73.5 %copy-start.3 = (bf16[768,1536]{1,0:T(8,128)(2,1)S(1)}, bf16[768,1536]{1,0:T(8,128)(2,1)}, u32[]{:S(2)}) copy-start(bf16[768,1536]{1,0:T(8,128)(2,1)} %refs_11_.1) | copy-start | bytes 7077892
  64.6 3.4 %copy-start.28 = (f32[4,256]{1,0:T(4,128)S(1)}, f32[4,256]{1,0:T(4,128)}, u32[]{:S(2)}) copy-start(f32[4,256]{1,0:T(4,128)} %conv_shared_ref.1) | copy-start | bytes 12292
  64.6 3.4 %copy-start.30 = (s32[2]{0:T(128)S(1)}, s32[2]{0:T(128)}, u32[]{:S(2)}) copy-start(s32[2]{0:T(128)} %copy-done.29) | copy-start | bytes 28
  64.6 3.4 %copy-start.31 = (f32[1,128]{1,0:T(1,128)S(1)}, f32[1,128]{1,0:T(1,128)}, u32[]{:S(2)}) copy-start(f32[1,128]{1,0:T(1,128)} %get-tuple-element.39.decay_log_ref) | copy-start | bytes 1540
  64.6 3.4 %copy-start.32 = (f32[1,128]{1,0:T(1,128)S(1)}, f32[1,128]{1,0:T(1,128)}, u32[]{:S(2)}) copy-start(f32[1,128]{1,0:T(1,128)} %get-tuple-element.40.step_bias_ref) | copy-start | bytes 1540
  64.6 3.4 %copy-start.34 = (f32[256]{0:T(256)S(1)}, f32[256]{0:T(256)}, u32[]{:S(2)}) copy-start(f32[256]{0:T(256)} %param.27) | copy-start | bytes 3076
  64.6 3.4 %copy-start.37 = (f32[12]{0:T(128)S(1)}, f32[12]{0:T(128)}, u32[]{:S(2)}) copy-start(f32[12]{0:T(128)} %skip_ref.1) | copy-start | bytes 148
  133.7 18.6 %copy-start.17 = (bf16[128,256]{1,0:T(8,128)(2,1)S(1)}, bf16[128,256]{1,0:T(8,128)(2,1)}, u32[]{:S(2)}) copy-start(bf16[128,256]{1,0:T(8,128)(2,1)} %copy-done.16) | copy-start | bytes 196612
  133.7 19.2 %copy-start.14 = (bf16[128,768]{1,0:T(8,128)(2,1)S(1)}, bf16[128,768]{1,0:T(8,128)(2,1)}, u32[]{:S(2)}) copy-start(bf16[128,768]{1,0:T(8,128)(2,1)} %copy-done.13) | copy-start | bytes 589828
  148.0 5.6 %collective-permute-start.3 = (bf16[32,1664]{1,0:T(8,128)(2,1)S(1)}, bf16[32,1664]{1,0:T(8,128)(2,1)S(1)}, u32[]{:S(2)}, u32[]{:S(2)}) collective-permute-start(bf16[32,1664]{1,0:T(8,128)(2,1)S(1)} %get-tuple-element.36), channel_id=1, source_target_pairs={{0,1},{1,0},{2,3},{3,2},{4,5},{5,4},{6,7},{7,6},{8,9},{9,8},{10,11... | collective-permute-start | bytes 319496 | tf_op jit(solution)/shard_map/ppermute | solution.py:34
  149.7 8.7 %collective-permute-start.5 = (bf16[32,1664]{1,0:T(8,128)(2,1)S(1)}, bf16[32,1664]{1,0:T(8,128)(2,1)S(1)}, u32[]{:S(2)}, u32[]{:S(2)}) collective-permute-start(bf16[32,1664]{1,0:T(8,128)(2,1)S(1)} %get-tuple-element.37), channel_id=1, source_target_pairs={{0,3},{1,2},{2,1},{3,0},{4,7},{5,6},{6,5},{7,4},{8,11},{9,10},{10,... | collective-permute-start | bytes 319496 | tf_op jit(solution)/shard_map/ppermute | solution.py:34
  152.2 9.9 %collective-permute-start.4 = (bf16[32,1664]{1,0:T(8,128)(2,1)S(1)}, bf16[32,1664]{1,0:T(8,128)(2,1)S(1)}, u32[]{:S(2)}, u32[]{:S(2)}) collective-permute-start(bf16[32,1664]{1,0:T(8,128)(2,1)S(1)} %get-tuple-element.38), channel_id=1, source_target_pairs={{0,2},{1,3},{2,0},{3,1},{4,6},{5,7},{6,4},{7,5},{8,10},{9,11},{10,... | collective-permute-start | bytes 319496 | tf_op jit(solution)/shard_map/ppermute | solution.py:34
  (29 other events, 39.2 us)

commit v2 on v1

v2 whole, which is shorter than its diff:
```python
import functools

import jax
import jax.numpy as jnp
from jax import lax
from jax.experimental import pallas as pl
from jax.experimental.pallas import tpu as pltpu
from jax.sharding import PartitionSpec as P

EPS = 1e-05
F32 = jnp.float32
BF16 = jnp.bfloat16
VMEM_BYTES = 63 * 1024 * 1024
CHEAP = pl.CostEstimate(flops=1, bytes_accessed=1, transcendentals=0)
HBM = pl.BlockSpec(memory_space=pltpu.HBM)
SMEM = pl.BlockSpec(memory_space=pltpu.SMEM)
VMEM = pl.BlockSpec(memory_space=pltpu.VMEM)


def peer_of(index, step, size):
    if size & (size - 1) == 0:
        return index ^ step
    return lax.rem(index + step, size)


def origin_of(index, step, size):
    if size & (size - 1) == 0:
        return index ^ step
    return lax.rem(index - step + size, size)


def permute(value, axis, step):
    size = lax.axis_size(axis)
    pairs = [(i, i ^ step if size & (size - 1) == 0 else (i + step) % size) for i in range(size)]
    return lax.ppermute(value, axis, pairs)


def invert(order, place):
    def one(slot, carry):
        place[order[slot]] = slot
        return carry

    lax.fori_loop(0, order.shape[0], one, 0, unroll=16)


def fetch(pairs, done, first=0):
    copies = [pltpu.make_async_copy(source, target, done.at[first + n]) for n, (source, target) in enumerate(pairs)]
    for copy in copies:
        copy.start()
    return copies


def pack_kernel(
    groups,
    slots,
    early,
    capacity,
    edge_block,
    chunk,
    ids_hbm,
    dest_hbm,
    reorder_hbm,
    inner_hbm,
    shared_hbm,
    states_ref,
    slot_of,
    recv_rows,
    new_slots,
    out_edges,
    leaving,
    out_late,
    *refs,
):
    out_early = refs[: groups - 1] if early else []
    ids, dest, reorder, place, edge_place, seen, kept, staged, inner, shared, read_done, write_done, small_done = refs[len(out_early) :]
    stride = slots // groups
    device = lax.axis_index("req")
    first = device * slots
    small = fetch(((ids_hbm, ids), (dest_hbm, dest), (reorder_hbm, reorder)), small_done)
    parts = [pl.ds(part * chunk, chunk) for part in range(slots // chunk)]
    reads = fetch([(states_ref.at[part], staged.at[part]) for part in parts], read_done)
    edges = fetch(((inner_hbm, inner), (shared_hbm, shared)), small_done, 3)
    for copy in small:
        copy.wait()
    invert(reorder, place)
    for group in range(groups):
        seen[group] = 0
    moving = ids[device] - first
    dump = groups * stride

    def to_peer(slot, carry):
        peer = lax.div(place[first + slot], slots)
        rank = seen[peer]
        stays = slot != moving
        slot_of[jnp.where(stays, peer * stride + rank, dump)] = slot
        edge_place[slot] = peer * edge_block + rank
        seen[peer] = rank + stays.astype(jnp.int32)
        return carry

    lax.fori_loop(0, slots, to_peer, 0, unroll=4)
    peer = lax.div(place[dest[device]], slots)
    edge_place[moving] = peer * edge_block + seen[peer]
    peer = lax.div(place[first + moving], slots)
    slot_of[peer * stride + seen[peer]] = moving

    for read in reads:
        read.wait()
    writes = [pltpu.make_async_copy(staged.at[moving], leaving, write_done.at[0])]
    writes[-1].start()
    for step in range(1, groups):
        peer = peer_of(device, step, groups)
        for rank in range(early):
            slot = slot_of[peer * stride + rank]
            writes.append(pltpu.make_async_copy(staged.at[slot], out_early[step - 1].at[rank], write_done.at[0]))
            writes[-1].start()
    for peer in range(groups):
        slot = slot_of[peer * stride + stride - 1]
        writes.append(pltpu.make_async_copy(staged.at[slot], out_late.at[peer], write_done.at[0]))
        writes[-1].start()

    keep = inner.shape[0]
    rows = groups * edge_block
    lane = lax.broadcasted_iota(jnp.int32, (1, slots), 1)
    places = jnp.zeros((1, slots), jnp.int32)
    for slot in range(slots):
        places = jnp.where(lane == slot, edge_place[slot], places)
    row = lax.broadcasted_iota(jnp.int32, (rows, slots), 0)
    inner_sum = jnp.zeros((rows, inner.shape[2]), F32)
    shared_sum = jnp.zeros((rows, shared.shape[2]), F32)
    for copy in edges:
        copy.wait()
    for k in range(keep):
        pick = jnp.where(row == places + k * capacity, 1.0, 0.0).astype(BF16)
        inner_sum = inner_sum + jnp.dot(pick, inner[k], preferred_element_type=F32)
        shared_sum = shared_sum + jnp.dot(pick, shared[k], preferred_element_type=F32)
    packed = jnp.concatenate([inner_sum, shared_sum], axis=1).astype(BF16)
    lanes = out_edges.shape[2]
    for peer in range(groups):
        for block in range(packed.shape[1] // lanes):
            here = packed[peer * edge_block : (peer + 1) * edge_block, block * lanes : (block + 1) * lanes]
            out_edges[peer, block * edge_block : (block + 1) * edge_block, :] = here

    def from_origin(origin, carry):
        away = ids[origin]

        def one(slot, rank):
            old = origin * slots + slot
            new = place[old] - first
            mine = jnp.logical_and(jnp.logical_and(new >= 0, new < slots), old != away)
            new_slots[jnp.where(mine, origin * stride + rank, dump)] = new
            recv_rows[jnp.where(mine, new, slots)] = origin * edge_block + rank
            return rank + mine.astype(jnp.int32)

        rank = lax.fori_loop(0, slots, one, 0, unroll=8)
        kept[origin] = rank
        new = place[away] - first
        mine = jnp.logical_and(new >= 0, new < slots)
        new_slots[jnp.where(mine, origin * stride + rank, dump)] = new
        return carry

    lax.fori_loop(0, groups, from_origin, 0)

    def migrated(origin, carry):
        new = place[dest[origin]] - first
        mine = jnp.logical_and(new >= 0, new < slots)
        recv_rows[jnp.where(mine, new, slots)] = origin * edge_block + kept[origin]
        return carry

    lax.fori_loop(0, groups, migrated, 0)
    for write in writes:
        write.wait()


def pack(mig_ids, mig_dest, reorder, edge_inner, edge_shared, states, groups, early, capacity, edge_block):
    slots = states.shape[0]
    stride = slots // groups
    width = edge_inner.shape[2] + edge_shared.shape[2]
    lanes = states.shape[3]
    chunk = 8
    shape = jax.ShapeDtypeStruct
    peers = groups - 1 if early else 0
    inner = edge_inner.transpose(1, 0, 2)
    shared = edge_shared.transpose(1, 0, 2)
    return pl.pallas_call(
        functools.partial(pack_kernel, groups, slots, early, capacity, edge_block, chunk),
        out_shape=(
            shape((slots + 1,), jnp.int32),
            shape((slots + 1,), jnp.int32),
            shape((slots + 1,), jnp.int32),
            shape((groups, edge_block * width // lanes, lanes), BF16),
            shape(states.shape[1:], BF16),
            shape((groups,) + states.shape[1:], BF16),
        )
        + (shape((early,) + states.shape[1:], BF16),) * peers,
        in_specs=[HBM] * 6,
        out_specs=(SMEM, SMEM, SMEM, VMEM, HBM, HBM) + (HBM,) * peers,
        scratch_shapes=[
            pltpu.SMEM(mig_ids.shape, jnp.int32),
            pltpu.SMEM(mig_dest.shape, jnp.int32),
            pltpu.SMEM(reorder.shape, jnp.int32),
            pltpu.SMEM(reorder.shape, jnp.int32),
            pltpu.SMEM((slots,), jnp.int32),
            pltpu.SMEM((groups,), jnp.int32),
            pltpu.SMEM((groups,), jnp.int32),
            pltpu.VMEM(states.shape, states.dtype),
            pltpu.VMEM(inner.shape, BF16),
            pltpu.VMEM(shared.shape, BF16),
            pltpu.SemaphoreType.DMA((slots // chunk,)),
            pltpu.SemaphoreType.DMA((1,)),
            pltpu.SemaphoreType.DMA((5,)),
        ],
        compiler_params=pltpu.CompilerParams(vmem_limit_bytes=VMEM_BYTES),
        cost_estimate=CHEAP,
        name="pack",
    )(mig_ids, mig_dest, reorder, inner, shared, states)


def shift_rows(value, by):
    by = by % value.shape[0]
    return pltpu.roll(value, by, 0) if by else value


def mix(edge, fresh, weight, bias, token):
    taps = weight.shape[0]
    summed = fresh * weight[taps - 1 : taps] + bias
    for tap in range(taps - 1):
        back = taps - 1 - tap
        moved = jnp.where(token >= back, shift_rows(fresh, back), shift_rows(edge, -tap))
        summed = summed + moved * weight[tap : tap + 1]
    return summed / (1.0 + jnp.exp(-summed))


def latest(edge, fresh, counts, token, window):
    keep = window - 1
    result = edge
    for length in range(1, window + 1):
        chosen = jnp.where(token + length < keep, shift_rows(edge, -length), shift_rows(fresh, keep - length))
        result = jnp.where(counts == length, chosen, result)
    return result


def token_kernel(
    window,
    heads,
    head_dim,
    state_dim,
    capacity,
    skip_ref,
    recv_ref,
    rows_ref,
    shared_ref,
    edges_ref,
    counts_ref,
    conv_inner_ref,
    inner_bias_ref,
    conv_shared_ref,
    shared_bias_ref,
    step_bias_ref,
    decay_log_ref,
    moved_ref,
    entry_ref,
    readout_ref,
    within_ref,
    decay_ref,
    gate_ref,
    new_inner_ref,
    new_shared_ref,
):
    inner = heads * head_dim
    rows = rows_ref.shape[0]
    wide = lax.broadcasted_iota(jnp.int32, (rows, 1), 0)
    token = lax.rem(wide, window)
    counts = counts_ref[...]
    valid = token < counts

    arrived = edges_ref.shape[0]
    place = jnp.zeros((rows, 1), jnp.int32)
    for slot in range(rows // window):
        place = jnp.where(lax.div(wide, window) == slot, recv_ref[slot], place)
    pick = lax.broadcasted_iota(jnp.int32, (rows, arrived), 1) == place + token * capacity
    pick = jnp.logical_and(pick, token < window - 1)
    edges = jnp.dot(jnp.where(pick, 1.0, 0.0).astype(BF16), edges_ref[...], preferred_element_type=F32)

    gate = rows_ref[:, :inner].astype(F32)
    gate_ref[...] = jnp.where(valid, gate / (1.0 + jnp.exp(-gate)), 0.0)

    value = rows_ref[:, inner:].astype(F32)
    edge = edges[:, :inner]
    keep = window - 1
    slots = rows // window
    row = lax.broadcasted_iota(jnp.int32, (slots, rows), 0)
    lane = lax.broadcasted_iota(jnp.int32, (slots, rows), 1)
    takes = [jnp.where(lane == row * window + k, 1.0, 0.0).astype(BF16) for k in range(keep)]
    newest = latest(edge, value, counts, token, window).astype(BF16)
    for k in range(keep):
        new_inner_ref[k] = jnp.dot(takes[k], newest, preferred_element_type=F32).astype(BF16)
    mixed = mix(edge, value, conv_inner_ref[...], inner_bias_ref[...], token)

    fresh = shared_ref[:, : 2 * state_dim].astype(F32)
    edge = edges[:, inner:]
    newest = latest(edge, fresh, counts, token, window).astype(BF16)
    for k in range(keep):
        new_shared_ref[k] = jnp.dot(takes[k], newest, preferred_element_type=F32).astype(BF16)
    shared = mix(edge, fresh, conv_shared_ref[...], shared_bias_ref[...], token)
    entry = shared[:, :state_dim]
    readout = shared[:, state_dim:]
    entry_ref[...] = entry.astype(BF16)
    readout_t = readout.T.astype(BF16)
    readout_ref[...] = readout_t

    raw = shared_ref[:, 2 * state_dim :]
    all_heads = raw.shape[1]
    from_head = lax.broadcasted_iota(jnp.int32, (all_heads, rows), 0)
    to_lane = lax.broadcasted_iota(jnp.int32, (all_heads, rows), 1)
    pick = jnp.logical_and(from_head == to_lane + lax.axis_index("head") * heads, to_lane < heads)
    raw = jnp.dot(raw, pick.astype(BF16), preferred_element_type=F32) + step_bias_ref[...]
    step = jnp.maximum(raw, 0.0) + jnp.log(1.0 + jnp.exp(-jnp.abs(raw)))
    step = jnp.where(valid, step, 0.0)
    drop = step * -jnp.exp(decay_log_ref[...])
    total = drop
    after = drop
    reach = 1
    while reach < window:
        total = total + jnp.where(token >= reach, shift_rows(total, reach), 0.0)
        after = after + jnp.where(token + reach < window, shift_rows(after, -reach), 0.0)
        reach *= 2
    after = jnp.where(token + 1 < window, shift_rows(after, -1), 0.0)
    total_t = total.T
    decay_ref[...] = jnp.exp(total_t)[: decay_ref.shape[0]]
    carry_t = (step * jnp.exp(after)).T

    slot_a = lax.div(lax.broadcasted_iota(jnp.int32, (rows, rows), 0), window)
    slot_b = lax.div(lax.broadcasted_iota(jnp.int32, (rows, rows), 1), window)
    row_a = lax.broadcasted_iota(jnp.int32, (rows, rows), 0)
    row_b = lax.broadcasted_iota(jnp.int32, (rows, rows), 1)
    causal = jnp.logical_and(slot_a == slot_b, row_a <= row_b)
    overlap = jnp.dot(entry.astype(BF16), readout_t, preferred_element_type=F32)
    overlap = jnp.where(causal, overlap, 0.0)
    for block in range(inner // rows):
        turned = mixed[:, block * rows : (block + 1) * rows].T
        for part in range(rows // head_dim):
            head = block * (rows // head_dim) + part
            mine = turned[part * head_dim : (part + 1) * head_dim]
            here = pl.ds(head * head_dim, head_dim)
            moved_ref[here, :] = (mine * carry_t[head : head + 1]).astype(BF16)
            gap = jnp.minimum(total_t[head : head + 1] - total[:, head : head + 1], 0.0)
            weight = overlap * jnp.exp(gap) * step[:, head : head + 1]
            within_ref[here, :] = skip_ref[head] * mine + jnp.dot(
                mine.astype(BF16), weight.astype(BF16), preferred_element_type=F32
            )


def token_part(
    skip_gain, recv_rows, rows, shared, edges, counts, conv_inner, inner_bias, conv_shared, shared_bias, step_bias, decay_log, window, heads, head_dim, state_dim, capacity
):
    count = rows.shape[0]
    inner = heads * head_dim
    padded = -(-heads // 8) * 8
    shape = jax.ShapeDtypeStruct
    return pl.pallas_call(
        functools.partial(token_kernel, window, heads, head_dim, state_dim, capacity),
        out_shape=(
            shape((inner, count), BF16),
            shape((count, state_dim), BF16),
            shape((state_dim, count), BF16),
            shape((inner, count), F32),
            shape((padded, count), F32),
            shape((count, inner), F32),
            shape((window - 1, count // window, inner), BF16),
            shape((window - 1, count // window, 2 * state_dim), BF16),
        ),
        in_specs=[SMEM] * 2 + [VMEM] * 10,
        out_specs=(VMEM,) * 8,
        compiler_params=pltpu.CompilerParams(vmem_limit_bytes=VMEM_BYTES),
        cost_estimate=CHEAP,
        name="token_rows",
    )(skip_gain, recv_rows, rows, shared, edges, counts, conv_inner, inner_bias, conv_shared, shared_bias, step_bias, decay_log)


def page_jobs(groups, stride, steps, pages, late, states_ref, new_slots, slot_of):
    device = lax.axis_index("req")
    jobs = []
    pages = list(pages)
    for step in steps:
        origin = origin_of(device, step, groups)
        arrived = pages.pop(0) if step else None
        for rank in range(stride - 1):
            at = origin * stride + rank
            jobs.append((arrived.at[rank] if step else states_ref.at[slot_of[at]], new_slots[at]))
    if late is not None:
        jobs += [(late.at[origin], new_slots[origin * stride + stride - 1]) for origin in range(groups)]
    return jobs


def load_pages(jobs, batch, pages_in, read_done):
    return fetch([(source, pages_in.at[n]) for n, (source, _) in enumerate(jobs)], read_done)


def batches(jobs, batch):
    return [range(start, min(start + batch, len(jobs))) for start in range(0, len(jobs), batch)]


def read_pages(window, batch, jobs, loads, pages_in, readout):
    heads, head_dim, state_dim = pages_in.shape[1:]
    count = readout.shape[1]
    lane_slot = lax.div(lax.broadcasted_iota(jnp.int32, (state_dim, count), 1), window)
    total = None
    for group in batches(jobs, batch):
        for n in group:
            loads[n].wait()
        wanted = [jnp.where(lane_slot == jobs[n][1], readout[...], jnp.zeros((), BF16)) for n in group]
        held = jnp.concatenate([pages_in[n].reshape(heads * head_dim, state_dim) for n in group], axis=1)
        read = jnp.dot(held, jnp.concatenate(wanted, axis=0), preferred_element_type=F32)
        total = read if total is None else total + read
    return total


def update_pages(window, batch, jobs, loads, pages_in, pages_out, write_done, out_ref, moved, entry, decay):
    heads, head_dim, state_dim = pages_in.shape[1:]
    count = entry.shape[0]
    row_slot = lax.div(lax.broadcasted_iota(jnp.int32, (count, state_dim), 0), window)
    stores = []
    for group in batches(jobs, batch):
        for n in group if loads else ():
            loads[n].wait()
        entries = [jnp.where(row_slot == jobs[n][1], entry[...], jnp.zeros((), BF16)) for n in group]
        added = jnp.dot(moved[...], jnp.concatenate(entries, axis=1), preferred_element_type=F32)
        for q, n in enumerate(group):
            slot = jobs[n][1]
            lane = slot * window + window - 1
            for head in range(heads):
                here = slice(head * head_dim, (head + 1) * head_dim)
                kept = pages_in[n, head].astype(F32) * decay[head, lane]
                pages_out[n, head] = (kept + added[here, q * state_dim : (q + 1) * state_dim]).astype(BF16)
            stores.append(pltpu.make_async_copy(pages_out.at[n], out_ref.at[slot], write_done.at[0]))
            stores[-1].start()
    return stores


def early_kernel(window, batch, groups, stride, steps, new_slots, slot_of, decay_hbm, moved_hbm, entry_hbm, readout_hbm, states_ref, *refs):
    count = len([step for step in steps if step])
    out_ref, read_ref, moved, entry, readout, decay, pages_in, pages_out, read_done, write_done, small_done = refs[count:]
    pairs = ((decay_hbm, decay), (moved_hbm, moved), (entry_hbm, entry), (readout_hbm, readout))
    small = fetch(pairs, small_done)
    jobs = page_jobs(groups, stride, steps, refs[:count], None, states_ref, new_slots, slot_of)
    loads = load_pages(jobs, batch, pages_in, read_done)
    for copy in small:
        copy.wait()
    read_ref[...] = read_pages(window, batch, jobs, loads, pages_in, readout)
    for store in update_pages(window, batch, jobs, [], pages_in, pages_out, write_done, out_ref, moved, entry, decay):
        store.wait()


def hidden_kernel(
    window,
    batch,
    groups,
    stride,
    shares,
    steps,
    heads,
    head_dim,
    started,
    new_slots,
    decay_hbm,
    readout_hbm,
    within_hbm,
    gate_hbm,
    gain_hbm,
    weight_hbm,
    late,
    *refs,
):
    pages, refs = refs[: len(steps)], refs[len(steps) :]
    read_hbm = refs[0] if started else None
    refs = refs[1 if started else 0 :]
    messages, refs = refs[:shares], refs[shares:]
    readout, decay, within, gate, gain, weight, read, rows_all, pages_in, read_done, small_done = refs
    jobs = page_jobs(groups, stride, steps, pages, late, None, new_slots, None)
    pairs = [(readout_hbm, readout), (decay_hbm, decay), (within_hbm, within), (gate_hbm, gate), (gain_hbm, gain), (weight_hbm, weight)]
    small = fetch(pairs[:1], small_done)
    loads = load_pages(jobs, batch, pages_in, read_done)
    small += fetch(pairs[1:] + ([(read_hbm, read)] if started else []), small_done, 1)
    small[0].wait()
    total = read_pages(window, batch, jobs, loads, pages_in, readout)
    for copy in small[1:]:
        copy.wait()
    read[...] = total + read[...] if started else total
    count, inner = gate.shape
    factor = decay[...]
    blocks = []
    for block in range(inner // count):
        parts = []
        for part in range(count // head_dim):
            head = block * (count // head_dim) + part
            here = pl.ds(head * head_dim, head_dim)
            parts.append(read[here, :] * factor[head : head + 1] + within[here, :])
        blocks.append(jnp.concatenate(parts, axis=0).T)
    gated = jnp.concatenate(blocks, axis=1) * gate[...]
    squares = jnp.sum(gated * gated, axis=1, keepdims=True)
    high = squares.astype(BF16)
    low = (squares - high.astype(F32)).astype(BF16)
    scaled = (gated * gain[...]).astype(BF16)
    width = weight.shape[1]
    rows_all[:, :width] = jnp.dot(scaled, weight[...], preferred_element_type=F32).astype(BF16)
    lane = lax.broadcasted_iota(jnp.int32, (count, rows_all.shape[1] - width), 1)
    rows_all[:, width:] = jnp.where(lane == 0, high, jnp.where(lane == 1, low, jnp.zeros((), BF16)))
    own = count // shares
    for step in range(shares):
        start = peer_of(lax.axis_index("head"), step, shares) * own
        messages[step][...] = rows_all[pl.ds(pl.multiple_of(start, own), own), :]


def update_kernel(window, batch, groups, stride, steps, started, new_slots, decay_hbm, moved_hbm, entry_hbm, late, *refs):
    pages, refs = refs[: len(steps)], refs[len(steps) + (1 if started else 0) :]
    out_ref, moved, entry, decay, pages_in, pages_out, read_done, write_done, small_done = refs
    small = fetch(((decay_hbm, decay), (moved_hbm, moved), (entry_hbm, entry)), small_done)
    jobs = page_jobs(groups, stride, steps, pages, late, None, new_slots, None)
    loads = load_pages(jobs, batch, pages_in, read_done)
    for copy in small:
        copy.wait()
    for store in update_pages(window, batch, jobs, loads, pages_in, pages_out, write_done, out_ref, moved, entry, decay):
        store.wait()


def state_part(new_slots, slot_of, early_pages, steps, late, states, moved, entry, readout, within, decay, gate, gain, out_weight, window, groups, shares):
    slots, heads, head_dim, _ = states.shape
    page = states.shape[1:]
    stride = slots // groups
    count, inner = gate.shape
    width = out_weight.shape[1]
    shape = jax.ShapeDtypeStruct
    new_states = shape(states.shape, BF16)
    batch = 4
    rest = [step for step in early_pages if step not in steps]
    others = [early_pages[step] for step in rest]
    params = pltpu.CompilerParams(vmem_limit_bytes=VMEM_BYTES)

    def held(*arrays):
        return [pltpu.VMEM(array.shape, array.dtype) for array in arrays]

    def paging(jobs, copies):
        return [pltpu.VMEM((jobs,) + page, BF16)] * copies + [pltpu.SemaphoreType.DMA((jobs,))]

    done = pltpu.SemaphoreType.DMA
    decay_scalars = pltpu.SMEM(decay.shape, F32)
    read, begun = [], []
    if steps:
        arrived = [early_pages[step] for step in steps if step]
        operands = [new_slots, slot_of, decay, moved, entry, readout, states] + arrived
        out = pl.pallas_call(
            functools.partial(early_kernel, window, batch, groups, stride, steps),
            out_shape=(new_states, shape((inner, count), F32)),
            in_specs=[SMEM] * 2 + [HBM] * (len(operands) - 2),
            out_specs=(HBM, VMEM),
            scratch_shapes=held(moved, entry, readout) + [decay_scalars] + paging(len(steps) * (stride - 1), 2) + [done((1,)), done((4,))],
            compiler_params=params,
            cost_estimate=CHEAP,
            name="early_pages",
        )(*operands)
        begun, read = [out[0]], [out[1]]
    jobs = groups + len(rest) * (stride - 1)
    operands = [new_slots, decay, readout, within, gate, gain, out_weight, late] + others + read
    message = shape((count // shares, width + 128), BF16)
    messages = pl.pallas_call(
        functools.partial(hidden_kernel, window, batch, groups, stride, shares, rest, heads, head_dim, bool(read)),
        out_shape=(message,) * shares,
        in_specs=[SMEM] + [HBM] * (len(operands) - 1),
        out_specs=(VMEM,) * shares,
        scratch_shapes=held(readout, decay, within, gate, gain, out_weight, within)
        + [pltpu.VMEM((count, width + 128), BF16)]
        + paging(jobs, 1)
        + [done((7,))],
        compiler_params=params,
        cost_estimate=CHEAP,
        name="hidden_rows",
    )(*operands)
    operands = [new_slots, decay, moved, entry, late] + others + begun
    out = pl.pallas_call(
        functools.partial(update_kernel, window, batch, groups, stride, rest, bool(begun)),
        out_shape=new_states,
        in_specs=[SMEM] + [HBM] * (len(operands) - 1),
        out_specs=HBM,
        scratch_shapes=held(moved, entry) + [decay_scalars] + paging(jobs, 2) + [done((1,)), done((3,))],
        input_output_aliases={len(operands) - 1: 0} if begun else {},
        compiler_params=params,
        cost_estimate=pl.CostEstimate(flops=1, bytes_accessed=4 * states.size, transcendentals=0),
        name="late_pages",
    )(*operands)
    return out, messages


def local(
    tokens,
    pre_gain,
    inner_weight,
    shared_weight,
    conv_inner,
    conv_inner_bias,
    conv_shared,
    conv_shared_bias,
    step_bias,
    decay_log,
    skip_gain,
    gate_gain,
    out_weight,
    states,
    edge_inner,
    edge_shared,
    counts,
    mig_ids,
    mig_dest,
    reorder,
):
    slots, heads, head_dim, state_dim = states.shape
    inner = heads * head_dim
    groups = lax.axis_size("req")
    shares = lax.axis_size("head")
    request_index = lax.axis_index("req")
    head_index = lax.axis_index("head")
    own_rows = tokens.shape[0]
    window = own_rows * shares // slots
    width = tokens.shape[1]
    stride = slots // groups
    keep = edge_inner.shape[1]
    early = stride - 1
    capacity = stride + 1
    edge_block = -(-keep * capacity // 16) * 16
    exchange = functools.partial(lax.all_to_all, axis_name="req", split_axis=0, concat_axis=0, tiled=True)

    packed = pack(mig_ids, mig_dest, reorder, edge_inner, edge_shared, states, groups, early, capacity, edge_block)
    slot_of, recv_rows, new_slots, send_edges, page, send_late = packed[:6]
    early_pages = {step: permute(sent, "req", step) for step, sent in enumerate(packed[6:], 1)}
    first = list(range(2, groups, 2))[:2] if early_pages else []
    rest = [step for step in range(2, groups) if step not in first] if early_pages else []
    edge_rows = send_edges.shape[1]
    pieces = exchange(jnp.concatenate([send_edges, page.reshape(groups, inner // groups, state_dim)], axis=1))
    edges = pieces[:, :edge_rows].reshape(groups, -1, edge_block, state_dim).transpose(0, 2, 1, 3)
    edges = edges.reshape(groups * edge_block, -1)
    rows_in = tokens.astype(F32)
    normed = (rows_in * lax.rsqrt(jnp.mean(rows_in * rows_in, axis=-1, keepdims=True) + EPS) * pre_gain).astype(BF16)
    normed, pieces = lax.optimization_barrier((normed, pieces))
    all_rows = lax.all_to_all(jnp.tile(normed, (shares, 1)), "head", split_axis=0, concat_axis=0, tiled=True)
    comes_from = jnp.argmax(mig_dest[None, :] == mig_ids[:, None], axis=1)
    first_pages = [early_pages[step] for step in first]
    pieces, all_rows, first_pages = lax.optimization_barrier((pieces[comes_from, edge_rows:], all_rows, first_pages))
    early_pages.update(zip(first, first_pages))
    arrived = exchange(pieces).reshape(states.shape[1:])
    leaving = lax.dynamic_index_in_dim(mig_ids, request_index, 0, keepdims=False)
    target = jnp.argmax(reorder == leaving) // slots
    inner_flat = inner_weight.reshape(width, 2 * inner)
    inner_rows = jnp.dot(all_rows, inner_flat, preferred_element_type=F32).astype(BF16)
    shared_rows = jnp.dot(all_rows, shared_weight, preferred_element_type=F32).astype(BF16)

    lanes = slots * window

    def in_lanes(vector):
        return jnp.pad(vector, (0, lanes - heads)).reshape(1, lanes)

    moved, entry, readout, within, decay, gate, new_inner, new_shared = token_part(
        skip_gain,
        recv_rows,
        inner_rows,
        shared_rows,
        edges,
        jnp.repeat(counts, window).reshape(lanes, 1),
        conv_inner,
        conv_inner_bias.reshape(1, -1),
        conv_shared,
        conv_shared_bias.reshape(1, -1),
        in_lanes(step_bias),
        in_lanes(decay_log),
        window,
        heads,
        head_dim,
        state_dim,
        capacity,
    )
    send_late, _ = lax.optimization_barrier((send_late, [early_pages[step] for step in rest] + [moved]))
    late = exchange(lax.dynamic_update_index_in_dim(send_late, arrived, target, 0))
    edge_inner_out = new_inner.transpose(1, 0, 2)
    edge_shared_out = new_shared.transpose(1, 0, 2)

    states_out, messages = state_part(
        new_slots,
        slot_of,
        early_pages,
        list(range(groups)) if early_pages else [],
        late,
        states,
        moved,
        entry,
        readout,
        within,
        decay,
        gate,
        gate_gain.reshape(1, -1),
        out_weight,
        window,
        groups,
        shares,
    )
    total = jnp.zeros(messages[0].shape, F32)
    for step in range(shares):
        piece = permute(messages[step], "head", step) if step else messages[step]
        total = total + piece.astype(F32)
    squares = total[:, width : width + 1] + total[:, width + 1 : width + 2]
    mixer = total[:, :width] * lax.rsqrt(squares / (inner * shares) + EPS)
    hidden_out = (rows_in + mixer).astype(BF16)
    return (hidden_out, states_out, edge_inner_out, edge_shared_out)


def solution(mesh):
    placed = (
        P(("req", "head"), None),
        P(),
        P(None, None, "head"),
        P(),
        P(None, "head"),
        P("head"),
        P(),
        P(),
        P("head"),
        P("head"),
        P("head"),
        P("head"),
        P("head", None),
        P("req", "head", None, None),
        P("req", None, "head"),
        P("req", None, None),
        P("req"),
        P(),
        P(),
        P(),
    )
    return jax.shard_map(
        local,
        mesh=mesh,
        in_specs=placed,
        out_specs=(
            P(("req", "head"), None),
            P("req", "head", None, None),
            P("req", None, "head"),
            P("req", None, None),
        ),
        check_vma=False,
    )
```

time: 166 us -> 122 us (0.73)
  waiting for transfers between devices: 59.8 us -> 30.9 us
  local copies, waits for them, and re-layouts: 39.4 us -> 14.7 us
  starting transfers between devices: 15 us -> 30.4 us
  blocking collectives: 9.52 us -> 0 us
  other arithmetic: 5.02 us -> 8.78 us
  between operations: 0.92 us -> 3.48 us
    all_to_all x1 -> x4, waiting for transfers between devices: 51.4 us -> 10.1 us  [the longest x1 7.57 us: local(): exchange(lax.dynamic_update_index_in_dim(send_late, arrived, target, 0))]
    unnamed x95 -> x26, local copies, waits for them, and re-layouts: 29 us -> 6.3 us
    all_to_all x1 -> x4, starting transfers between devices: 6.41 us -> 20.2 us  [the longest x1 5.7 us: local(): exchange(lax.dynamic_update_index_in_dim(send_late, arrived, target, 0))]
    ppermute x6 -> x10, waiting for transfers between devices: 8.38 us -> 20.9 us  [permute(): return lax.ppermute(value, axis, pairs)]
    all_to_all x1 -> x0, blocking collectives: 9.52 us -> none  [local(): edges = exchange(send_edges)]
    dynamic_update_slice x3 -> x1, local copies, waits for them, and re-layouts: 4.63 us -> 1.6 us  [local(): lax.dynamic_update_index_in_dim(send_late, arrived, target, 0)]
    pallas_call x2 -> x4, Pallas kernels: 27.4 us -> 25 us  [the longest x1 9.72 us: state_part(): pl.pallas_call(functools.partial(early_kernel, window, batch, groups, str...]
    another operation x1 -> x2, other arithmetic: 0.08 us -> 1.99 us  [the longest x1 1.3 us: local(): target = jnp.argmax(reorder == leaving) // slots]
  transfers between devices with their start and end apart: 7 -> 14, of which waited for: 3 -> 6; matrix products, arithmetic and copies ran while one was open for 15% -> 18% of each run, Pallas kernels for 1% -> 15%
where the time goes in v2:
time: 122 us
  waiting for transfers between devices  30.9 us (25%)
  starting transfers between devices  30.4 us (25%)
  Pallas kernels  29.1 us (24%)
  local copies, waits for them, and re-layouts  14.7 us (12%)
  other arithmetic  8.78 us (7%)
  matrix products  4.29 us (4%)
  between operations  3.48 us (3%)
    ppermute x10, waiting for transfers between devices, permute(): return lax.ppermute(value, axis, pairs)  20.9 us
    ppermute x10, starting transfers between devices, permute(): return lax.ppermute(value, axis, pairs)  10.2 us
    pallas_call x1, Pallas kernels, state_part(): pl.pallas_call(functools.partial(early_kernel, window, batch, groups, str...  9.72 us
    all_to_all x1, waiting for transfers between devices, local(): exchange(lax.dynamic_update_index_in_dim(send_late, arrived, target, 0))  7.57 us
    unnamed x26, local copies, waits for them, and re-layouts  6.3 us
    pallas_call x1, Pallas kernels, pack(): pl.pallas_call(functools.partial(pack_kernel, groups, slots, early, capac...  6.28 us
    all_to_all x1, starting transfers between devices, local(): exchange(lax.dynamic_update_index_in_dim(send_late, arrived, target, 0))  5.7 us
    all_to_all x1, starting transfers between devices, local(): arrived = exchange(pieces).reshape(states.shape[1:])  5.33 us
  transfers between devices with their start and end apart: 14, of which 6 were waited for; matrix products, arithmetic and copies ran while one was open for 18% of the time, Pallas kernels for 15%

profile of v2, /device:TPU:2, one launch (start us, length us, event | category | flops | bytes accessed | tf_op | source)
XLA Modules:
  0.0 121.6 jit_solution(14948917318440092817)
XLA Ops:
  0.7 6.3 %pack.1 = (s32[33]{0:T(128)}, s32[33]{0:T(128)}, s32[33]{0:T(128)}, bf16[8,128,128]{2,1,0:T(8,128)(2,1)}, bf16[12,64,128]{2,1,0:T(8,128)(2,1)}, /*index=5*/bf16[...) custom-call(s32[8]{0:T(128)} %ids_hbm.1, ...), custom_call_target="tpu_custom_call" | custom-call | flops 1 | bytes 1 | tf_op jit(solution)/shard_map/pack/pallas_call | solution.py:184
  7.0 1.9 %pad_maximum_fusion = bf16[8,224,128]{2,1,0:T(8,128)(2,1)} fusion(bf16[8,96,128]{2,1,0:T(8,128)(2,1)} %bitcast.33, bf16[8,128,128]{2,1,0:T(8,128)(2,1)} %get-tuple-element.42), kind=kLoop, calls=%fused_computation.3 | loop fusion | flops 917504 | bytes 917504 | tf_op jit(solution)/shard_map/concatenate | solution.py:637
  8.8 4.3 %all-to-all-start = ((bf16[8,224,128]{2,1,0:T(8,128)(2,1)}), bf16[8,224,128]{2,1,0:T(8,128)(2,1)S(1)}, u32[]{:S(2)}, u32[]{:S(2)}) async-start(bf16[8,224,128]{2,1,0:T(8,128)(2,1)} %pad_maximum_fusion), calls=%async_computation | async-start | bytes 917504 | tf_op jit(solution)/shard_map/all_to_all | solution.py:637
  13.1 2.0 %collective-permute-start.1 = (bf16[3,12,64,128]{3,2,1,0:T(8,128)(2,1)}, bf16[3,12,64,128]{3,2,1,0:T(8,128)(2,1)S(1)}, u32[]{:S(2)}, u32[]{:S(2)}) collective-permute-start(bf16[3,12,64,128]{3,2,1,0:T(8,128)(2,1)} %get-tuple-element.48), channel_id=1, source_target_pairs={{0,16},{4,20},{8,24},{12,28},{16,0},{20,4},{24,8},{28,12},{1,17},{... | collective-permute-start | bytes 1769480 | tf_op jit(solution)/shard_map/ppermute | solution.py:35
  16.8 1.5 %collective-permute-start.4 = (bf16[3,12,64,128]{3,2,1,0:T(8,128)(2,1)}, bf16[3,12,64,128]{3,2,1,0:T(8,128)(2,1)}, u32[]{:S(2)}, u32[]{:S(2)}) collective-permute-start(bf16[3,12,64,128]{3,2,1,0:T(8,128)(2,1)} %get-tuple-element.57), channel_id=1, source_target_pairs={{0,24},{4,28},{8,16},{12,20},{16,8},{20,12},{24,0},{28,4},{1,25},{... | collective-permute-start | bytes 1769480 | tf_op jit(solution)/shard_map/ppermute | solution.py:35
  21.7 4.9 %all-to-all-start.1 = ((bf16[4,32,1536]{2,1,0:T(8,128)(2,1)}), bf16[4,32,1536]{2,1,0:T(8,128)(2,1)S(1)}, u32[]{:S(2)}, u32[]{:S(2)}) async-start(bf16[4,32,1536]{2,1,0:T(8,128)(2,1)} %tile.2), calls=%async_computation.1 | async-start | bytes 786432 | tf_op jit(solution)/shard_map/all_to_all | solution.py:643
  26.6 1.3 %compare_reduce_fusion = (pred[]{:T(512)}, s32[]{:T(128)}) fusion(s32[256]{0:T(256)S(1)} %copy-done.4, s32[]{:T(128)} %bitcast.10), kind=kLoop, calls=%fused_computation.21 | loop fusion | flops 2041 | bytes 1033 | tf_op jit(solution)/shard_map/local/reduce | solution.py:650
  30.6 5.5 %copy.50 = bf16[192,8,2,768]{3,1,2,0:T(8,128)(2,1)} copy(bf16[192,8,2,768]{3,2,1,0:T(2,128)(2,1)} %bitcast.27) | data formatting | bytes 9437184
  42.1 5.3 %all-to-all-start.2 = ((bf16[8,96,128]{2,1,0:T(8,128)(2,1)}), bf16[8,96,128]{2,1,0:T(8,128)(2,1)}, u32[]{:S(2)}, u32[]{:S(2)}) async-start(bf16[8,96,128]{2,1,0:T(8,128)(2,1)} %copy.49), calls=%async_computation.2 | async-start | bytes 393216 | tf_op jit(solution)/shard_map/all_to_all | solution.py:648
  47.4 3.9 %convolution_convert_fusion.rows_ref = bf16[128,1536]{1,0:T(8,128)(2,1)} fusion(bf16[128,1536]{1,0:T(8,128)(2,1)S(1)} %bitcast.28, bf16[1536,1536]{1,0:T(8,128)(2,1)} %bitcast.26), kind=kOutput, calls=%fused_computation.1 | convolution fusion | flops 604176384 | bytes 5505024 | tf_op jit(solution)/shard_map/dot_general | solution.py:652
  52.5 4.1 %token_rows.1 = (bf16[768,128]{1,0:T(8,128)(2,1)}, bf16[128,128]{1,0:T(8,128)(2,1)}, bf16[128,128]{1,0:T(8,128)(2,1)}, f32[768,128]{1,0:T(8,128)}, f32[16,128]{1...) custom-call(f32[12]{0:T(128)} %skip_ref.1, ...), custom_call_target="tpu_custom_call" | custom-call | flops 1 | bytes 1 | tf_op jit(solution)/shard_map/token_rows/pallas_call | solution.py:360
  56.6 2.7 %collective-permute-done.4.refs_5_ = bf16[3,12,64,128]{3,2,1,0:T(8,128)(2,1)} collective-permute-done((bf16[3,12,64,128]{3,2,1,0:T(8,128)(2,1)}, bf16[3,12,64,128]{3,2,1,0:T(8,128)(2,1)}, u32[]{:S(2)}, u32[]{:S(2)}) %collective-permute-start.4) | collective-permute-done | bytes 589856 | tf_op jit(solution)/shard_map/ppermute | solution.py:35
  59.3 11.7 %collective-permute-done.5.refs_6_ = bf16[3,12,64,128]{3,2,1,0:T(8,128)(2,1)} collective-permute-done((bf16[3,12,64,128]{3,2,1,0:T(8,128)(2,1)}, bf16[3,12,64,128]{3,2,1,0:T(8,128)(2,1)}, u32[]{:S(2)}, u32[]{:S(2)}) %collective-permute-start.5) | collective-permute-done | bytes 589856 | tf_op jit(solution)/shard_map/ppermute | solution.py:35
  70.9 2.5 %all-to-all-done.2 = bf16[8,96,128]{2,1,0:T(8,128)(2,1)} async-done(((bf16[8,96,128]{2,1,0:T(8,128)(2,1)}), bf16[8,96,128]{2,1,0:T(8,128)(2,1)}, u32[]{:S(2)}, u32[]{:S(2)}) %all-to-all-start.2) | async-done | bytes 196640 | tf_op jit(solution)/shard_map/all_to_all | solution.py:648
  73.4 1.6 %constant_dynamic-update-slice_fusion = bf16[8,12,64,128]{3,2,1,0:T(8,128)(2,1)} fusion(bf16[8,12,64,128]{3,2,1,0:T(8,128)(2,1)} %get-tuple-element.60, bf16[1,12,64,128]{3,2,1,0:T(8,128)(2,1)} %bitcast.9, s32[]{:T(128)S(6)} %select_n.27), kind=kLoop, calls=%fused_computation.28 | loop fusion | bytes 393220 | tf_op jit(solution)/shard_map/jit(dynamic_update_index_in_dim)/dynamic_update_slice | solution.py:680
  75.0 5.7 %all-to-all-start.3 = ((bf16[8,12,64,128]{3,2,1,0:T(8,128)(2,1)}), bf16[8,12,64,128]{3,2,1,0:T(8,128)(2,1)}, u32[]{:S(2)}, u32[]{:S(2)}) async-start(bf16[8,12,64,128]{3,2,1,0:T(8,128)(2,1)} %constant_dynamic-update-slice_fusion), calls=%async_computation.3 | async-start | bytes 3145728 | tf_op jit(solution)/shard_map/all_to_all | solution.py:680
  81.5 1.6 %collective-permute-done.6.refs_0_ = bf16[3,12,64,128]{3,2,1,0:T(8,128)(2,1)} collective-permute-done((bf16[3,12,64,128]{3,2,1,0:T(8,128)(2,1)}, bf16[3,12,64,128]{3,2,1,0:T(8,128)(2,1)}, u32[]{:S(2)}, u32[]{:S(2)}) %collective-permute-start.6) | collective-permute-done | bytes 589856 | tf_op jit(solution)/shard_map/ppermute | solution.py:35
  83.1 9.7 %early_pages.1 = (bf16[32,12,64,128]{3,2,1,0:T(8,128)(2,1)}, f32[768,128]{1,0:T(8,128)}) custom-call(s32[33]{0:T(128)} %get-tuple-element.40.new_slots, s32[33]{0:T(128)} %get-tuple-element.63.slot_of, f32[16,128]{1,0:T(8,128)} %get-tuple-element.50.decay_hbm, bf16[768,128]{1,0:T(8,128)(2,1)} %get-tuple-element.59.moved_hbm, ...), custom_call_target="tpu_custom_call" | custom-call | flops 1 | bytes 1 | tf_op jit(solution)/shard_map/early_pages/pallas_call | solution.py:551
  92.8 7.6 %all-to-all-done.3.late = bf16[8,12,64,128]{3,2,1,0:T(8,128)(2,1)} async-done(((bf16[8,12,64,128]{3,2,1,0:T(8,128)(2,1)}), bf16[8,12,64,128]{3,2,1,0:T(8,128)(2,1)}, u32[]{:S(2)}, u32[]{:S(2)}) %all-to-all-start.3) | async-done | bytes 1572896 | tf_op jit(solution)/shard_map/all_to_all | solution.py:680
  100.4 5.2 %hidden_rows.1 = (bf16[32,1664]{1,0:T(8,128)(2,1)}, bf16[32,1664]{1,0:T(8,128)(2,1)}, bf16[32,1664]{1,0:T(8,128)(2,1)}, bf16[32,1664]{1,0:T(8,128)(2,1)}) custom-call(s32[33]{0:T(128)} %get-tuple-element.40.new_slots, f32[16,128]{1,0:T(8,128)} %get-tuple-element.50.decay_hbm, bf16[128,128]{1,0:T(8,128)(2,1)} %get-tuple-element.51.readout_hbm, ...), custom_call_target="tpu_custom_call" | custom-call | flops 1 | bytes 1 | tf_op jit(solution)/shard_map/hidden_rows/pallas_call | solution.py:565
  105.5 3.7 %collective-permute-start.9 = (bf16[32,1664]{1,0:T(8,128)(2,1)}, bf16[32,1664]{1,0:T(8,128)(2,1)}, u32[]{:S(2)}, u32[]{:S(2)}) collective-permute-start(bf16[32,1664]{1,0:T(8,128)(2,1)} %get-tuple-element.72), channel_id=1, source_target_pairs={{0,3},{1,2},{2,1},{3,0},{4,7},{5,6},{6,5},{7,4},{8,11},{9,10},{10,... | collective-permute-start | bytes 319496 | tf_op jit(solution)/shard_map/ppermute | solution.py:35
  110.0 3.8 %late_pages.1 = bf16[32,12,64,128]{3,2,1,0:T(8,128)(2,1)} custom-call(s32[33]{0:T(128)} %get-tuple-element.40.new_slots, f32[16,128]{1,0:T(8,128)} %get-tuple-element.50.decay_hbm, bf16[768,128]{1,0:T(8,128)(2,1)} %get-tuple-element.59.moved_hbm, bf16[128,128]{1,0:T(8,128)(2,1)} %get-tuple-element.64.entry_hbm, ...), custom_call_target="tpu_custom_call", output_to_operand_aliasing={{}: (5, {})} | custom-call | flops 1 | bytes 12582912 | tf_op jit(solution)/shard_map/late_pages/pallas_call | solution.py:579
  113.9 4.9 %collective-permute-done.8 = bf16[32,1664]{1,0:T(8,128)(2,1)} collective-permute-done((bf16[32,1664]{1,0:T(8,128)(2,1)}, bf16[32,1664]{1,0:T(8,128)(2,1)}, u32[]{:S(2)}, u32[]{:S(2)}) %collective-permute-start.8) | collective-permute-done | bytes 106528 | tf_op jit(solution)/shard_map/ppermute | solution.py:35
  120.0 1.6 %fusion.3 = bf16[32,1536]{1,0:T(8,128)(2,1)} fusion(bf16[32,1536]{1,0:T(8,128)(2,1)} %param.20, f32[32,1664]{1,0:T(8,128)S(1)} %convert_add_fusion.1, f32[32]{0:T(128)S(1)} %fusion.7), kind=kLoop, calls=%fused_computation.12 | loop fusion | flops 196608 | bytes 393344 | tf_op jit(solution)/shard_map/convert_element_type | solution.py:709
  (61 shorter events, 15.2 us)
Async XLA Ops:
  0.6 50.7 %copy-start = (bf16[1536,304]{0,1:T(8,128)(2,1)S(1)}, bf16[1536,304]{0,1:T(8,128)(2,1)}, u32[]{:S(2)}) copy-start(bf16[1536,304]{0,1:T(8,128)(2,1)} %param.23) | copy-start | bytes 2801668
  0.6 18.7 %copy-start.7 = (s32[8]{0:T(128)S(1)}, s32[8]{0:T(128)}, u32[]{:S(2)}) copy-start(s32[8]{0:T(128)} %ids_hbm.1) | copy-start | bytes 100
  0.7 19.3 %copy-start.3 = (f32[1536]{0:T(1024)S(1)}, f32[1536]{0:T(1024)}, u32[]{:S(2)}) copy-start(f32[1536]{0:T(1024)} %param.21) | copy-start | bytes 18436
  0.7 25.9 %copy-start.4 = (s32[256]{0:T(256)S(1)}, s32[256]{0:T(256)}, u32[]{:S(2)}) copy-start(s32[256]{0:T(256)} %reorder_hbm.1) | copy-start | bytes 3076
  8.8 12.1 %all-to-all-start = ((bf16[8,224,128]{2,1,0:T(8,128)(2,1)}), bf16[8,224,128]{2,1,0:T(8,128)(2,1)S(1)}, u32[]{:S(2)}, u32[]{:S(2)}) async-start(bf16[8,224,128]{2,1,0:T(8,128)(2,1)} %pad_maximum_fusion), calls=%async_computation | async-start | bytes 917504 | tf_op jit(solution)/shard_map/all_to_all | solution.py:637
  13.1 27.8 %collective-permute-start = (bf16[3,12,64,128]{3,2,1,0:T(8,128)(2,1)}, bf16[3,12,64,128]{3,2,1,0:T(8,128)(2,1)S(1)}, u32[]{:S(2)}, u32[]{:S(2)}) collective-permute-start(bf16[3,12,64,128]{3,2,1,0:T(8,128)(2,1)} %get-tuple-element.47), channel_id=1, source_target_pairs={{0,8},{4,12},{8,0},{12,4},{16,24},{20,28},{24,16},{28,20},{1,9},{5... | collective-permute-start | bytes 1769480 | tf_op jit(solution)/shard_map/ppermute | solution.py:35
  13.1 28.2 %collective-permute-start.1 = (bf16[3,12,64,128]{3,2,1,0:T(8,128)(2,1)}, bf16[3,12,64,128]{3,2,1,0:T(8,128)(2,1)S(1)}, u32[]{:S(2)}, u32[]{:S(2)}) collective-permute-start(bf16[3,12,64,128]{3,2,1,0:T(8,128)(2,1)} %get-tuple-element.48), channel_id=1, source_target_pairs={{0,16},{4,20},{8,24},{12,28},{16,0},{20,4},{24,8},{28,12},{1,17},{... | collective-permute-start | bytes 1769480 | tf_op jit(solution)/shard_map/ppermute | solution.py:35
  15.1 41.5 %collective-permute-start.2 = (bf16[3,12,64,128]{3,2,1,0:T(8,128)(2,1)}, bf16[3,12,64,128]{3,2,1,0:T(8,128)(2,1)}, u32[]{:S(2)}, u32[]{:S(2)}) collective-permute-start(bf16[3,12,64,128]{3,2,1,0:T(8,128)(2,1)} %get-tuple-element.55), channel_id=1, source_target_pairs={{0,12},{4,8},{8,4},{12,0},{16,28},{20,24},{24,20},{28,16},{1,13},{... | collective-permute-start | bytes 1769480 | tf_op jit(solution)/shard_map/ppermute | solution.py:35
  15.8 40.8 %collective-permute-start.3 = (bf16[3,12,64,128]{3,2,1,0:T(8,128)(2,1)}, bf16[3,12,64,128]{3,2,1,0:T(8,128)(2,1)}, u32[]{:S(2)}, u32[]{:S(2)}) collective-permute-start(bf16[3,12,64,128]{3,2,1,0:T(8,128)(2,1)} %get-tuple-element.56), channel_id=1, source_target_pairs={{0,20},{4,16},{8,28},{12,24},{16,4},{20,0},{24,12},{28,8},{1,21},{... | collective-permute-start | bytes 1769480 | tf_op jit(solution)/shard_map/ppermute | solution.py:35
  16.8 42.4 %collective-permute-start.4 = (bf16[3,12,64,128]{3,2,1,0:T(8,128)(2,1)}, bf16[3,12,64,128]{3,2,1,0:T(8,128)(2,1)}, u32[]{:S(2)}, u32[]{:S(2)}) collective-permute-start(bf16[3,12,64,128]{3,2,1,0:T(8,128)(2,1)} %get-tuple-element.57), channel_id=1, source_target_pairs={{0,24},{4,28},{8,16},{12,20},{16,8},{20,12},{24,0},{28,4},{1,25},{... | collective-permute-start | bytes 1769480 | tf_op jit(solution)/shard_map/ppermute | solution.py:35
  21.7 19.6 %all-to-all-start.1 = ((bf16[4,32,1536]{2,1,0:T(8,128)(2,1)}), bf16[4,32,1536]{2,1,0:T(8,128)(2,1)S(1)}, u32[]{:S(2)}, u32[]{:S(2)}) async-start(bf16[4,32,1536]{2,1,0:T(8,128)(2,1)} %tile.2), calls=%async_computation.1 | async-start | bytes 786432 | tf_op jit(solution)/shard_map/all_to_all | solution.py:643
  30.5 6.9 %copy-start.10 = (f32[12]{0:T(128)S(1)}, f32[12]{0:T(128)}, u32[]{:S(2)}) copy-start(f32[12]{0:T(128)} %param.29) | copy-start | bytes 148
  30.5 6.9 %copy-start.11 = (f32[12]{0:T(128)S(1)}, f32[12]{0:T(128)}, u32[]{:S(2)}) copy-start(f32[12]{0:T(128)} %param.28) | copy-start | bytes 148
  30.5 7.4 %copy-start.8 = (s32[8]{0:T(128)S(1)}, s32[8]{0:T(128)}, u32[]{:S(2)}) copy-start(s32[8]{0:T(128)} %dest_hbm.1) | copy-start | bytes 100
  40.9 10.8 %copy-start.1 = (bf16[3,12,64,128]{3,2,1,0:T(8,128)(2,1)}, bf16[3,12,64,128]{3,2,1,0:T(8,128)(2,1)S(1)}, u32[]{:S(2)}) copy-start(bf16[3,12,64,128]{3,2,1,0:T(8,128)(2,1)S(1)} %collective-permute-done.refs_1_) | copy-start | bytes 1769476
  40.9 30.0 %collective-permute-start.5 = (bf16[3,12,64,128]{3,2,1,0:T(8,128)(2,1)}, bf16[3,12,64,128]{3,2,1,0:T(8,128)(2,1)}, u32[]{:S(2)}, u32[]{:S(2)}) collective-permute-start(bf16[3,12,64,128]{3,2,1,0:T(8,128)(2,1)} %get-tuple-element.58), channel_id=1, source_target_pairs={{0,28},{4,24},{8,20},{12,16},{16,12},{20,8},{24,4},{28,0},{1,29},{... | collective-permute-start | bytes 1769480 | tf_op jit(solution)/shard_map/ppermute | solution.py:35
  41.3 11.2 %copy-start.2 = (bf16[3,12,64,128]{3,2,1,0:T(8,128)(2,1)}, bf16[3,12,64,128]{3,2,1,0:T(8,128)(2,1)S(1)}, u32[]{:S(2)}) copy-start(bf16[3,12,64,128]{3,2,1,0:T(8,128)(2,1)S(1)} %collective-permute-done.1.refs_3_) | copy-start | bytes 1769476
  42.1 31.3 %all-to-all-start.2 = ((bf16[8,96,128]{2,1,0:T(8,128)(2,1)}), bf16[8,96,128]{2,1,0:T(8,128)(2,1)}, u32[]{:S(2)}, u32[]{:S(2)}) async-start(bf16[8,96,128]{2,1,0:T(8,128)(2,1)} %copy.49), calls=%async_computation.2 | async-start | bytes 393216 | tf_op jit(solution)/shard_map/all_to_all | solution.py:648
  47.4 33.5 %copy-start.6 = (f32[768]{0:T(1024)S(1)}, f32[768]{0:T(1024)}, u32[]{:S(2)}) copy-start(f32[768]{0:T(1024)} %param.31) | copy-start | bytes 9220
  75.0 25.3 %all-to-all-start.3 = ((bf16[8,12,64,128]{3,2,1,0:T(8,128)(2,1)}), bf16[8,12,64,128]{3,2,1,0:T(8,128)(2,1)}, u32[]{:S(2)}, u32[]{:S(2)}) async-start(bf16[8,12,64,128]{3,2,1,0:T(8,128)(2,1)} %constant_dynamic-update-slice_fusion), calls=%async_computation.3 | async-start | bytes 3145728 | tf_op jit(solution)/shard_map/all_to_all | solution.py:680
  80.7 2.3 %collective-permute-start.6 = (bf16[3,12,64,128]{3,2,1,0:T(8,128)(2,1)}, bf16[3,12,64,128]{3,2,1,0:T(8,128)(2,1)}, u32[]{:S(2)}, u32[]{:S(2)}) collective-permute-start(bf16[3,12,64,128]{3,2,1,0:T(8,128)(2,1)} %get-tuple-element.65), channel_id=1, source_target_pairs={{0,4},{4,0},{8,12},{12,8},{16,20},{20,16},{24,28},{28,24},{1,5},{5... | collective-permute-start | bytes 1769480 | tf_op jit(solution)/shard_map/ppermute | solution.py:35
  105.5 8.3 %collective-permute-start.9 = (bf16[32,1664]{1,0:T(8,128)(2,1)}, bf16[32,1664]{1,0:T(8,128)(2,1)}, u32[]{:S(2)}, u32[]{:S(2)}) collective-permute-start(bf16[32,1664]{1,0:T(8,128)(2,1)} %get-tuple-element.72), channel_id=1, source_target_pairs={{0,3},{1,2},{2,1},{3,0},{4,7},{5,6},{6,5},{7,4},{8,11},{9,10},{10,... | collective-permute-start | bytes 319496 | tf_op jit(solution)/shard_map/ppermute | solution.py:35
  109.2 9.5 %collective-permute-start.8 = (bf16[32,1664]{1,0:T(8,128)(2,1)}, bf16[32,1664]{1,0:T(8,128)(2,1)}, u32[]{:S(2)}, u32[]{:S(2)}) collective-permute-start(bf16[32,1664]{1,0:T(8,128)(2,1)} %get-tuple-element.71), channel_id=1, source_target_pairs={{0,2},{1,3},{2,0},{3,1},{4,6},{5,7},{6,4},{7,5},{8,10},{9,11},{10,... | collective-permute-start | bytes 319496 | tf_op jit(solution)/shard_map/ppermute | solution.py:35
  109.2 9.5 %collective-permute-start.7 = (bf16[32,1664]{1,0:T(8,128)(2,1)}, bf16[32,1664]{1,0:T(8,128)(2,1)}, u32[]{:S(2)}, u32[]{:S(2)}) collective-permute-start(bf16[32,1664]{1,0:T(8,128)(2,1)} %get-tuple-element.70), channel_id=1, source_target_pairs={{0,1},{1,0},{2,3},{3,2},{4,5},{5,4},{6,7},{7,6},{8,9},{9,8},{10,11... | collective-permute-start | bytes 319496 | tf_op jit(solution)/shard_map/ppermute | solution.py:35
  (2 other events, 11.8 us)

commit v3 on v2

--- a/solution.py
+++ b/solution.py
@@ -118,6 +118,12 @@
         writes.append(pltpu.make_async_copy(staged.at[slot], out_late.at[peer], write_done.at[0]))
         writes[-1].start()
 
+    pieces = staged[moving].reshape(-1, staged.shape[3])
+    edge_rows = edge_block * (inner.shape[2] + shared.shape[2]) // staged.shape[3]
+    share = pieces.shape[0] // groups
+    if out_edges.shape[1] > edge_rows:
+        for peer in range(groups):
+            out_edges[peer, edge_rows:, :] = pieces[peer * share : (peer + 1) * share]
     keep = inner.shape[0]
     rows = groups * edge_block
     lane = lax.broadcasted_iota(jnp.int32, (1, slots), 1)
@@ -176,6 +182,7 @@
     stride = slots // groups
     width = edge_inner.shape[2] + edge_shared.shape[2]
     lanes = states.shape[3]
+    share = states.shape[1] * states.shape[2] // groups
     chunk = 8
     shape = jax.ShapeDtypeStruct
     peers = groups - 1 if early else 0
@@ -187,7 +194,7 @@
             shape((slots + 1,), jnp.int32),
             shape((slots + 1,), jnp.int32),
             shape((slots + 1,), jnp.int32),
-            shape((groups, edge_block * width // lanes, lanes), BF16),
+            shape((groups, edge_block * width // lanes + (share if share % 16 == 0 else 0), lanes), BF16),
             shape(states.shape[1:], BF16),
             shape((groups,) + states.shape[1:], BF16),
         )
@@ -532,6 +539,7 @@
     shape = jax.ShapeDtypeStruct
     new_states = shape(states.shape, BF16)
     batch = 4
+    floating = list(range(3, groups - 1, 2))
     rest = [step for step in early_pages if step not in steps]
     others = [early_pages[step] for step in rest]
     params = pltpu.CompilerParams(vmem_limit_bytes=VMEM_BYTES)
@@ -555,7 +563,7 @@
             out_specs=(HBM, VMEM),
             scratch_shapes=held(moved, entry, readout) + [decay_scalars] + paging(len(steps) * (stride - 1), 2) + [done((1,)), done((4,))],
             compiler_params=params,
-            cost_estimate=CHEAP,
+            cost_estimate=pl.CostEstimate(flops=12_000_000_000, bytes_accessed=1, transcendentals=0),
             name="early_pages",
         )(*operands)
         begun, read = [out[0]], [out[1]]
@@ -588,6 +596,35 @@
         name="late_pages",
     )(*operands)
     return out, messages
+
+
+def finish_kernel(full, tokens_hbm, *refs):
+    count = (len(refs) - 3) // 2
+    hbm, out_ref, tokens, held, done = refs[:count], refs[count], refs[count + 1], refs[count + 2 : -1], refs[-1]
+    copies = fetch([(tokens_hbm, tokens)] + list(zip(hbm, held)), done)
+    for copy in copies:
+        copy.wait()
+    total = held[0][...].astype(F32)
+    for message in held[1:]:
+        total = total + message[...].astype(F32)
+    width = tokens.shape[1]
+    squares = total[:, width : width + 1] + total[:, width + 1 : width + 2]
+    mixer = total[:, :width] * lax.rsqrt(squares / full + EPS)
+    out_ref[...] = (tokens[...].astype(F32) + mixer).astype(BF16)
+
+
+def finish(tokens, messages, full):
+    return pl.pallas_call(
+        functools.partial(finish_kernel, full),
+        out_shape=jax.ShapeDtypeStruct(tokens.shape, BF16),
+        in_specs=[HBM] * (1 + len(messages)),
+        out_specs=VMEM,
+        scratch_shapes=[pltpu.VMEM(array.shape, BF16) for array in [tokens] + messages]
+        + [pltpu.SemaphoreType.DMA((1 + len(messages),))],
+        compiler_params=pltpu.CompilerParams(vmem_limit_bytes=VMEM_BYTES),
+        cost_estimate=CHEAP,
+        name="finish",
+    )(tokens, *messages)
 
 
 def local(
@@ -630,22 +667,29 @@
 
     packed = pack(mig_ids, mig_dest, reorder, edge_inner, edge_shared, states, groups, early, capacity, edge_block)
     slot_of, recv_rows, new_slots, send_edges, page, send_late = packed[:6]
-    early_pages = {step: permute(sent, "req", step) for step, sent in enumerate(packed[6:], 1)}
+    sent = dict(enumerate(packed[6:], 1))
+    behind = list(range(groups - 2, groups)) if len(sent) > 2 else []
+    early_pages = {step: permute(sent[step], "req", step) for step in sent if step not in behind}
     first = list(range(2, groups, 2))[:2] if early_pages else []
+    floating = list(range(3, groups - 1, 2))
     rest = [step for step in range(2, groups) if step not in first] if early_pages else []
-    edge_rows = send_edges.shape[1]
-    pieces = exchange(jnp.concatenate([send_edges, page.reshape(groups, inner // groups, state_dim)], axis=1))
+    edge_rows = edge_block * (inner + 2 * state_dim) // state_dim
+    if send_edges.shape[1] == edge_rows:
+        send_edges = jnp.concatenate([send_edges, page.reshape(groups, inner // groups, state_dim)], axis=1)
+    pieces = exchange(send_edges)
     edges = pieces[:, :edge_rows].reshape(groups, -1, edge_block, state_dim).transpose(0, 2, 1, 3)
     edges = edges.reshape(groups * edge_block, -1)
     rows_in = tokens.astype(F32)
     normed = (rows_in * lax.rsqrt(jnp.mean(rows_in * rows_in, axis=-1, keepdims=True) + EPS) * pre_gain).astype(BF16)
-    normed, pieces = lax.optimization_barrier((normed, pieces))
-    all_rows = lax.all_to_all(jnp.tile(normed, (shares, 1)), "head", split_axis=0, concat_axis=0, tiled=True)
     comes_from = jnp.argmax(mig_dest[None, :] == mig_ids[:, None], axis=1)
-    first_pages = [early_pages[step] for step in first]
-    pieces, all_rows, first_pages = lax.optimization_barrier((pieces[comes_from, edge_rows:], all_rows, first_pages))
-    early_pages.update(zip(first, first_pages))
-    arrived = exchange(pieces).reshape(states.shape[1:])
+    pieces = pieces[comes_from, edge_rows:]
+    arrived = exchange(pieces)
+    for step in behind:
+        waiting, _ = lax.optimization_barrier((sent[step], arrived))
+        early_pages[step] = permute(waiting, "req", step)
+    arrived = arrived.reshape(states.shape[1:])
+    all_rows = lax.all_gather(normed, "head", axis=0, tiled=True)
+    all_rows, inner_weight, _ = lax.optimization_barrier((all_rows, inner_weight, pieces))
     leaving = lax.dynamic_index_in_dim(mig_ids, request_index, 0, keepdims=False)
     target = jnp.argmax(reorder == leaving) // slots
     inner_flat = inner_weight.reshape(width, 2 * inner)
@@ -676,7 +720,6 @@
         state_dim,
         capacity,
     )
-    send_late, _ = lax.optimization_barrier((send_late, [early_pages[step] for step in rest] + [moved]))
     late = exchange(lax.dynamic_update_index_in_dim(send_late, arrived, target, 0))
     edge_inner_out = new_inner.transpose(1, 0, 2)
     edge_shared_out = new_shared.transpose(1, 0, 2)
@@ -685,7 +728,7 @@
         new_slots,
         slot_of,
         early_pages,
-        list(range(groups)) if early_pages else [],
+        list(range(groups)) if sent else [],
         late,
         states,
         moved,
@@ -700,13 +743,8 @@
         groups,
         shares,
     )
-    total = jnp.zeros(messages[0].shape, F32)
-    for step in range(shares):
-        piece = permute(messages[step], "head", step) if step else messages[step]
-        total = total + piece.astype(F32)
-    squares = total[:, width : width + 1] + total[:, width + 1 : width + 2]
-    mixer = total[:, :width] * lax.rsqrt(squares / (inner * shares) + EPS)
-    hidden_out = (rows_in + mixer).astype(BF16)
+    messages = [permute(message, "head", step) if step else message for step, message in enumerate(messages)]
+    hidden_out = finish(tokens, messages, inner * shares)
     return (hidden_out, states_out, edge_inner_out, edge_shared_out)
 
 

time: 122 us -> 114 us (0.934)
  blocking collectives: 0 us -> 15 us
  waiting for transfers between devices: 30.9 us -> 17.6 us
  starting transfers between devices: 30.4 us -> 24.3 us
  other arithmetic: 8.78 us -> 4.01 us
  Pallas kernels: 29.1 us -> 31.1 us
  local copies, waits for them, and re-layouts: 14.7 us -> 13 us
    all_gather x0 -> x1, blocking collectives: none -> 15 us  [local(): all_rows = lax.all_gather(normed, 'head', axis=0, tiled=True)]
    ppermute x10, waiting for transfers between devices: 20.9 us -> 9.66 us  [permute(): return lax.ppermute(value, axis, pairs)]
    all_to_all x3 -> x2, starting transfers between devices: 14.5 us -> 8.79 us  [the longest x1 4.52 us: local(): arrived = exchange(pieces)]
    all_to_all x3 -> x2, waiting for transfers between devices: 2.49 us -> 0.01 us  [the longest x1 0.01 us: local(): pieces = exchange(send_edges)]
    pallas_call x0 -> x1, Pallas kernels: none -> 1.95 us  [finish(): pl.pallas_call(functools.partial(finish_kernel, full), out_shape=jax.Shap...]
    concatenate x2 -> x1, other arithmetic: 1.86 us -> 0.01 us  [local(): pieces = pieces[comes_from, edge_rows:]]
    convert_element_type x1 -> x0, other arithmetic: 1.63 us -> none  [local(): hidden_out = (rows_in + mixer).astype(BF16)]
  transfers between devices with their start and end apart: 14 -> 13, of which waited for: 6 -> 3; matrix products, arithmetic and copies ran while one was open for 18% -> 19% of each run, Pallas kernels for 15% -> 16%
where the time goes in v3:
time: 114 us; the launch traced here: 113 us
  Pallas kernels  31.1 us (27%)
  starting transfers between devices  24.3 us (21%)
  waiting for transfers between devices  17.6 us (15%)
  blocking collectives  15 us (13%)
  local copies, waits for them, and re-layouts  13 us (11%)
  matrix products  4.28 us (4%)
  other arithmetic  4.01 us (4%)
  between operations  3.65 us (3%)
    all_gather x1, blocking collectives, local(): all_rows = lax.all_gather(normed, 'head', axis=0, tiled=True)  15 us
    ppermute x10, starting transfers between devices, permute(): return lax.ppermute(value, axis, pairs)  10.4 us
    pallas_call x1, Pallas kernels, state_part(): pl.pallas_call(functools.partial(early_kernel, window, batch, groups, str...  9.72 us
    ppermute x10, waiting for transfers between devices, permute(): return lax.ppermute(value, axis, pairs)  9.66 us
    all_to_all x1, waiting for transfers between devices, local(): exchange(lax.dynamic_update_index_in_dim(send_late, arrived, target, 0))  7.89 us
    pallas_call x1, Pallas kernels, pack(): pl.pallas_call(functools.partial(pack_kernel, groups, slots, early, capac...  6.33 us
    unnamed x26, local copies, waits for them, and re-layouts  6.26 us
    all_to_all x1, starting transfers between devices, local(): exchange(lax.dynamic_update_index_in_dim(send_late, arrived, target, 0))  5.13 us
  transfers between devices with their start and end apart: 13, of which 3 were waited for; matrix products, arithmetic and copies ran while one was open for 19% of the time, Pallas kernels for 16%

profile of v3, /device:TPU:2, one launch (start us, length us, event | category | flops | bytes accessed | tf_op | source)
XLA Modules:
  0.0 112.8 jit_solution(2486645283948800901)
XLA Ops:
  0.7 6.3 %pack.1 = (s32[33]{0:T(128)}, s32[33]{0:T(128)}, s32[33]{0:T(128)}, bf16[8,224,128]{2,1,0:T(8,128)(2,1)}, bf16[12,64,128]{2,1,0:T(8,128)(2,1)}, /*index=5*/bf16[...) custom-call(s32[8]{0:T(128)} %ids_hbm.1, ...), custom_call_target="tpu_custom_call" | custom-call | flops 1 | bytes 1 | tf_op jit(solution)/shard_map/pack/pallas_call | solution.py:191
  7.1 4.3 %all-to-all-start = ((bf16[8,224,128]{2,1,0:T(8,128)(2,1)}), bf16[8,224,128]{2,1,0:T(8,128)(2,1)S(1)}, u32[]{:S(2)}, u32[]{:S(2)}) async-start(bf16[8,224,128]{2,1,0:T(8,128)(2,1)} %get-tuple-element.38), calls=%async_computation | async-start | bytes 917504 | tf_op jit(solution)/shard_map/all_to_all | solution.py:679
  11.9 1.4 %collective-permute-start.2 = (bf16[3,12,64,128]{3,2,1,0:T(8,128)(2,1)}, bf16[3,12,64,128]{3,2,1,0:T(8,128)(2,1)}, u32[]{:S(2)}, u32[]{:S(2)}) collective-permute-start(bf16[3,12,64,128]{3,2,1,0:T(8,128)(2,1)} %get-tuple-element.53), channel_id=1, source_target_pairs={{0,12},{4,8},{8,4},{12,0},{16,28},{20,24},{24,20},{28,16},{1,13},{... | collective-permute-start | bytes 1769480 | tf_op jit(solution)/shard_map/ppermute | solution.py:35
  13.2 1.5 %collective-permute-start.3 = (bf16[3,12,64,128]{3,2,1,0:T(8,128)(2,1)}, bf16[3,12,64,128]{3,2,1,0:T(8,128)(2,1)}, u32[]{:S(2)}, u32[]{:S(2)}) collective-permute-start(bf16[3,12,64,128]{3,2,1,0:T(8,128)(2,1)} %get-tuple-element.54), channel_id=1, source_target_pairs={{0,16},{4,20},{8,24},{12,28},{16,0},{20,4},{24,8},{28,12},{1,17},{... | collective-permute-start | bytes 1769480 | tf_op jit(solution)/shard_map/ppermute | solution.py:35
  15.7 1.0 fusion
  16.7 1.0 fusion.2
  18.3 1.3 %compare_reduce_fusion = (pred[]{:T(512)}, s32[]{:T(128)}) fusion(s32[256]{0:T(256)S(1)} %copy-done.2, s32[]{:T(128)} %bitcast.8), kind=kLoop, calls=%fused_computation.11 | loop fusion | flops 2041 | bytes 1033 | tf_op jit(solution)/shard_map/local/reduce | solution.py:694
  19.8 1.1 %gather_fusion = bf16[8,96,128]{2,0,1:T(8,128)(2,1)S(1)} fusion(bf16[8,224,128]{2,0,1:T(8,128)(2,1)S(1)} %copy.45, s32[8]{0:T(128)S(1)} %fusion.5), kind=kCustom, calls=%fused_computation | custom fusion | bytes 393280 | tf_op jit(solution)/shard_map/gather | solution.py:685
  21.7 4.5 %all-to-all-start.1 = ((bf16[8,96,128]{2,1,0:T(8,128)(2,1)}), bf16[8,96,128]{2,1,0:T(8,128)(2,1)S(1)}, u32[]{:S(2)}, u32[]{:S(2)}) async-start(bf16[8,96,128]{2,1,0:T(8,128)(2,1)} %copy.49), calls=%async_computation.1 | async-start | bytes 393216 | tf_op jit(solution)/shard_map/all_to_all | solution.py:686
  31.4 15.0 %all_gather.3 = bf16[128,1536]{1,0:T(8,128)(2,1)S(1)} all-gather(bf16[32,1536]{1,0:T(8,128)(2,1)S(1)} %fusion.2), channel_id=1, replica_groups=mesh['req'=8,'head'=4] {'head'}, dimensions={0}, use_global_device_ids=true | all-gather | bytes 491520 | tf_op jit(solution)/shard_map/all_gather | solution.py:691
  46.4 1.5 %collective-permute-start.5 = (bf16[3,12,64,128]{3,2,1,0:T(8,128)(2,1)}, bf16[3,12,64,128]{3,2,1,0:T(8,128)(2,1)}, u32[]{:S(2)}, u32[]{:S(2)}) collective-permute-start(bf16[3,12,64,128]{3,2,1,0:T(8,128)(2,1)} %get-tuple-element.57), channel_id=1, source_target_pairs={{0,24},{4,28},{8,16},{12,20},{16,8},{20,12},{24,0},{28,4},{1,25},{... | collective-permute-start | bytes 1769480 | tf_op jit(solution)/shard_map/ppermute | solution.py:35
  49.1 5.5 %copy.50 = bf16[192,8,2,768]{3,1,2,0:T(8,128)(2,1)} copy(bf16[192,8,2,768]{3,2,1,0:T(2,128)(2,1)} %bitcast.25) | data formatting | bytes 9437184
  56.8 5.1 %all-to-all-start.2 = ((bf16[8,12,64,128]{3,2,1,0:T(8,128)(2,1)}), bf16[8,12,64,128]{3,2,1,0:T(8,128)(2,1)}, u32[]{:S(2)}, u32[]{:S(2)}) async-start(bf16[8,12,64,128]{3,2,1,0:T(8,128)(2,1)} %constant_dynamic-update-slice_fusion), calls=%async_computation.2 | async-start | bytes 3145728 | tf_op jit(solution)/shard_map/all_to_all | solution.py:723
  61.9 3.9 %convolution_convert_fusion.rows_ref = bf16[128,1536]{1,0:T(8,128)(2,1)} fusion(bf16[128,1536]{1,0:T(8,128)(2,1)S(1)} %all_gather.3, bf16[1536,1536]{1,0:T(8,128)(2,1)} %bitcast.24), kind=kOutput, calls=%fused_computation.1 | convolution fusion | flops 604176384 | bytes 5505024 | tf_op jit(solution)/shard_map/dot_general | solution.py:696
  65.8 4.1 %token_rows.1 = (bf16[768,128]{1,0:T(8,128)(2,1)}, bf16[128,128]{1,0:T(8,128)(2,1)}, bf16[128,128]{1,0:T(8,128)(2,1)}, f32[768,128]{1,0:T(8,128)}, f32[16,128]{1...) custom-call(f32[12]{0:T(128)} %skip_ref.1, ...), custom_call_target="tpu_custom_call" | custom-call | flops 1 | bytes 1 | tf_op jit(solution)/shard_map/token_rows/pallas_call | solution.py:367
  70.0 4.8 %collective-permute-done.6.refs_6_ = bf16[3,12,64,128]{3,2,1,0:T(8,128)(2,1)} collective-permute-done((bf16[3,12,64,128]{3,2,1,0:T(8,128)(2,1)}, bf16[3,12,64,128]{3,2,1,0:T(8,128)(2,1)}, u32[]{:S(2)}, u32[]{:S(2)}) %collective-permute-start.6) | collective-permute-done | bytes 589856 | tf_op jit(solution)/shard_map/ppermute | solution.py:35
  74.7 9.7 %early_pages.1 = (bf16[32,12,64,128]{3,2,1,0:T(8,128)(2,1)}, f32[768,128]{1,0:T(8,128)}) custom-call(s32[33]{0:T(128)} %get-tuple-element.36.new_slots, s32[33]{0:T(128)} %get-tuple-element.48.slot_of, f32[16,128]{1,0:T(8,128)} %get-tuple-element.42.decay_hbm, bf16[768,128]{1,0:T(8,128)(2,1)} %get-tuple-element.49.moved_hbm, ...), custom_call_target="tpu_custom_call" | custom-call | flops 12000000000 | bytes 1 | tf_op jit(solution)/shard_map/early_pages/pallas_call | solution.py:559
  84.4 7.9 %all-to-all-done.2.late = bf16[8,12,64,128]{3,2,1,0:T(8,128)(2,1)} async-done(((bf16[8,12,64,128]{3,2,1,0:T(8,128)(2,1)}), bf16[8,12,64,128]{3,2,1,0:T(8,128)(2,1)}, u32[]{:S(2)}, u32[]{:S(2)}) %all-to-all-start.2) | async-done | bytes 1572896 | tf_op jit(solution)/shard_map/all_to_all | solution.py:723
  92.3 5.1 %hidden_rows.1 = (bf16[32,1664]{1,0:T(8,128)(2,1)}, bf16[32,1664]{1,0:T(8,128)(2,1)}, bf16[32,1664]{1,0:T(8,128)(2,1)}, bf16[32,1664]{1,0:T(8,128)(2,1)}) custom-call(s32[33]{0:T(128)} %get-tuple-element.36.new_slots, f32[16,128]{1,0:T(8,128)} %get-tuple-element.42.decay_hbm, bf16[128,128]{1,0:T(8,128)(2,1)} %get-tuple-element.43.readout_hbm, ...), custom_call_target="tpu_custom_call" | custom-call | flops 1 | bytes 1 | tf_op jit(solution)/shard_map/hidden_rows/pallas_call | solution.py:573
  97.5 1.6 %collective-permute-start.7 = (bf16[32,1664]{1,0:T(8,128)(2,1)}, bf16[32,1664]{1,0:T(8,128)(2,1)}, u32[]{:S(2)}, u32[]{:S(2)}) collective-permute-start(bf16[32,1664]{1,0:T(8,128)(2,1)} %get-tuple-element.62), channel_id=1, source_target_pairs={{0,1},{1,0},{2,3},{3,2},{4,5},{5,4},{6,7},{7,6},{8,9},{9,8},{10,11... | collective-permute-start | bytes 319496 | tf_op jit(solution)/shard_map/ppermute | solution.py:35
  99.1 2.6 %collective-permute-start.8 = (bf16[32,1664]{1,0:T(8,128)(2,1)}, bf16[32,1664]{1,0:T(8,128)(2,1)}, u32[]{:S(2)}, u32[]{:S(2)}) collective-permute-start(bf16[32,1664]{1,0:T(8,128)(2,1)} %get-tuple-element.63), channel_id=1, source_target_pairs={{0,2},{1,3},{2,0},{3,1},{4,6},{5,7},{6,4},{7,5},{8,10},{9,11},{10,... | collective-permute-start | bytes 319496 | tf_op jit(solution)/shard_map/ppermute | solution.py:35
  101.9 3.8 %late_pages.1 = bf16[32,12,64,128]{3,2,1,0:T(8,128)(2,1)} custom-call(s32[33]{0:T(128)} %get-tuple-element.36.new_slots, f32[16,128]{1,0:T(8,128)} %get-tuple-element.42.decay_hbm, bf16[768,128]{1,0:T(8,128)(2,1)} %get-tuple-element.49.moved_hbm, bf16[128,128]{1,0:T(8,128)(2,1)} %get-tuple-element.50.entry_hbm, ...), custom_call_target="tpu_custom_call", output_to_operand_aliasing={{}: (5, {})} | custom-call | flops 1 | bytes 12582912 | tf_op jit(solution)/shard_map/late_pages/pallas_call | solution.py:587
  105.8 4.9 %collective-permute-done.8.refs_2_ = bf16[32,1664]{1,0:T(8,128)(2,1)} collective-permute-done((bf16[32,1664]{1,0:T(8,128)(2,1)}, bf16[32,1664]{1,0:T(8,128)(2,1)}, u32[]{:S(2)}, u32[]{:S(2)}) %collective-permute-start.8) | collective-permute-done | bytes 106528 | tf_op jit(solution)/shard_map/ppermute | solution.py:35
  110.7 1.9 %finish.1 = bf16[32,1536]{1,0:T(8,128)(2,1)} custom-call(bf16[32,1536]{1,0:T(8,128)(2,1)} %tokens_hbm.1, bf16[32,1664]{1,0:T(8,128)(2,1)} %get-tuple-element.61.refs_0_, bf16[32,1664]{1,0:T(8,128)(2,1)} %collective-permute-done.7.refs_1_, bf16[32,1664]{1,0:T(8,128)(2,1)} %collective-permute-done.8.refs_2_, bf16[32,1664]{1,0:T(8,128)(2,1)} %collective-permute-done.9.refs_3_), custom_call_target="tpu_custom_call" | custom-call | flops 1 | bytes 1 | tf_op jit(solution)/shard_map/finish/pallas_call | solution.py:617
  (56 shorter events, 9.3 us)
Async XLA Ops:
  0.6 48.0 %copy-start = (bf16[1536,304]{0,1:T(8,128)(2,1)S(1)}, bf16[1536,304]{0,1:T(8,128)(2,1)}, u32[]{:S(2)}) copy-start(bf16[1536,304]{0,1:T(8,128)(2,1)} %param.23) | copy-start | bytes 2801668
  0.7 14.4 %copy-start.6 = (s32[8]{0:T(128)S(1)}, s32[8]{0:T(128)}, u32[]{:S(2)}) copy-start(s32[8]{0:T(128)} %ids_hbm.1) | copy-start | bytes 100
  0.7 14.4 %copy-start.5 = (s32[8]{0:T(128)S(1)}, s32[8]{0:T(128)}, u32[]{:S(2)}) copy-start(s32[8]{0:T(128)} %dest_hbm.1) | copy-start | bytes 100
  0.7 17.7 %copy-start.2 = (s32[256]{0:T(256)S(1)}, s32[256]{0:T(256)}, u32[]{:S(2)}) copy-start(s32[256]{0:T(256)} %reorder_hbm.1) | copy-start | bytes 3076
  0.7 16.1 %copy-start.1 = (f32[1536]{0:T(1024)S(1)}, f32[1536]{0:T(1024)}, u32[]{:S(2)}) copy-start(f32[1536]{0:T(1024)} %param.21) | copy-start | bytes 18436
  0.7 25.5 %copy-start.8 = (f32[12]{0:T(128)S(1)}, f32[12]{0:T(128)}, u32[]{:S(2)}) copy-start(f32[12]{0:T(128)} %param.29) | copy-start | bytes 148
  0.7 25.5 %copy-start.9 = (f32[12]{0:T(128)S(1)}, f32[12]{0:T(128)}, u32[]{:S(2)}) copy-start(f32[12]{0:T(128)} %param.28) | copy-start | bytes 148
  0.7 28.7 %copy-start.7 = (s32[32]{0:T(128)S(1)}, s32[32]{0:T(128)}, u32[]{:S(2)}) copy-start(s32[32]{0:T(128)} %param.36) | copy-start | bytes 388
  0.7 29.5 %copy-start.3 = (f32[768]{0:T(1024)S(1)}, f32[768]{0:T(1024)}, u32[]{:S(2)}) copy-start(f32[768]{0:T(1024)} %param.25) | copy-start | bytes 9220
  0.7 30.1 %copy-start.4 = (f32[768]{0:T(1024)S(1)}, f32[768]{0:T(1024)}, u32[]{:S(2)}) copy-start(f32[768]{0:T(1024)} %param.31) | copy-start | bytes 9220
  7.1 12.6 %all-to-all-start = ((bf16[8,224,128]{2,1,0:T(8,128)(2,1)}), bf16[8,224,128]{2,1,0:T(8,128)(2,1)S(1)}, u32[]{:S(2)}, u32[]{:S(2)}) async-start(bf16[8,224,128]{2,1,0:T(8,128)(2,1)} %get-tuple-element.38), calls=%async_computation | async-start | bytes 917504 | tf_op jit(solution)/shard_map/all_to_all | solution.py:679
  11.3 35.0 %collective-permute-start = (bf16[3,12,64,128]{3,2,1,0:T(8,128)(2,1)}, bf16[3,12,64,128]{3,2,1,0:T(8,128)(2,1)S(1)}, u32[]{:S(2)}, u32[]{:S(2)}) collective-permute-start(bf16[3,12,64,128]{3,2,1,0:T(8,128)(2,1)} %get-tuple-element.51), channel_id=1, source_target_pairs={{0,4},{4,0},{8,12},{12,8},{16,20},{20,16},{24,28},{28,24},{1,5},{5... | collective-permute-start | bytes 1769480 | tf_op jit(solution)/shard_map/ppermute | solution.py:35
  11.5 36.4 %collective-permute-start.1 = (bf16[3,12,64,128]{3,2,1,0:T(8,128)(2,1)}, bf16[3,12,64,128]{3,2,1,0:T(8,128)(2,1)S(1)}, u32[]{:S(2)}, u32[]{:S(2)}) collective-permute-start(bf16[3,12,64,128]{3,2,1,0:T(8,128)(2,1)} %get-tuple-element.52), channel_id=1, source_target_pairs={{0,8},{4,12},{8,0},{12,4},{16,24},{20,28},{24,16},{28,20},{1,9},{5... | collective-permute-start | bytes 1769480 | tf_op jit(solution)/shard_map/ppermute | solution.py:35
  11.9 58.1 %collective-permute-start.2 = (bf16[3,12,64,128]{3,2,1,0:T(8,128)(2,1)}, bf16[3,12,64,128]{3,2,1,0:T(8,128)(2,1)}, u32[]{:S(2)}, u32[]{:S(2)}) collective-permute-start(bf16[3,12,64,128]{3,2,1,0:T(8,128)(2,1)} %get-tuple-element.53), channel_id=1, source_target_pairs={{0,12},{4,8},{8,4},{12,0},{16,28},{20,24},{24,20},{28,16},{1,13},{... | collective-permute-start | bytes 1769480 | tf_op jit(solution)/shard_map/ppermute | solution.py:35
  13.2 56.7 %collective-permute-start.3 = (bf16[3,12,64,128]{3,2,1,0:T(8,128)(2,1)}, bf16[3,12,64,128]{3,2,1,0:T(8,128)(2,1)}, u32[]{:S(2)}, u32[]{:S(2)}) collective-permute-start(bf16[3,12,64,128]{3,2,1,0:T(8,128)(2,1)} %get-tuple-element.54), channel_id=1, source_target_pairs={{0,16},{4,20},{8,24},{12,28},{16,0},{20,4},{24,8},{28,12},{1,17},{... | collective-permute-start | bytes 1769480 | tf_op jit(solution)/shard_map/ppermute | solution.py:35
  14.7 55.3 %collective-permute-start.4 = (bf16[3,12,64,128]{3,2,1,0:T(8,128)(2,1)}, bf16[3,12,64,128]{3,2,1,0:T(8,128)(2,1)}, u32[]{:S(2)}, u32[]{:S(2)}) collective-permute-start(bf16[3,12,64,128]{3,2,1,0:T(8,128)(2,1)} %get-tuple-element.55), channel_id=1, source_target_pairs={{0,20},{4,16},{8,28},{12,24},{16,4},{20,0},{24,12},{28,8},{1,21},{... | collective-permute-start | bytes 1769480 | tf_op jit(solution)/shard_map/ppermute | solution.py:35
  21.7 24.7 %all-to-all-start.1 = ((bf16[8,96,128]{2,1,0:T(8,128)(2,1)}), bf16[8,96,128]{2,1,0:T(8,128)(2,1)S(1)}, u32[]{:S(2)}, u32[]{:S(2)}) async-start(bf16[8,96,128]{2,1,0:T(8,128)(2,1)} %copy.49), calls=%async_computation.1 | async-start | bytes 393216 | tf_op jit(solution)/shard_map/all_to_all | solution.py:686
  46.4 8.1 %copy-start.10 = (bf16[3,12,64,128]{3,2,1,0:T(8,128)(2,1)}, bf16[3,12,64,128]{3,2,1,0:T(8,128)(2,1)S(1)}, u32[]{:S(2)}) copy-start(bf16[3,12,64,128]{3,2,1,0:T(8,128)(2,1)S(1)} %collective-permute-done.refs_0_) | copy-start | bytes 1769476
  46.4 23.6 %collective-permute-start.5 = (bf16[3,12,64,128]{3,2,1,0:T(8,128)(2,1)}, bf16[3,12,64,128]{3,2,1,0:T(8,128)(2,1)}, u32[]{:S(2)}, u32[]{:S(2)}) collective-permute-start(bf16[3,12,64,128]{3,2,1,0:T(8,128)(2,1)} %get-tuple-element.57), channel_id=1, source_target_pairs={{0,24},{4,28},{8,16},{12,20},{16,8},{20,12},{24,0},{28,4},{1,25},{... | collective-permute-start | bytes 1769480 | tf_op jit(solution)/shard_map/ppermute | solution.py:35
  47.9 26.8 %collective-permute-start.6 = (bf16[3,12,64,128]{3,2,1,0:T(8,128)(2,1)}, bf16[3,12,64,128]{3,2,1,0:T(8,128)(2,1)}, u32[]{:S(2)}, u32[]{:S(2)}) collective-permute-start(bf16[3,12,64,128]{3,2,1,0:T(8,128)(2,1)} %get-tuple-element.59), channel_id=1, source_target_pairs={{0,28},{4,24},{8,20},{12,16},{16,12},{20,8},{24,4},{28,0},{1,29},{... | collective-permute-start | bytes 1769480 | tf_op jit(solution)/shard_map/ppermute | solution.py:35
  56.8 35.5 %all-to-all-start.2 = ((bf16[8,12,64,128]{3,2,1,0:T(8,128)(2,1)}), bf16[8,12,64,128]{3,2,1,0:T(8,128)(2,1)}, u32[]{:S(2)}, u32[]{:S(2)}) async-start(bf16[8,12,64,128]{3,2,1,0:T(8,128)(2,1)} %constant_dynamic-update-slice_fusion), calls=%async_computation.2 | async-start | bytes 3145728 | tf_op jit(solution)/shard_map/all_to_all | solution.py:723
  97.5 8.3 %collective-permute-start.7 = (bf16[32,1664]{1,0:T(8,128)(2,1)}, bf16[32,1664]{1,0:T(8,128)(2,1)}, u32[]{:S(2)}, u32[]{:S(2)}) collective-permute-start(bf16[32,1664]{1,0:T(8,128)(2,1)} %get-tuple-element.62), channel_id=1, source_target_pairs={{0,1},{1,0},{2,3},{3,2},{4,5},{5,4},{6,7},{7,6},{8,9},{9,8},{10,11... | collective-permute-start | bytes 319496 | tf_op jit(solution)/shard_map/ppermute | solution.py:35
  99.1 11.6 %collective-permute-start.8 = (bf16[32,1664]{1,0:T(8,128)(2,1)}, bf16[32,1664]{1,0:T(8,128)(2,1)}, u32[]{:S(2)}, u32[]{:S(2)}) collective-permute-start(bf16[32,1664]{1,0:T(8,128)(2,1)} %get-tuple-element.63), channel_id=1, source_target_pairs={{0,2},{1,3},{2,0},{3,1},{4,6},{5,7},{6,4},{7,5},{8,10},{9,11},{10,... | collective-permute-start | bytes 319496 | tf_op jit(solution)/shard_map/ppermute | solution.py:35
  101.7 9.0 %collective-permute-start.9 = (bf16[32,1664]{1,0:T(8,128)(2,1)}, bf16[32,1664]{1,0:T(8,128)(2,1)}, u32[]{:S(2)}, u32[]{:S(2)}) collective-permute-start(bf16[32,1664]{1,0:T(8,128)(2,1)} %get-tuple-element.64), channel_id=1, source_target_pairs={{0,3},{1,2},{2,1},{3,0},{4,7},{5,6},{6,5},{7,4},{8,11},{9,10},{10,... | collective-permute-start | bytes 319496 | tf_op jit(solution)/shard_map/ppermute | solution.py:35
  (1 other events, 6.6 us)

commit v4 on v3

--- a/solution.py
+++ b/solution.py
@@ -668,7 +668,7 @@
     packed = pack(mig_ids, mig_dest, reorder, edge_inner, edge_shared, states, groups, early, capacity, edge_block)
     slot_of, recv_rows, new_slots, send_edges, page, send_late = packed[:6]
     sent = dict(enumerate(packed[6:], 1))
-    behind = list(range(groups - 2, groups)) if len(sent) > 2 else []
+    behind = [1, groups - 2, groups - 1] if len(sent) > 2 else []
     early_pages = {step: permute(sent[step], "req", step) for step in sent if step not in behind}
     first = list(range(2, groups, 2))[:2] if early_pages else []
     floating = list(range(3, groups - 1, 2))
@@ -685,7 +685,7 @@
     pieces = pieces[comes_from, edge_rows:]
     arrived = exchange(pieces)
     for step in behind:
-        waiting, _ = lax.optimization_barrier((sent[step], arrived))
+        waiting, _ = lax.optimization_barrier((sent[step], pieces if step == groups - 2 else arrived))
         early_pages[step] = permute(waiting, "req", step)
     arrived = arrived.reshape(states.shape[1:])
     all_rows = lax.all_gather(normed, "head", axis=0, tiled=True)

time: 114 us -> 111 us (0.974)
  waiting for transfers between devices: 17.6 us -> 14.9 us
    all_to_all x1, waiting for transfers between devices: 7.89 us -> 6.48 us  [local(): exchange(lax.dynamic_update_index_in_dim(send_late, arrived, target, 0))]
    ppermute x10, waiting for transfers between devices: 9.66 us -> 8.43 us  [permute(): return lax.ppermute(value, axis, pairs)]
where the time goes in v4:
time: 111 us; the launch traced here: 110 us
  Pallas kernels  31.1 us (28%)
  starting transfers between devices  24.4 us (22%)
  blocking collectives  15 us (14%)
  waiting for transfers between devices  14.9 us (13%)
  local copies, waits for them, and re-layouts  13 us (12%)
  matrix products  4.28 us (4%)
  other arithmetic  4.01 us (4%)
  between operations  3.68 us (3%)
    all_gather x1, blocking collectives, local(): all_rows = lax.all_gather(normed, 'head', axis=0, tiled=True)  15 us
    ppermute x10, starting transfers between devices, permute(): return lax.ppermute(value, axis, pairs)  11 us
    pallas_call x1, Pallas kernels, state_part(): pl.pallas_call(functools.partial(early_kernel, window, batch, groups, str...  9.72 us
    ppermute x10, waiting for transfers between devices, permute(): return lax.ppermute(value, axis, pairs)  8.43 us
    all_to_all x1, waiting for transfers between devices, local(): exchange(lax.dynamic_update_index_in_dim(send_late, arrived, target, 0))  6.48 us
    pallas_call x1, Pallas kernels, pack(): pl.pallas_call(functools.partial(pack_kernel, groups, slots, early, capac...  6.33 us
    unnamed x26, local copies, waits for them, and re-layouts  6.26 us
    pallas_call x1, Pallas kernels, state_part(): pl.pallas_call(functools.partial(hidden_kernel, window, batch, groups, st...  5.13 us
  transfers between devices with their start and end apart: 13, of which 3 were waited for; matrix products, arithmetic and copies ran while one was open for 19% of the time, Pallas kernels for 16%

profile of v4, /device:TPU:2, one launch (start us, length us, event | category | flops | bytes accessed | tf_op | source)
XLA Modules:
  0.0 110.3 jit_solution(3554294294943593730)
XLA Ops:
  0.7 6.3 %pack.1 = (s32[33]{0:T(128)}, s32[33]{0:T(128)}, s32[33]{0:T(128)}, bf16[8,224,128]{2,1,0:T(8,128)(2,1)}, bf16[12,64,128]{2,1,0:T(8,128)(2,1)}, /*index=5*/bf16[...) custom-call(s32[8]{0:T(128)} %ids_hbm.1, ...), custom_call_target="tpu_custom_call" | custom-call | flops 1 | bytes 1 | tf_op jit(solution)/shard_map/pack/pallas_call | solution.py:191
  7.1 4.3 %all-to-all-start = ((bf16[8,224,128]{2,1,0:T(8,128)(2,1)}), bf16[8,224,128]{2,1,0:T(8,128)(2,1)S(1)}, u32[]{:S(2)}, u32[]{:S(2)}) async-start(bf16[8,224,128]{2,1,0:T(8,128)(2,1)} %get-tuple-element.39), calls=%async_computation | async-start | bytes 917504 | tf_op jit(solution)/shard_map/all_to_all | solution.py:679
  11.4 1.5 %collective-permute-start.2 = (bf16[3,12,64,128]{3,2,1,0:T(8,128)(2,1)}, bf16[3,12,64,128]{3,2,1,0:T(8,128)(2,1)S(1)}, u32[]{:S(2)}, u32[]{:S(2)}) collective-permute-start(bf16[3,12,64,128]{3,2,1,0:T(8,128)(2,1)} %get-tuple-element.55), channel_id=1, source_target_pairs={{0,12},{4,8},{8,4},{12,0},{16,28},{20,24},{24,20},{28,16},{1,13},{... | collective-permute-start | bytes 1769480 | tf_op jit(solution)/shard_map/ppermute | solution.py:35
  12.8 1.5 %collective-permute-start.3 = (bf16[3,12,64,128]{3,2,1,0:T(8,128)(2,1)}, bf16[3,12,64,128]{3,2,1,0:T(8,128)(2,1)}, u32[]{:S(2)}, u32[]{:S(2)}) collective-permute-start(bf16[3,12,64,128]{3,2,1,0:T(8,128)(2,1)} %get-tuple-element.56), channel_id=1, source_target_pairs={{0,16},{4,20},{8,24},{12,28},{16,0},{20,4},{24,8},{28,12},{1,17},{... | collective-permute-start | bytes 1769480 | tf_op jit(solution)/shard_map/ppermute | solution.py:35
  15.5 1.0 fusion
  18.2 1.3 %compare_reduce_fusion = (pred[]{:T(512)}, s32[]{:T(128)}) fusion(s32[256]{0:T(256)S(1)} %copy-done.2, s32[]{:T(128)} %bitcast.8), kind=kLoop, calls=%fused_computation.11 | loop fusion | flops 2041 | bytes 1033 | tf_op jit(solution)/shard_map/local/reduce | solution.py:694
  19.7 1.1 %gather_fusion = bf16[8,96,128]{2,0,1:T(8,128)(2,1)S(1)} fusion(bf16[8,224,128]{2,0,1:T(8,128)(2,1)S(1)} %copy.45, s32[8]{0:T(128)S(1)} %fusion.5), kind=kCustom, calls=%fused_computation | custom fusion | bytes 393280 | tf_op jit(solution)/shard_map/gather | solution.py:685
  21.5 4.7 %all-to-all-start.1 = ((bf16[8,96,128]{2,1,0:T(8,128)(2,1)}), bf16[8,96,128]{2,1,0:T(8,128)(2,1)S(1)}, u32[]{:S(2)}, u32[]{:S(2)}) async-start(bf16[8,96,128]{2,1,0:T(8,128)(2,1)} %copy.49), calls=%async_computation.1 | async-start | bytes 393216 | tf_op jit(solution)/shard_map/all_to_all | solution.py:686
  31.4 15.0 %all_gather.3 = bf16[128,1536]{1,0:T(8,128)(2,1)S(1)} all-gather(bf16[32,1536]{1,0:T(8,128)(2,1)S(1)} %fusion.2), channel_id=1, replica_groups=mesh['req'=8,'head'=4] {'head'}, dimensions={0}, use_global_device_ids=true | all-gather | bytes 491520 | tf_op jit(solution)/shard_map/all_gather | solution.py:691
  46.4 1.5 %collective-permute-start.5 = (bf16[3,12,64,128]{3,2,1,0:T(8,128)(2,1)}, bf16[3,12,64,128]{3,2,1,0:T(8,128)(2,1)}, u32[]{:S(2)}, u32[]{:S(2)}) collective-permute-start(bf16[3,12,64,128]{3,2,1,0:T(8,128)(2,1)} %get-tuple-element.59), channel_id=1, source_target_pairs={{0,24},{4,28},{8,16},{12,20},{16,8},{20,12},{24,0},{28,4},{1,25},{... | collective-permute-start | bytes 1769480 | tf_op jit(solution)/shard_map/ppermute | solution.py:35
  48.0 1.5 %collective-permute-start.6 = (bf16[3,12,64,128]{3,2,1,0:T(8,128)(2,1)}, bf16[3,12,64,128]{3,2,1,0:T(8,128)(2,1)}, u32[]{:S(2)}, u32[]{:S(2)}) collective-permute-start(bf16[3,12,64,128]{3,2,1,0:T(8,128)(2,1)} %get-tuple-element.61), channel_id=1, source_target_pairs={{0,28},{4,24},{8,20},{12,16},{16,12},{20,8},{24,4},{28,0},{1,29},{... | collective-permute-start | bytes 1769480 | tf_op jit(solution)/shard_map/ppermute | solution.py:35
  49.9 5.5 %copy.50 = bf16[192,8,2,768]{3,1,2,0:T(8,128)(2,1)} copy(bf16[192,8,2,768]{3,2,1,0:T(2,128)(2,1)} %bitcast.25) | data formatting | bytes 9437184
  57.7 4.4 %all-to-all-start.2 = ((bf16[8,12,64,128]{3,2,1,0:T(8,128)(2,1)}), bf16[8,12,64,128]{3,2,1,0:T(8,128)(2,1)}, u32[]{:S(2)}, u32[]{:S(2)}) async-start(bf16[8,12,64,128]{3,2,1,0:T(8,128)(2,1)} %constant_dynamic-update-slice_fusion), calls=%async_computation.2 | async-start | bytes 3145728 | tf_op jit(solution)/shard_map/all_to_all | solution.py:723
  62.1 3.9 %convolution_convert_fusion.rows_ref = bf16[128,1536]{1,0:T(8,128)(2,1)} fusion(bf16[128,1536]{1,0:T(8,128)(2,1)S(1)} %all_gather.3, bf16[1536,1536]{1,0:T(8,128)(2,1)} %bitcast.24), kind=kOutput, calls=%fused_computation.1 | convolution fusion | flops 604176384 | bytes 5505024 | tf_op jit(solution)/shard_map/dot_general | solution.py:696
  66.0 4.1 %token_rows.1 = (bf16[768,128]{1,0:T(8,128)(2,1)}, bf16[128,128]{1,0:T(8,128)(2,1)}, bf16[128,128]{1,0:T(8,128)(2,1)}, f32[768,128]{1,0:T(8,128)}, f32[16,128]{1...) custom-call(f32[12]{0:T(128)} %skip_ref.1, ...), custom_call_target="tpu_custom_call" | custom-call | flops 1 | bytes 1 | tf_op jit(solution)/shard_map/token_rows/pallas_call | solution.py:367
  70.2 4.5 %collective-permute-done.6.refs_6_ = bf16[3,12,64,128]{3,2,1,0:T(8,128)(2,1)} collective-permute-done((bf16[3,12,64,128]{3,2,1,0:T(8,128)(2,1)}, bf16[3,12,64,128]{3,2,1,0:T(8,128)(2,1)}, u32[]{:S(2)}, u32[]{:S(2)}) %collective-permute-start.6) | collective-permute-done | bytes 589856 | tf_op jit(solution)/shard_map/ppermute | solution.py:35
  74.6 9.7 %early_pages.1 = (bf16[32,12,64,128]{3,2,1,0:T(8,128)(2,1)}, f32[768,128]{1,0:T(8,128)}) custom-call(s32[33]{0:T(128)} %get-tuple-element.37.new_slots, s32[33]{0:T(128)} %get-tuple-element.49.slot_of, f32[16,128]{1,0:T(8,128)} %get-tuple-element.43.decay_hbm, bf16[768,128]{1,0:T(8,128)(2,1)} %get-tuple-element.50.moved_hbm, ...), custom_call_target="tpu_custom_call" | custom-call | flops 12000000000 | bytes 1 | tf_op jit(solution)/shard_map/early_pages/pallas_call | solution.py:559
  84.4 6.5 %all-to-all-done.2.late = bf16[8,12,64,128]{3,2,1,0:T(8,128)(2,1)} async-done(((bf16[8,12,64,128]{3,2,1,0:T(8,128)(2,1)}), bf16[8,12,64,128]{3,2,1,0:T(8,128)(2,1)}, u32[]{:S(2)}, u32[]{:S(2)}) %all-to-all-start.2) | async-done | bytes 1572896 | tf_op jit(solution)/shard_map/all_to_all | solution.py:723
  90.8 5.1 %hidden_rows.1 = (bf16[32,1664]{1,0:T(8,128)(2,1)}, bf16[32,1664]{1,0:T(8,128)(2,1)}, bf16[32,1664]{1,0:T(8,128)(2,1)}, bf16[32,1664]{1,0:T(8,128)(2,1)}) custom-call(s32[33]{0:T(128)} %get-tuple-element.37.new_slots, f32[16,128]{1,0:T(8,128)} %get-tuple-element.43.decay_hbm, bf16[128,128]{1,0:T(8,128)(2,1)} %get-tuple-element.44.readout_hbm, ...), custom_call_target="tpu_custom_call" | custom-call | flops 1 | bytes 1 | tf_op jit(solution)/shard_map/hidden_rows/pallas_call | solution.py:573
  96.8 2.2 %collective-permute-start.8 = (bf16[32,1664]{1,0:T(8,128)(2,1)}, bf16[32,1664]{1,0:T(8,128)(2,1)}, u32[]{:S(2)}, u32[]{:S(2)}) collective-permute-start(bf16[32,1664]{1,0:T(8,128)(2,1)} %get-tuple-element.65), channel_id=1, source_target_pairs={{0,2},{1,3},{2,0},{3,1},{4,6},{5,7},{6,4},{7,5},{8,10},{9,11},{10,... | collective-permute-start | bytes 319496 | tf_op jit(solution)/shard_map/ppermute | solution.py:35
  99.0 1.4 %collective-permute-start.9 = (bf16[32,1664]{1,0:T(8,128)(2,1)}, bf16[32,1664]{1,0:T(8,128)(2,1)}, u32[]{:S(2)}, u32[]{:S(2)}) collective-permute-start(bf16[32,1664]{1,0:T(8,128)(2,1)} %get-tuple-element.66), channel_id=1, source_target_pairs={{0,3},{1,2},{2,1},{3,0},{4,7},{5,6},{6,5},{7,4},{8,11},{9,10},{10,... | collective-permute-start | bytes 319496 | tf_op jit(solution)/shard_map/ppermute | solution.py:35
  100.4 3.9 %late_pages.1 = bf16[32,12,64,128]{3,2,1,0:T(8,128)(2,1)} custom-call(s32[33]{0:T(128)} %get-tuple-element.37.new_slots, f32[16,128]{1,0:T(8,128)} %get-tuple-element.43.decay_hbm, bf16[768,128]{1,0:T(8,128)(2,1)} %get-tuple-element.50.moved_hbm, bf16[128,128]{1,0:T(8,128)(2,1)} %get-tuple-element.51.entry_hbm, ...), custom_call_target="tpu_custom_call", output_to_operand_aliasing={{}: (5, {})} | custom-call | flops 1 | bytes 12582912 | tf_op jit(solution)/shard_map/late_pages/pallas_call | solution.py:587
  104.3 3.9 %collective-permute-done.8.refs_2_ = bf16[32,1664]{1,0:T(8,128)(2,1)} collective-permute-done((bf16[32,1664]{1,0:T(8,128)(2,1)}, bf16[32,1664]{1,0:T(8,128)(2,1)}, u32[]{:S(2)}, u32[]{:S(2)}) %collective-permute-start.8) | collective-permute-done | bytes 106528 | tf_op jit(solution)/shard_map/ppermute | solution.py:35
  108.2 1.9 %finish.1 = bf16[32,1536]{1,0:T(8,128)(2,1)} custom-call(bf16[32,1536]{1,0:T(8,128)(2,1)} %tokens_hbm.1, bf16[32,1664]{1,0:T(8,128)(2,1)} %get-tuple-element.63.refs_0_, bf16[32,1664]{1,0:T(8,128)(2,1)} %collective-permute-done.7.refs_1_, bf16[32,1664]{1,0:T(8,128)(2,1)} %collective-permute-done.8.refs_2_, bf16[32,1664]{1,0:T(8,128)(2,1)} %collective-permute-done.9.refs_3_), custom_call_target="tpu_custom_call" | custom-call | flops 1 | bytes 1 | tf_op jit(solution)/shard_map/finish/pallas_call | solution.py:617
  (56 shorter events, 10.0 us)
Async XLA Ops:
  0.6 48.9 %copy-start = (bf16[1536,304]{0,1:T(8,128)(2,1)S(1)}, bf16[1536,304]{0,1:T(8,128)(2,1)}, u32[]{:S(2)}) copy-start(bf16[1536,304]{0,1:T(8,128)(2,1)} %param.23) | copy-start | bytes 2801668
  0.7 14.2 %copy-start.6 = (s32[8]{0:T(128)S(1)}, s32[8]{0:T(128)}, u32[]{:S(2)}) copy-start(s32[8]{0:T(128)} %ids_hbm.1) | copy-start | bytes 100
  0.7 14.2 %copy-start.5 = (s32[8]{0:T(128)S(1)}, s32[8]{0:T(128)}, u32[]{:S(2)}) copy-start(s32[8]{0:T(128)} %dest_hbm.1) | copy-start | bytes 100
  0.7 17.5 %copy-start.2 = (s32[256]{0:T(256)S(1)}, s32[256]{0:T(256)}, u32[]{:S(2)}) copy-start(s32[256]{0:T(256)} %reorder_hbm.1) | copy-start | bytes 3076
  0.7 15.9 %copy-start.1 = (f32[1536]{0:T(1024)S(1)}, f32[1536]{0:T(1024)}, u32[]{:S(2)}) copy-start(f32[1536]{0:T(1024)} %param.21) | copy-start | bytes 18436
  0.7 25.5 %copy-start.8 = (f32[12]{0:T(128)S(1)}, f32[12]{0:T(128)}, u32[]{:S(2)}) copy-start(f32[12]{0:T(128)} %param.29) | copy-start | bytes 148
  0.7 25.5 %copy-start.9 = (f32[12]{0:T(128)S(1)}, f32[12]{0:T(128)}, u32[]{:S(2)}) copy-start(f32[12]{0:T(128)} %param.28) | copy-start | bytes 148
  0.7 28.7 %copy-start.7 = (s32[32]{0:T(128)S(1)}, s32[32]{0:T(128)}, u32[]{:S(2)}) copy-start(s32[32]{0:T(128)} %param.36) | copy-start | bytes 388
  0.7 29.5 %copy-start.3 = (f32[768]{0:T(1024)S(1)}, f32[768]{0:T(1024)}, u32[]{:S(2)}) copy-start(f32[768]{0:T(1024)} %param.25) | copy-start | bytes 9220
  0.7 30.1 %copy-start.4 = (f32[768]{0:T(1024)S(1)}, f32[768]{0:T(1024)}, u32[]{:S(2)}) copy-start(f32[768]{0:T(1024)} %param.31) | copy-start | bytes 9220
  7.1 12.4 %all-to-all-start = ((bf16[8,224,128]{2,1,0:T(8,128)(2,1)}), bf16[8,224,128]{2,1,0:T(8,128)(2,1)S(1)}, u32[]{:S(2)}, u32[]{:S(2)}) async-start(bf16[8,224,128]{2,1,0:T(8,128)(2,1)} %get-tuple-element.39), calls=%async_computation | async-start | bytes 917504 | tf_op jit(solution)/shard_map/all_to_all | solution.py:679
  11.3 36.5 %collective-permute-start.1 = (bf16[3,12,64,128]{3,2,1,0:T(8,128)(2,1)}, bf16[3,12,64,128]{3,2,1,0:T(8,128)(2,1)S(1)}, u32[]{:S(2)}, u32[]{:S(2)}) collective-permute-start(bf16[3,12,64,128]{3,2,1,0:T(8,128)(2,1)} %get-tuple-element.54), channel_id=1, source_target_pairs={{0,8},{4,12},{8,0},{12,4},{16,24},{20,28},{24,16},{28,20},{1,9},{5... | collective-permute-start | bytes 1769480 | tf_op jit(solution)/shard_map/ppermute | solution.py:35
  11.4 36.6 %collective-permute-start.2 = (bf16[3,12,64,128]{3,2,1,0:T(8,128)(2,1)}, bf16[3,12,64,128]{3,2,1,0:T(8,128)(2,1)S(1)}, u32[]{:S(2)}, u32[]{:S(2)}) collective-permute-start(bf16[3,12,64,128]{3,2,1,0:T(8,128)(2,1)} %get-tuple-element.55), channel_id=1, source_target_pairs={{0,12},{4,8},{8,4},{12,0},{16,28},{20,24},{24,20},{28,16},{1,13},{... | collective-permute-start | bytes 1769480 | tf_op jit(solution)/shard_map/ppermute | solution.py:35
  12.8 57.3 %collective-permute-start.3 = (bf16[3,12,64,128]{3,2,1,0:T(8,128)(2,1)}, bf16[3,12,64,128]{3,2,1,0:T(8,128)(2,1)}, u32[]{:S(2)}, u32[]{:S(2)}) collective-permute-start(bf16[3,12,64,128]{3,2,1,0:T(8,128)(2,1)} %get-tuple-element.56), channel_id=1, source_target_pairs={{0,16},{4,20},{8,24},{12,28},{16,0},{20,4},{24,8},{28,12},{1,17},{... | collective-permute-start | bytes 1769480 | tf_op jit(solution)/shard_map/ppermute | solution.py:35
  14.3 55.8 %collective-permute-start.4 = (bf16[3,12,64,128]{3,2,1,0:T(8,128)(2,1)}, bf16[3,12,64,128]{3,2,1,0:T(8,128)(2,1)}, u32[]{:S(2)}, u32[]{:S(2)}) collective-permute-start(bf16[3,12,64,128]{3,2,1,0:T(8,128)(2,1)} %get-tuple-element.57), channel_id=1, source_target_pairs={{0,20},{4,16},{8,28},{12,24},{16,4},{20,0},{24,12},{28,8},{1,21},{... | collective-permute-start | bytes 1769480 | tf_op jit(solution)/shard_map/ppermute | solution.py:35
  21.5 26.3 %all-to-all-start.1 = ((bf16[8,96,128]{2,1,0:T(8,128)(2,1)}), bf16[8,96,128]{2,1,0:T(8,128)(2,1)S(1)}, u32[]{:S(2)}, u32[]{:S(2)}) async-start(bf16[8,96,128]{2,1,0:T(8,128)(2,1)} %copy.49), calls=%async_computation.1 | async-start | bytes 393216 | tf_op jit(solution)/shard_map/all_to_all | solution.py:686
  46.4 23.7 %collective-permute-start.5 = (bf16[3,12,64,128]{3,2,1,0:T(8,128)(2,1)}, bf16[3,12,64,128]{3,2,1,0:T(8,128)(2,1)}, u32[]{:S(2)}, u32[]{:S(2)}) collective-permute-start(bf16[3,12,64,128]{3,2,1,0:T(8,128)(2,1)} %get-tuple-element.59), channel_id=1, source_target_pairs={{0,24},{4,28},{8,16},{12,20},{16,8},{20,12},{24,0},{28,4},{1,25},{... | collective-permute-start | bytes 1769480 | tf_op jit(solution)/shard_map/ppermute | solution.py:35
  47.9 7.5 %copy-start.10 = (bf16[3,12,64,128]{3,2,1,0:T(8,128)(2,1)}, bf16[3,12,64,128]{3,2,1,0:T(8,128)(2,1)S(1)}, u32[]{:S(2)}) copy-start(bf16[3,12,64,128]{3,2,1,0:T(8,128)(2,1)S(1)} %collective-permute-done.1.refs_1_) | copy-start | bytes 1769476
  47.9 22.3 %collective-permute-start = (bf16[3,12,64,128]{3,2,1,0:T(8,128)(2,1)}, bf16[3,12,64,128]{3,2,1,0:T(8,128)(2,1)}, u32[]{:S(2)}, u32[]{:S(2)}) collective-permute-start(bf16[3,12,64,128]{3,2,1,0:T(8,128)(2,1)} %get-tuple-element.53), channel_id=1, source_target_pairs={{0,4},{4,0},{8,12},{12,8},{16,20},{20,16},{24,28},{28,24},{1,5},{5... | collective-permute-start | bytes 1769480 | tf_op jit(solution)/shard_map/ppermute | solution.py:35
  48.0 26.7 %collective-permute-start.6 = (bf16[3,12,64,128]{3,2,1,0:T(8,128)(2,1)}, bf16[3,12,64,128]{3,2,1,0:T(8,128)(2,1)}, u32[]{:S(2)}, u32[]{:S(2)}) collective-permute-start(bf16[3,12,64,128]{3,2,1,0:T(8,128)(2,1)} %get-tuple-element.61), channel_id=1, source_target_pairs={{0,28},{4,24},{8,20},{12,16},{16,12},{20,8},{24,4},{28,0},{1,29},{... | collective-permute-start | bytes 1769480 | tf_op jit(solution)/shard_map/ppermute | solution.py:35
  57.7 33.1 %all-to-all-start.2 = ((bf16[8,12,64,128]{3,2,1,0:T(8,128)(2,1)}), bf16[8,12,64,128]{3,2,1,0:T(8,128)(2,1)}, u32[]{:S(2)}, u32[]{:S(2)}) async-start(bf16[8,12,64,128]{3,2,1,0:T(8,128)(2,1)} %constant_dynamic-update-slice_fusion), calls=%async_computation.2 | async-start | bytes 3145728 | tf_op jit(solution)/shard_map/all_to_all | solution.py:723
  96.0 8.3 %collective-permute-start.7 = (bf16[32,1664]{1,0:T(8,128)(2,1)}, bf16[32,1664]{1,0:T(8,128)(2,1)}, u32[]{:S(2)}, u32[]{:S(2)}) collective-permute-start(bf16[32,1664]{1,0:T(8,128)(2,1)} %get-tuple-element.64), channel_id=1, source_target_pairs={{0,1},{1,0},{2,3},{3,2},{4,5},{5,4},{6,7},{7,6},{8,9},{9,8},{10,11... | collective-permute-start | bytes 319496 | tf_op jit(solution)/shard_map/ppermute | solution.py:35
  96.8 11.4 %collective-permute-start.8 = (bf16[32,1664]{1,0:T(8,128)(2,1)}, bf16[32,1664]{1,0:T(8,128)(2,1)}, u32[]{:S(2)}, u32[]{:S(2)}) collective-permute-start(bf16[32,1664]{1,0:T(8,128)(2,1)} %get-tuple-element.65), channel_id=1, source_target_pairs={{0,2},{1,3},{2,0},{3,1},{4,6},{5,7},{6,4},{7,5},{8,10},{9,11},{10,... | collective-permute-start | bytes 319496 | tf_op jit(solution)/shard_map/ppermute | solution.py:35
  99.0 9.2 %collective-permute-start.9 = (bf16[32,1664]{1,0:T(8,128)(2,1)}, bf16[32,1664]{1,0:T(8,128)(2,1)}, u32[]{:S(2)}, u32[]{:S(2)}) collective-permute-start(bf16[32,1664]{1,0:T(8,128)(2,1)} %get-tuple-element.66), channel_id=1, source_target_pairs={{0,3},{1,2},{2,1},{3,0},{4,7},{5,6},{6,5},{7,4},{8,11},{9,10},{10,... | collective-permute-start | bytes 319496 | tf_op jit(solution)/shard_map/ppermute | solution.py:35
  (1 other events, 7.4 us)

commit v5 on v4

--- a/solution.py
+++ b/solution.py
@@ -103,20 +103,18 @@
     peer = lax.div(place[first + moving], slots)
     slot_of[peer * stride + seen[peer]] = moving
 
-    for read in reads:
-        read.wait()
-    writes = [pltpu.make_async_copy(staged.at[moving], leaving, write_done.at[0])]
-    writes[-1].start()
+    jobs = [(moving, leaving)]
     for step in range(1, groups):
         peer = peer_of(device, step, groups)
-        for rank in range(early):
-            slot = slot_of[peer * stride + rank]
-            writes.append(pltpu.make_async_copy(staged.at[slot], out_early[step - 1].at[rank], write_done.at[0]))
-            writes[-1].start()
-    for peer in range(groups):
-        slot = slot_of[peer * stride + stride - 1]
-        writes.append(pltpu.make_async_copy(staged.at[slot], out_late.at[peer], write_done.at[0]))
-        writes[-1].start()
+        jobs += [(slot_of[peer * stride + rank], out_early[step - 1].at[rank]) for rank in range(early)]
+    jobs += [(slot_of[peer * stride + stride - 1], out_late.at[peer]) for peer in range(groups)]
+    writes = [pltpu.make_async_copy(staged.at[slot], target, write_done.at[0]) for slot, target in jobs]
+    half = len(reads) // 2
+    for lower in (True, False):
+        for read in reads[:half] if lower else reads[half:]:
+            read.wait()
+        for (slot, _), write in zip(jobs, writes):
+            pl.when((slot < half * chunk) == lower)(write.start)
 
     pieces = staged[moving].reshape(-1, staged.shape[3])
     edge_rows = edge_block * (inner.shape[2] + shared.shape[2]) // staged.shape[3]
@@ -743,7 +741,7 @@
         groups,
         shares,
     )
-    messages = [permute(message, "head", step) if step else message for step, message in enumerate(messages)]
+    messages = [permute(messages[step], "head", step) for step in range(shares - 1, 0, -1)] + [messages[0]]
     hidden_out = finish(tokens, messages, inner * shares)
     return (hidden_out, states_out, edge_inner_out, edge_shared_out)
 

time: 111 us -> 111 us (level)
  no operation moved by 1% of the time
where the time goes in v5:
time: 111 us; the launch traced here: 110 us
  Pallas kernels  30.7 us (28%)
  starting transfers between devices  24.4 us (22%)
  waiting for transfers between devices  15 us (14%)
  blocking collectives  15 us (14%)
  local copies, waits for them, and re-layouts  13 us (12%)
  matrix products  4.28 us (4%)
  other arithmetic  4.01 us (4%)
  between operations  3.68 us (3%)
    all_gather x1, blocking collectives, local(): all_rows = lax.all_gather(normed, 'head', axis=0, tiled=True)  15 us
    ppermute x10, starting transfers between devices, permute(): return lax.ppermute(value, axis, pairs)  11 us
    pallas_call x1, Pallas kernels, state_part(): pl.pallas_call(functools.partial(early_kernel, window, batch, groups, str...  9.72 us
    ppermute x10, waiting for transfers between devices, permute(): return lax.ppermute(value, axis, pairs)  8.53 us
    all_to_all x1, waiting for transfers between devices, local(): exchange(lax.dynamic_update_index_in_dim(send_late, arrived, target, 0))  6.48 us
    unnamed x26, local copies, waits for them, and re-layouts  6.26 us
    pallas_call x1, Pallas kernels, pack(): pl.pallas_call(functools.partial(pack_kernel, groups, slots, early, capac...  6 us
    pallas_call x1, Pallas kernels, state_part(): pl.pallas_call(functools.partial(hidden_kernel, window, batch, groups, st...  5.13 us
  transfers between devices with their start and end apart: 13, of which 3 were waited for; matrix products, arithmetic and copies ran while one was open for 19% of the time, Pallas kernels for 16%

profile of v5, /device:TPU:2, one launch (start us, length us, event | category | flops | bytes accessed | tf_op | source)
XLA Modules:
  0.0 110.1 jit_solution(6509803028321633423)
XLA Ops:
  0.7 6.0 %pack.1 = (s32[33]{0:T(128)}, s32[33]{0:T(128)}, s32[33]{0:T(128)}, bf16[8,224,128]{2,1,0:T(8,128)(2,1)}, bf16[12,64,128]{2,1,0:T(8,128)(2,1)}, /*index=5*/bf16[...) custom-call(s32[8]{0:T(128)} %ids_hbm.1, ...), custom_call_target="tpu_custom_call" | custom-call | flops 1 | bytes 1 | tf_op jit(solution)/shard_map/pack/pallas_call | solution.py:189
  6.8 4.3 %all-to-all-start = ((bf16[8,224,128]{2,1,0:T(8,128)(2,1)}), bf16[8,224,128]{2,1,0:T(8,128)(2,1)S(1)}, u32[]{:S(2)}, u32[]{:S(2)}) async-start(bf16[8,224,128]{2,1,0:T(8,128)(2,1)} %get-tuple-element.39), calls=%async_computation | async-start | bytes 917504 | tf_op jit(solution)/shard_map/all_to_all | solution.py:677
  11.1 1.5 %collective-permute-start.2 = (bf16[3,12,64,128]{3,2,1,0:T(8,128)(2,1)}, bf16[3,12,64,128]{3,2,1,0:T(8,128)(2,1)S(1)}, u32[]{:S(2)}, u32[]{:S(2)}) collective-permute-start(bf16[3,12,64,128]{3,2,1,0:T(8,128)(2,1)} %get-tuple-element.55), channel_id=1, source_target_pairs={{0,12},{4,8},{8,4},{12,0},{16,28},{20,24},{24,20},{28,16},{1,13},{... | collective-permute-start | bytes 1769480 | tf_op jit(solution)/shard_map/ppermute | solution.py:35
  12.5 1.5 %collective-permute-start.3 = (bf16[3,12,64,128]{3,2,1,0:T(8,128)(2,1)}, bf16[3,12,64,128]{3,2,1,0:T(8,128)(2,1)}, u32[]{:S(2)}, u32[]{:S(2)}) collective-permute-start(bf16[3,12,64,128]{3,2,1,0:T(8,128)(2,1)} %get-tuple-element.56), channel_id=1, source_target_pairs={{0,16},{4,20},{8,24},{12,28},{16,0},{20,4},{24,8},{28,12},{1,17},{... | collective-permute-start | bytes 1769480 | tf_op jit(solution)/shard_map/ppermute | solution.py:35
  15.2 1.0 fusion
  17.8 1.3 %compare_reduce_fusion = (pred[]{:T(512)}, s32[]{:T(128)}) fusion(s32[256]{0:T(256)S(1)} %copy-done.2, s32[]{:T(128)} %bitcast.8), kind=kLoop, calls=%fused_computation.11 | loop fusion | flops 2041 | bytes 1033 | tf_op jit(solution)/shard_map/local/reduce | solution.py:692
  19.3 1.1 %gather_fusion = bf16[8,96,128]{2,0,1:T(8,128)(2,1)S(1)} fusion(bf16[8,224,128]{2,0,1:T(8,128)(2,1)S(1)} %copy.45, s32[8]{0:T(128)S(1)} %fusion.5), kind=kCustom, calls=%fused_computation | custom fusion | bytes 393280 | tf_op jit(solution)/shard_map/gather | solution.py:683
  21.2 4.7 %all-to-all-start.1 = ((bf16[8,96,128]{2,1,0:T(8,128)(2,1)}), bf16[8,96,128]{2,1,0:T(8,128)(2,1)S(1)}, u32[]{:S(2)}, u32[]{:S(2)}) async-start(bf16[8,96,128]{2,1,0:T(8,128)(2,1)} %copy.49), calls=%async_computation.1 | async-start | bytes 393216 | tf_op jit(solution)/shard_map/all_to_all | solution.py:684
  31.1 15.0 %all_gather.3 = bf16[128,1536]{1,0:T(8,128)(2,1)S(1)} all-gather(bf16[32,1536]{1,0:T(8,128)(2,1)S(1)} %fusion.2), channel_id=1, replica_groups=mesh['req'=8,'head'=4] {'head'}, dimensions={0}, use_global_device_ids=true | all-gather | bytes 491520 | tf_op jit(solution)/shard_map/all_gather | solution.py:689
  46.1 1.5 %collective-permute-start.5 = (bf16[3,12,64,128]{3,2,1,0:T(8,128)(2,1)}, bf16[3,12,64,128]{3,2,1,0:T(8,128)(2,1)}, u32[]{:S(2)}, u32[]{:S(2)}) collective-permute-start(bf16[3,12,64,128]{3,2,1,0:T(8,128)(2,1)} %get-tuple-element.59), channel_id=1, source_target_pairs={{0,24},{4,28},{8,16},{12,20},{16,8},{20,12},{24,0},{28,4},{1,25},{... | collective-permute-start | bytes 1769480 | tf_op jit(solution)/shard_map/ppermute | solution.py:35
  47.6 1.5 %collective-permute-start.6 = (bf16[3,12,64,128]{3,2,1,0:T(8,128)(2,1)}, bf16[3,12,64,128]{3,2,1,0:T(8,128)(2,1)}, u32[]{:S(2)}, u32[]{:S(2)}) collective-permute-start(bf16[3,12,64,128]{3,2,1,0:T(8,128)(2,1)} %get-tuple-element.61), channel_id=1, source_target_pairs={{0,28},{4,24},{8,20},{12,16},{16,12},{20,8},{24,4},{28,0},{1,29},{... | collective-permute-start | bytes 1769480 | tf_op jit(solution)/shard_map/ppermute | solution.py:35
  49.6 5.5 %copy.50 = bf16[192,8,2,768]{3,1,2,0:T(8,128)(2,1)} copy(bf16[192,8,2,768]{3,2,1,0:T(2,128)(2,1)} %bitcast.25) | data formatting | bytes 9437184
  57.4 4.4 %all-to-all-start.2 = ((bf16[8,12,64,128]{3,2,1,0:T(8,128)(2,1)}), bf16[8,12,64,128]{3,2,1,0:T(8,128)(2,1)}, u32[]{:S(2)}, u32[]{:S(2)}) async-start(bf16[8,12,64,128]{3,2,1,0:T(8,128)(2,1)} %constant_dynamic-update-slice_fusion), calls=%async_computation.2 | async-start | bytes 3145728 | tf_op jit(solution)/shard_map/all_to_all | solution.py:721
  61.8 3.9 %convolution_convert_fusion.rows_ref = bf16[128,1536]{1,0:T(8,128)(2,1)} fusion(bf16[128,1536]{1,0:T(8,128)(2,1)S(1)} %all_gather.3, bf16[1536,1536]{1,0:T(8,128)(2,1)} %bitcast.24), kind=kOutput, calls=%fused_computation.1 | convolution fusion | flops 604176384 | bytes 5505024 | tf_op jit(solution)/shard_map/dot_general | solution.py:694
  65.7 4.1 %token_rows.1 = (bf16[768,128]{1,0:T(8,128)(2,1)}, bf16[128,128]{1,0:T(8,128)(2,1)}, bf16[128,128]{1,0:T(8,128)(2,1)}, f32[768,128]{1,0:T(8,128)}, f32[16,128]{1...) custom-call(f32[12]{0:T(128)} %skip_ref.1, ...), custom_call_target="tpu_custom_call" | custom-call | flops 1 | bytes 1 | tf_op jit(solution)/shard_map/token_rows/pallas_call | solution.py:365
  69.8 4.5 %collective-permute-done.6.refs_6_ = bf16[3,12,64,128]{3,2,1,0:T(8,128)(2,1)} collective-permute-done((bf16[3,12,64,128]{3,2,1,0:T(8,128)(2,1)}, bf16[3,12,64,128]{3,2,1,0:T(8,128)(2,1)}, u32[]{:S(2)}, u32[]{:S(2)}) %collective-permute-start.6) | collective-permute-done | bytes 589856 | tf_op jit(solution)/shard_map/ppermute | solution.py:35
  74.3 9.7 %early_pages.1 = (bf16[32,12,64,128]{3,2,1,0:T(8,128)(2,1)}, f32[768,128]{1,0:T(8,128)}) custom-call(s32[33]{0:T(128)} %get-tuple-element.37.new_slots, s32[33]{0:T(128)} %get-tuple-element.49.slot_of, f32[16,128]{1,0:T(8,128)} %get-tuple-element.43.decay_hbm, bf16[768,128]{1,0:T(8,128)(2,1)} %get-tuple-element.50.moved_hbm, ...), custom_call_target="tpu_custom_call" | custom-call | flops 12000000000 | bytes 1 | tf_op jit(solution)/shard_map/early_pages/pallas_call | solution.py:557
  84.0 6.5 %all-to-all-done.2.late = bf16[8,12,64,128]{3,2,1,0:T(8,128)(2,1)} async-done(((bf16[8,12,64,128]{3,2,1,0:T(8,128)(2,1)}), bf16[8,12,64,128]{3,2,1,0:T(8,128)(2,1)}, u32[]{:S(2)}, u32[]{:S(2)}) %all-to-all-start.2) | async-done | bytes 1572896 | tf_op jit(solution)/shard_map/all_to_all | solution.py:721
  90.5 5.1 %hidden_rows.1 = (bf16[32,1664]{1,0:T(8,128)(2,1)}, bf16[32,1664]{1,0:T(8,128)(2,1)}, bf16[32,1664]{1,0:T(8,128)(2,1)}, bf16[32,1664]{1,0:T(8,128)(2,1)}) custom-call(s32[33]{0:T(128)} %get-tuple-element.37.new_slots, f32[16,128]{1,0:T(8,128)} %get-tuple-element.43.decay_hbm, bf16[128,128]{1,0:T(8,128)(2,1)} %get-tuple-element.44.readout_hbm, ...), custom_call_target="tpu_custom_call" | custom-call | flops 1 | bytes 1 | tf_op jit(solution)/shard_map/hidden_rows/pallas_call | solution.py:571
  95.7 2.5 %collective-permute-start.7 = (bf16[32,1664]{1,0:T(8,128)(2,1)}, bf16[32,1664]{1,0:T(8,128)(2,1)}, u32[]{:S(2)}, u32[]{:S(2)}) collective-permute-start(bf16[32,1664]{1,0:T(8,128)(2,1)} %get-tuple-element.63), channel_id=1, source_target_pairs={{0,3},{1,2},{2,1},{3,0},{4,7},{5,6},{6,5},{7,4},{8,11},{9,10},{10,... | collective-permute-start | bytes 319496 | tf_op jit(solution)/shard_map/ppermute | solution.py:35
  98.1 2.0 %collective-permute-start.9 = (bf16[32,1664]{1,0:T(8,128)(2,1)}, bf16[32,1664]{1,0:T(8,128)(2,1)}, u32[]{:S(2)}, u32[]{:S(2)}) collective-permute-start(bf16[32,1664]{1,0:T(8,128)(2,1)} %get-tuple-element.65), channel_id=1, source_target_pairs={{0,1},{1,0},{2,3},{3,2},{4,5},{5,4},{6,7},{7,6},{8,9},{9,8},{10,11... | collective-permute-start | bytes 319496 | tf_op jit(solution)/shard_map/ppermute | solution.py:35
  100.1 3.8 %late_pages.1 = bf16[32,12,64,128]{3,2,1,0:T(8,128)(2,1)} custom-call(s32[33]{0:T(128)} %get-tuple-element.37.new_slots, f32[16,128]{1,0:T(8,128)} %get-tuple-element.43.decay_hbm, bf16[768,128]{1,0:T(8,128)(2,1)} %get-tuple-element.50.moved_hbm, bf16[128,128]{1,0:T(8,128)(2,1)} %get-tuple-element.51.entry_hbm, ...), custom_call_target="tpu_custom_call", output_to_operand_aliasing={{}: (5, {})} | custom-call | flops 1 | bytes 12582912 | tf_op jit(solution)/shard_map/late_pages/pallas_call | solution.py:585
  104.0 4.0 %collective-permute-done.8.refs_1_ = bf16[32,1664]{1,0:T(8,128)(2,1)} collective-permute-done((bf16[32,1664]{1,0:T(8,128)(2,1)}, bf16[32,1664]{1,0:T(8,128)(2,1)}, u32[]{:S(2)}, u32[]{:S(2)}) %collective-permute-start.8) | collective-permute-done | bytes 106528 | tf_op jit(solution)/shard_map/ppermute | solution.py:35
  108.0 1.9 %finish.1 = bf16[32,1536]{1,0:T(8,128)(2,1)} custom-call(bf16[32,1536]{1,0:T(8,128)(2,1)} %tokens_hbm.1, bf16[32,1664]{1,0:T(8,128)(2,1)} %collective-permute-done.7.refs_0_, bf16[32,1664]{1,0:T(8,128)(2,1)} %collective-permute-done.8.refs_1_, bf16[32,1664]{1,0:T(8,128)(2,1)} %collective-permute-done.9.refs_2_, bf16[32,1664]{1,0:T(8,128)(2,1)} %get-tuple-element.66.refs_3_), custom_call_target="tpu_custom_call" | custom-call | flops 1 | bytes 1 | tf_op jit(solution)/shard_map/finish/pallas_call | solution.py:615
  (56 shorter events, 9.2 us)
Async XLA Ops:
  0.6 48.6 %copy-start = (bf16[1536,304]{0,1:T(8,128)(2,1)S(1)}, bf16[1536,304]{0,1:T(8,128)(2,1)}, u32[]{:S(2)}) copy-start(bf16[1536,304]{0,1:T(8,128)(2,1)} %param.23) | copy-start | bytes 2801668
  0.7 13.9 %copy-start.6 = (s32[8]{0:T(128)S(1)}, s32[8]{0:T(128)}, u32[]{:S(2)}) copy-start(s32[8]{0:T(128)} %ids_hbm.1) | copy-start | bytes 100
  0.7 13.8 %copy-start.5 = (s32[8]{0:T(128)S(1)}, s32[8]{0:T(128)}, u32[]{:S(2)}) copy-start(s32[8]{0:T(128)} %dest_hbm.1) | copy-start | bytes 100
  0.7 17.2 %copy-start.2 = (s32[256]{0:T(256)S(1)}, s32[256]{0:T(256)}, u32[]{:S(2)}) copy-start(s32[256]{0:T(256)} %reorder_hbm.1) | copy-start | bytes 3076
  0.7 15.6 %copy-start.1 = (f32[1536]{0:T(1024)S(1)}, f32[1536]{0:T(1024)}, u32[]{:S(2)}) copy-start(f32[1536]{0:T(1024)} %param.21) | copy-start | bytes 18436
  0.7 25.2 %copy-start.8 = (f32[12]{0:T(128)S(1)}, f32[12]{0:T(128)}, u32[]{:S(2)}) copy-start(f32[12]{0:T(128)} %param.29) | copy-start | bytes 148
  0.7 25.2 %copy-start.9 = (f32[12]{0:T(128)S(1)}, f32[12]{0:T(128)}, u32[]{:S(2)}) copy-start(f32[12]{0:T(128)} %param.28) | copy-start | bytes 148
  0.7 28.4 %copy-start.7 = (s32[32]{0:T(128)S(1)}, s32[32]{0:T(128)}, u32[]{:S(2)}) copy-start(s32[32]{0:T(128)} %param.36) | copy-start | bytes 388
  0.7 29.2 %copy-start.3 = (f32[768]{0:T(1024)S(1)}, f32[768]{0:T(1024)}, u32[]{:S(2)}) copy-start(f32[768]{0:T(1024)} %param.25) | copy-start | bytes 9220
  0.7 29.7 %copy-start.4 = (f32[768]{0:T(1024)S(1)}, f32[768]{0:T(1024)}, u32[]{:S(2)}) copy-start(f32[768]{0:T(1024)} %param.31) | copy-start | bytes 9220
  6.8 12.4 %all-to-all-start = ((bf16[8,224,128]{2,1,0:T(8,128)(2,1)}), bf16[8,224,128]{2,1,0:T(8,128)(2,1)S(1)}, u32[]{:S(2)}, u32[]{:S(2)}) async-start(bf16[8,224,128]{2,1,0:T(8,128)(2,1)} %get-tuple-element.39), calls=%async_computation | async-start | bytes 917504 | tf_op jit(solution)/shard_map/all_to_all | solution.py:677
  11.0 36.5 %collective-permute-start.1 = (bf16[3,12,64,128]{3,2,1,0:T(8,128)(2,1)}, bf16[3,12,64,128]{3,2,1,0:T(8,128)(2,1)S(1)}, u32[]{:S(2)}, u32[]{:S(2)}) collective-permute-start(bf16[3,12,64,128]{3,2,1,0:T(8,128)(2,1)} %get-tuple-element.54), channel_id=1, source_target_pairs={{0,8},{4,12},{8,0},{12,4},{16,24},{20,28},{24,16},{28,20},{1,9},{5... | collective-permute-start | bytes 1769480 | tf_op jit(solution)/shard_map/ppermute | solution.py:35
  11.1 36.6 %collective-permute-start.2 = (bf16[3,12,64,128]{3,2,1,0:T(8,128)(2,1)}, bf16[3,12,64,128]{3,2,1,0:T(8,128)(2,1)S(1)}, u32[]{:S(2)}, u32[]{:S(2)}) collective-permute-start(bf16[3,12,64,128]{3,2,1,0:T(8,128)(2,1)} %get-tuple-element.55), channel_id=1, source_target_pairs={{0,12},{4,8},{8,4},{12,0},{16,28},{20,24},{24,20},{28,16},{1,13},{... | collective-permute-start | bytes 1769480 | tf_op jit(solution)/shard_map/ppermute | solution.py:35
  12.5 57.3 %collective-permute-start.3 = (bf16[3,12,64,128]{3,2,1,0:T(8,128)(2,1)}, bf16[3,12,64,128]{3,2,1,0:T(8,128)(2,1)}, u32[]{:S(2)}, u32[]{:S(2)}) collective-permute-start(bf16[3,12,64,128]{3,2,1,0:T(8,128)(2,1)} %get-tuple-element.56), channel_id=1, source_target_pairs={{0,16},{4,20},{8,24},{12,28},{16,0},{20,4},{24,8},{28,12},{1,17},{... | collective-permute-start | bytes 1769480 | tf_op jit(solution)/shard_map/ppermute | solution.py:35
  14.0 55.8 %collective-permute-start.4 = (bf16[3,12,64,128]{3,2,1,0:T(8,128)(2,1)}, bf16[3,12,64,128]{3,2,1,0:T(8,128)(2,1)}, u32[]{:S(2)}, u32[]{:S(2)}) collective-permute-start(bf16[3,12,64,128]{3,2,1,0:T(8,128)(2,1)} %get-tuple-element.57), channel_id=1, source_target_pairs={{0,20},{4,16},{8,28},{12,24},{16,4},{20,0},{24,12},{28,8},{1,21},{... | collective-permute-start | bytes 1769480 | tf_op jit(solution)/shard_map/ppermute | solution.py:35
  21.2 26.4 %all-to-all-start.1 = ((bf16[8,96,128]{2,1,0:T(8,128)(2,1)}), bf16[8,96,128]{2,1,0:T(8,128)(2,1)S(1)}, u32[]{:S(2)}, u32[]{:S(2)}) async-start(bf16[8,96,128]{2,1,0:T(8,128)(2,1)} %copy.49), calls=%async_computation.1 | async-start | bytes 393216 | tf_op jit(solution)/shard_map/all_to_all | solution.py:684
  46.1 23.8 %collective-permute-start.5 = (bf16[3,12,64,128]{3,2,1,0:T(8,128)(2,1)}, bf16[3,12,64,128]{3,2,1,0:T(8,128)(2,1)}, u32[]{:S(2)}, u32[]{:S(2)}) collective-permute-start(bf16[3,12,64,128]{3,2,1,0:T(8,128)(2,1)} %get-tuple-element.59), channel_id=1, source_target_pairs={{0,24},{4,28},{8,16},{12,20},{16,8},{20,12},{24,0},{28,4},{1,25},{... | collective-permute-start | bytes 1769480 | tf_op jit(solution)/shard_map/ppermute | solution.py:35
  47.5 7.5 %copy-start.10 = (bf16[3,12,64,128]{3,2,1,0:T(8,128)(2,1)}, bf16[3,12,64,128]{3,2,1,0:T(8,128)(2,1)S(1)}, u32[]{:S(2)}) copy-start(bf16[3,12,64,128]{3,2,1,0:T(8,128)(2,1)S(1)} %collective-permute-done.1.refs_1_) | copy-start | bytes 1769476
  47.5 22.3 %collective-permute-start = (bf16[3,12,64,128]{3,2,1,0:T(8,128)(2,1)}, bf16[3,12,64,128]{3,2,1,0:T(8,128)(2,1)}, u32[]{:S(2)}, u32[]{:S(2)}) collective-permute-start(bf16[3,12,64,128]{3,2,1,0:T(8,128)(2,1)} %get-tuple-element.53), channel_id=1, source_target_pairs={{0,4},{4,0},{8,12},{12,8},{16,20},{20,16},{24,28},{28,24},{1,5},{5... | collective-permute-start | bytes 1769480 | tf_op jit(solution)/shard_map/ppermute | solution.py:35
  47.6 26.7 %collective-permute-start.6 = (bf16[3,12,64,128]{3,2,1,0:T(8,128)(2,1)}, bf16[3,12,64,128]{3,2,1,0:T(8,128)(2,1)}, u32[]{:S(2)}, u32[]{:S(2)}) collective-permute-start(bf16[3,12,64,128]{3,2,1,0:T(8,128)(2,1)} %get-tuple-element.61), channel_id=1, source_target_pairs={{0,28},{4,24},{8,20},{12,16},{16,12},{20,8},{24,4},{28,0},{1,29},{... | collective-permute-start | bytes 1769480 | tf_op jit(solution)/shard_map/ppermute | solution.py:35
  57.4 33.1 %all-to-all-start.2 = ((bf16[8,12,64,128]{3,2,1,0:T(8,128)(2,1)}), bf16[8,12,64,128]{3,2,1,0:T(8,128)(2,1)}, u32[]{:S(2)}, u32[]{:S(2)}) async-start(bf16[8,12,64,128]{3,2,1,0:T(8,128)(2,1)} %constant_dynamic-update-slice_fusion), calls=%async_computation.2 | async-start | bytes 3145728 | tf_op jit(solution)/shard_map/all_to_all | solution.py:721
  95.7 8.3 %collective-permute-start.7 = (bf16[32,1664]{1,0:T(8,128)(2,1)}, bf16[32,1664]{1,0:T(8,128)(2,1)}, u32[]{:S(2)}, u32[]{:S(2)}) collective-permute-start(bf16[32,1664]{1,0:T(8,128)(2,1)} %get-tuple-element.63), channel_id=1, source_target_pairs={{0,3},{1,2},{2,1},{3,0},{4,7},{5,6},{6,5},{7,4},{8,11},{9,10},{10,... | collective-permute-start | bytes 319496 | tf_op jit(solution)/shard_map/ppermute | solution.py:35
  98.1 9.9 %collective-permute-start.8 = (bf16[32,1664]{1,0:T(8,128)(2,1)}, bf16[32,1664]{1,0:T(8,128)(2,1)}, u32[]{:S(2)}, u32[]{:S(2)}) collective-permute-start(bf16[32,1664]{1,0:T(8,128)(2,1)} %get-tuple-element.64), channel_id=1, source_target_pairs={{0,2},{1,3},{2,0},{3,1},{4,6},{5,7},{6,4},{7,5},{8,10},{9,11},{10,... | collective-permute-start | bytes 319496 | tf_op jit(solution)/shard_map/ppermute | solution.py:35
  98.1 9.9 %collective-permute-start.9 = (bf16[32,1664]{1,0:T(8,128)(2,1)}, bf16[32,1664]{1,0:T(8,128)(2,1)}, u32[]{:S(2)}, u32[]{:S(2)}) collective-permute-start(bf16[32,1664]{1,0:T(8,128)(2,1)} %get-tuple-element.65), channel_id=1, source_target_pairs={{0,1},{1,0},{2,3},{3,2},{4,5},{5,4},{6,7},{7,6},{8,9},{9,8},{10,11... | collective-permute-start | bytes 319496 | tf_op jit(solution)/shard_map/ppermute | solution.py:35
  (1 other events, 7.4 us)

commit v6 on v5

--- a/solution.py
+++ b/solution.py
@@ -109,12 +109,10 @@
         jobs += [(slot_of[peer * stride + rank], out_early[step - 1].at[rank]) for rank in range(early)]
     jobs += [(slot_of[peer * stride + stride - 1], out_late.at[peer]) for peer in range(groups)]
     writes = [pltpu.make_async_copy(staged.at[slot], target, write_done.at[0]) for slot, target in jobs]
-    half = len(reads) // 2
-    for lower in (True, False):
-        for read in reads[:half] if lower else reads[half:]:
-            read.wait()
+    for part, read in enumerate(reads):
+        read.wait()
         for (slot, _), write in zip(jobs, writes):
-            pl.when((slot < half * chunk) == lower)(write.start)
+            pl.when(lax.div(slot, chunk) == part)(write.start)
 
     pieces = staged[moving].reshape(-1, staged.shape[3])
     edge_rows = edge_block * (inner.shape[2] + shared.shape[2]) // staged.shape[3]

time: 111 us -> 112 us (level)
  Pallas kernels: 30.7 us -> 31.9 us
    pallas_call x1, Pallas kernels: 6 us -> 7.18 us  [pack(): pl.pallas_call(functools.partial(pack_kernel, groups, slots, early, capac...]
where the time goes in v6:
time: 112 us; the launch traced here: 111 us
  Pallas kernels  31.9 us (28%)
  starting transfers between devices  24.4 us (22%)
  waiting for transfers between devices  15 us (13%)
  blocking collectives  15 us (13%)
  local copies, waits for them, and re-layouts  13 us (12%)
  matrix products  4.28 us (4%)
  other arithmetic  4.01 us (4%)
  between operations  3.68 us (3%)
    all_gather x1, blocking collectives, local(): all_rows = lax.all_gather(normed, 'head', axis=0, tiled=True)  15 us
    ppermute x10, starting transfers between devices, permute(): return lax.ppermute(value, axis, pairs)  11 us
    pallas_call x1, Pallas kernels, state_part(): pl.pallas_call(functools.partial(early_kernel, window, batch, groups, str...  9.71 us
    ppermute x10, waiting for transfers between devices, permute(): return lax.ppermute(value, axis, pairs)  8.54 us
    pallas_call x1, Pallas kernels, pack(): pl.pallas_call(functools.partial(pack_kernel, groups, slots, early, capac...  7.18 us
    all_to_all x1, waiting for transfers between devices, local(): exchange(lax.dynamic_update_index_in_dim(send_late, arrived, target, 0))  6.48 us
    unnamed x26, local copies, waits for them, and re-layouts  6.26 us
    pallas_call x1, Pallas kernels, state_part(): pl.pallas_call(functools.partial(hidden_kernel, window, batch, groups, st...  5.14 us
  transfers between devices with their start and end apart: 13, of which 3 were waited for; matrix products, arithmetic and copies ran while one was open for 19% of the time, Pallas kernels for 16%

profile of v6, /device:TPU:2, one launch (start us, length us, event | category | flops | bytes accessed | tf_op | source)
XLA Modules:
  0.0 111.3 jit_solution(2707545475166317544)
XLA Ops:
  0.7 7.2 %pack.1 = (s32[33]{0:T(128)}, s32[33]{0:T(128)}, s32[33]{0:T(128)}, bf16[8,224,128]{2,1,0:T(8,128)(2,1)}, bf16[12,64,128]{2,1,0:T(8,128)(2,1)}, /*index=5*/bf16[...) custom-call(s32[8]{0:T(128)} %ids_hbm.1, ...), custom_call_target="tpu_custom_call" | custom-call | flops 1 | bytes 1 | tf_op jit(solution)/shard_map/pack/pallas_call | solution.py:187
  7.9 4.3 %all-to-all-start = ((bf16[8,224,128]{2,1,0:T(8,128)(2,1)}), bf16[8,224,128]{2,1,0:T(8,128)(2,1)S(1)}, u32[]{:S(2)}, u32[]{:S(2)}) async-start(bf16[8,224,128]{2,1,0:T(8,128)(2,1)} %get-tuple-element.39), calls=%async_computation | async-start | bytes 917504 | tf_op jit(solution)/shard_map/all_to_all | solution.py:675
  12.2 1.5 %collective-permute-start.2 = (bf16[3,12,64,128]{3,2,1,0:T(8,128)(2,1)}, bf16[3,12,64,128]{3,2,1,0:T(8,128)(2,1)S(1)}, u32[]{:S(2)}, u32[]{:S(2)}) collective-permute-start(bf16[3,12,64,128]{3,2,1,0:T(8,128)(2,1)} %get-tuple-element.55), channel_id=1, source_target_pairs={{0,12},{4,8},{8,4},{12,0},{16,28},{20,24},{24,20},{28,16},{1,13},{... | collective-permute-start | bytes 1769480 | tf_op jit(solution)/shard_map/ppermute | solution.py:35
  13.7 1.5 %collective-permute-start.3 = (bf16[3,12,64,128]{3,2,1,0:T(8,128)(2,1)}, bf16[3,12,64,128]{3,2,1,0:T(8,128)(2,1)}, u32[]{:S(2)}, u32[]{:S(2)}) collective-permute-start(bf16[3,12,64,128]{3,2,1,0:T(8,128)(2,1)} %get-tuple-element.56), channel_id=1, source_target_pairs={{0,16},{4,20},{8,24},{12,28},{16,0},{20,4},{24,8},{28,12},{1,17},{... | collective-permute-start | bytes 1769480 | tf_op jit(solution)/shard_map/ppermute | solution.py:35
  16.4 1.0 fusion
  19.0 1.3 %compare_reduce_fusion = (pred[]{:T(512)}, s32[]{:T(128)}) fusion(s32[256]{0:T(256)S(1)} %copy-done.2, s32[]{:T(128)} %bitcast.8), kind=kLoop, calls=%fused_computation.11 | loop fusion | flops 2041 | bytes 1033 | tf_op jit(solution)/shard_map/local/reduce | solution.py:690
  20.5 1.1 %gather_fusion = bf16[8,96,128]{2,0,1:T(8,128)(2,1)S(1)} fusion(bf16[8,224,128]{2,0,1:T(8,128)(2,1)S(1)} %copy.45, s32[8]{0:T(128)S(1)} %fusion.5), kind=kCustom, calls=%fused_computation | custom fusion | bytes 393280 | tf_op jit(solution)/shard_map/gather | solution.py:681
  22.4 4.7 %all-to-all-start.1 = ((bf16[8,96,128]{2,1,0:T(8,128)(2,1)}), bf16[8,96,128]{2,1,0:T(8,128)(2,1)S(1)}, u32[]{:S(2)}, u32[]{:S(2)}) async-start(bf16[8,96,128]{2,1,0:T(8,128)(2,1)} %copy.49), calls=%async_computation.1 | async-start | bytes 393216 | tf_op jit(solution)/shard_map/all_to_all | solution.py:682
  32.3 15.0 %all_gather.3 = bf16[128,1536]{1,0:T(8,128)(2,1)S(1)} all-gather(bf16[32,1536]{1,0:T(8,128)(2,1)S(1)} %fusion.2), channel_id=1, replica_groups=mesh['req'=8,'head'=4] {'head'}, dimensions={0}, use_global_device_ids=true | all-gather | bytes 491520 | tf_op jit(solution)/shard_map/all_gather | solution.py:687
  47.2 1.5 %collective-permute-start.5 = (bf16[3,12,64,128]{3,2,1,0:T(8,128)(2,1)}, bf16[3,12,64,128]{3,2,1,0:T(8,128)(2,1)}, u32[]{:S(2)}, u32[]{:S(2)}) collective-permute-start(bf16[3,12,64,128]{3,2,1,0:T(8,128)(2,1)} %get-tuple-element.59), channel_id=1, source_target_pairs={{0,24},{4,28},{8,16},{12,20},{16,8},{20,12},{24,0},{28,4},{1,25},{... | collective-permute-start | bytes 1769480 | tf_op jit(solution)/shard_map/ppermute | solution.py:35
  48.8 1.5 %collective-permute-start.6 = (bf16[3,12,64,128]{3,2,1,0:T(8,128)(2,1)}, bf16[3,12,64,128]{3,2,1,0:T(8,128)(2,1)}, u32[]{:S(2)}, u32[]{:S(2)}) collective-permute-start(bf16[3,12,64,128]{3,2,1,0:T(8,128)(2,1)} %get-tuple-element.61), channel_id=1, source_target_pairs={{0,28},{4,24},{8,20},{12,16},{16,12},{20,8},{24,4},{28,0},{1,29},{... | collective-permute-start | bytes 1769480 | tf_op jit(solution)/shard_map/ppermute | solution.py:35
  50.8 5.5 %copy.50 = bf16[192,8,2,768]{3,1,2,0:T(8,128)(2,1)} copy(bf16[192,8,2,768]{3,2,1,0:T(2,128)(2,1)} %bitcast.25) | data formatting | bytes 9437184
  58.5 4.4 %all-to-all-start.2 = ((bf16[8,12,64,128]{3,2,1,0:T(8,128)(2,1)}), bf16[8,12,64,128]{3,2,1,0:T(8,128)(2,1)}, u32[]{:S(2)}, u32[]{:S(2)}) async-start(bf16[8,12,64,128]{3,2,1,0:T(8,128)(2,1)} %constant_dynamic-update-slice_fusion), calls=%async_computation.2 | async-start | bytes 3145728 | tf_op jit(solution)/shard_map/all_to_all | solution.py:719
  63.0 3.9 %convolution_convert_fusion.rows_ref = bf16[128,1536]{1,0:T(8,128)(2,1)} fusion(bf16[128,1536]{1,0:T(8,128)(2,1)S(1)} %all_gather.3, bf16[1536,1536]{1,0:T(8,128)(2,1)} %bitcast.24), kind=kOutput, calls=%fused_computation.1 | convolution fusion | flops 604176384 | bytes 5505024 | tf_op jit(solution)/shard_map/dot_general | solution.py:692
  66.9 4.1 %token_rows.1 = (bf16[768,128]{1,0:T(8,128)(2,1)}, bf16[128,128]{1,0:T(8,128)(2,1)}, bf16[128,128]{1,0:T(8,128)(2,1)}, f32[768,128]{1,0:T(8,128)}, f32[16,128]{1...) custom-call(f32[12]{0:T(128)} %skip_ref.1, ...), custom_call_target="tpu_custom_call" | custom-call | flops 1 | bytes 1 | tf_op jit(solution)/shard_map/token_rows/pallas_call | solution.py:363
  71.0 4.5 %collective-permute-done.6.refs_6_ = bf16[3,12,64,128]{3,2,1,0:T(8,128)(2,1)} collective-permute-done((bf16[3,12,64,128]{3,2,1,0:T(8,128)(2,1)}, bf16[3,12,64,128]{3,2,1,0:T(8,128)(2,1)}, u32[]{:S(2)}, u32[]{:S(2)}) %collective-permute-start.6) | collective-permute-done | bytes 589856 | tf_op jit(solution)/shard_map/ppermute | solution.py:35
  75.5 9.7 %early_pages.1 = (bf16[32,12,64,128]{3,2,1,0:T(8,128)(2,1)}, f32[768,128]{1,0:T(8,128)}) custom-call(s32[33]{0:T(128)} %get-tuple-element.37.new_slots, s32[33]{0:T(128)} %get-tuple-element.49.slot_of, f32[16,128]{1,0:T(8,128)} %get-tuple-element.43.decay_hbm, bf16[768,128]{1,0:T(8,128)(2,1)} %get-tuple-element.50.moved_hbm, ...), custom_call_target="tpu_custom_call" | custom-call | flops 12000000000 | bytes 1 | tf_op jit(solution)/shard_map/early_pages/pallas_call | solution.py:555
  85.2 6.5 %all-to-all-done.2.late = bf16[8,12,64,128]{3,2,1,0:T(8,128)(2,1)} async-done(((bf16[8,12,64,128]{3,2,1,0:T(8,128)(2,1)}), bf16[8,12,64,128]{3,2,1,0:T(8,128)(2,1)}, u32[]{:S(2)}, u32[]{:S(2)}) %all-to-all-start.2) | async-done | bytes 1572896 | tf_op jit(solution)/shard_map/all_to_all | solution.py:719
  91.7 5.1 %hidden_rows.1 = (bf16[32,1664]{1,0:T(8,128)(2,1)}, bf16[32,1664]{1,0:T(8,128)(2,1)}, bf16[32,1664]{1,0:T(8,128)(2,1)}, bf16[32,1664]{1,0:T(8,128)(2,1)}) custom-call(s32[33]{0:T(128)} %get-tuple-element.37.new_slots, f32[16,128]{1,0:T(8,128)} %get-tuple-element.43.decay_hbm, bf16[128,128]{1,0:T(8,128)(2,1)} %get-tuple-element.44.readout_hbm, ...), custom_call_target="tpu_custom_call" | custom-call | flops 1 | bytes 1 | tf_op jit(solution)/shard_map/hidden_rows/pallas_call | solution.py:569
  96.8 2.5 %collective-permute-start.7 = (bf16[32,1664]{1,0:T(8,128)(2,1)}, bf16[32,1664]{1,0:T(8,128)(2,1)}, u32[]{:S(2)}, u32[]{:S(2)}) collective-permute-start(bf16[32,1664]{1,0:T(8,128)(2,1)} %get-tuple-element.63), channel_id=1, source_target_pairs={{0,3},{1,2},{2,1},{3,0},{4,7},{5,6},{6,5},{7,4},{8,11},{9,10},{10,... | collective-permute-start | bytes 319496 | tf_op jit(solution)/shard_map/ppermute | solution.py:35
  99.3 2.0 %collective-permute-start.9 = (bf16[32,1664]{1,0:T(8,128)(2,1)}, bf16[32,1664]{1,0:T(8,128)(2,1)}, u32[]{:S(2)}, u32[]{:S(2)}) collective-permute-start(bf16[32,1664]{1,0:T(8,128)(2,1)} %get-tuple-element.65), channel_id=1, source_target_pairs={{0,1},{1,0},{2,3},{3,2},{4,5},{5,4},{6,7},{7,6},{8,9},{9,8},{10,11... | collective-permute-start | bytes 319496 | tf_op jit(solution)/shard_map/ppermute | solution.py:35
  101.3 3.8 %late_pages.1 = bf16[32,12,64,128]{3,2,1,0:T(8,128)(2,1)} custom-call(s32[33]{0:T(128)} %get-tuple-element.37.new_slots, f32[16,128]{1,0:T(8,128)} %get-tuple-element.43.decay_hbm, bf16[768,128]{1,0:T(8,128)(2,1)} %get-tuple-element.50.moved_hbm, bf16[128,128]{1,0:T(8,128)(2,1)} %get-tuple-element.51.entry_hbm, ...), custom_call_target="tpu_custom_call", output_to_operand_aliasing={{}: (5, {})} | custom-call | flops 1 | bytes 12582912 | tf_op jit(solution)/shard_map/late_pages/pallas_call | solution.py:583
  105.2 4.0 %collective-permute-done.8.refs_1_ = bf16[32,1664]{1,0:T(8,128)(2,1)} collective-permute-done((bf16[32,1664]{1,0:T(8,128)(2,1)}, bf16[32,1664]{1,0:T(8,128)(2,1)}, u32[]{:S(2)}, u32[]{:S(2)}) %collective-permute-start.8) | collective-permute-done | bytes 106528 | tf_op jit(solution)/shard_map/ppermute | solution.py:35
  109.2 1.9 %finish.1 = bf16[32,1536]{1,0:T(8,128)(2,1)} custom-call(bf16[32,1536]{1,0:T(8,128)(2,1)} %tokens_hbm.1, bf16[32,1664]{1,0:T(8,128)(2,1)} %collective-permute-done.7.refs_0_, bf16[32,1664]{1,0:T(8,128)(2,1)} %collective-permute-done.8.refs_1_, bf16[32,1664]{1,0:T(8,128)(2,1)} %collective-permute-done.9.refs_2_, bf16[32,1664]{1,0:T(8,128)(2,1)} %get-tuple-element.66.refs_3_), custom_call_target="tpu_custom_call" | custom-call | flops 1 | bytes 1 | tf_op jit(solution)/shard_map/finish/pallas_call | solution.py:613
  (56 shorter events, 9.2 us)
Async XLA Ops:
  0.6 49.7 %copy-start = (bf16[1536,304]{0,1:T(8,128)(2,1)S(1)}, bf16[1536,304]{0,1:T(8,128)(2,1)}, u32[]{:S(2)}) copy-start(bf16[1536,304]{0,1:T(8,128)(2,1)} %param.23) | copy-start | bytes 2801668
  0.7 15.0 %copy-start.6 = (s32[8]{0:T(128)S(1)}, s32[8]{0:T(128)}, u32[]{:S(2)}) copy-start(s32[8]{0:T(128)} %ids_hbm.1) | copy-start | bytes 100
  0.7 15.0 %copy-start.5 = (s32[8]{0:T(128)S(1)}, s32[8]{0:T(128)}, u32[]{:S(2)}) copy-start(s32[8]{0:T(128)} %dest_hbm.1) | copy-start | bytes 100
  0.7 18.4 %copy-start.2 = (s32[256]{0:T(256)S(1)}, s32[256]{0:T(256)}, u32[]{:S(2)}) copy-start(s32[256]{0:T(256)} %reorder_hbm.1) | copy-start | bytes 3076
  0.7 16.7 %copy-start.1 = (f32[1536]{0:T(1024)S(1)}, f32[1536]{0:T(1024)}, u32[]{:S(2)}) copy-start(f32[1536]{0:T(1024)} %param.21) | copy-start | bytes 18436
  0.7 26.4 %copy-start.8 = (f32[12]{0:T(128)S(1)}, f32[12]{0:T(128)}, u32[]{:S(2)}) copy-start(f32[12]{0:T(128)} %param.29) | copy-start | bytes 148
  0.7 26.4 %copy-start.9 = (f32[12]{0:T(128)S(1)}, f32[12]{0:T(128)}, u32[]{:S(2)}) copy-start(f32[12]{0:T(128)} %param.28) | copy-start | bytes 148
  0.7 29.6 %copy-start.7 = (s32[32]{0:T(128)S(1)}, s32[32]{0:T(128)}, u32[]{:S(2)}) copy-start(s32[32]{0:T(128)} %param.36) | copy-start | bytes 388
  0.7 30.3 %copy-start.3 = (f32[768]{0:T(1024)S(1)}, f32[768]{0:T(1024)}, u32[]{:S(2)}) copy-start(f32[768]{0:T(1024)} %param.25) | copy-start | bytes 9220
  0.7 30.9 %copy-start.4 = (f32[768]{0:T(1024)S(1)}, f32[768]{0:T(1024)}, u32[]{:S(2)}) copy-start(f32[768]{0:T(1024)} %param.31) | copy-start | bytes 9220
  7.9 12.4 %all-to-all-start = ((bf16[8,224,128]{2,1,0:T(8,128)(2,1)}), bf16[8,224,128]{2,1,0:T(8,128)(2,1)S(1)}, u32[]{:S(2)}, u32[]{:S(2)}) async-start(bf16[8,224,128]{2,1,0:T(8,128)(2,1)} %get-tuple-element.39), calls=%async_computation | async-start | bytes 917504 | tf_op jit(solution)/shard_map/all_to_all | solution.py:675
  12.2 36.5 %collective-permute-start.1 = (bf16[3,12,64,128]{3,2,1,0:T(8,128)(2,1)}, bf16[3,12,64,128]{3,2,1,0:T(8,128)(2,1)S(1)}, u32[]{:S(2)}, u32[]{:S(2)}) collective-permute-start(bf16[3,12,64,128]{3,2,1,0:T(8,128)(2,1)} %get-tuple-element.54), channel_id=1, source_target_pairs={{0,8},{4,12},{8,0},{12,4},{16,24},{20,28},{24,16},{28,20},{1,9},{5... | collective-permute-start | bytes 1769480 | tf_op jit(solution)/shard_map/ppermute | solution.py:35
  12.2 36.6 %collective-permute-start.2 = (bf16[3,12,64,128]{3,2,1,0:T(8,128)(2,1)}, bf16[3,12,64,128]{3,2,1,0:T(8,128)(2,1)S(1)}, u32[]{:S(2)}, u32[]{:S(2)}) collective-permute-start(bf16[3,12,64,128]{3,2,1,0:T(8,128)(2,1)} %get-tuple-element.55), channel_id=1, source_target_pairs={{0,12},{4,8},{8,4},{12,0},{16,28},{20,24},{24,20},{28,16},{1,13},{... | collective-permute-start | bytes 1769480 | tf_op jit(solution)/shard_map/ppermute | solution.py:35
  13.7 57.3 %collective-permute-start.3 = (bf16[3,12,64,128]{3,2,1,0:T(8,128)(2,1)}, bf16[3,12,64,128]{3,2,1,0:T(8,128)(2,1)}, u32[]{:S(2)}, u32[]{:S(2)}) collective-permute-start(bf16[3,12,64,128]{3,2,1,0:T(8,128)(2,1)} %get-tuple-element.56), channel_id=1, source_target_pairs={{0,16},{4,20},{8,24},{12,28},{16,0},{20,4},{24,8},{28,12},{1,17},{... | collective-permute-start | bytes 1769480 | tf_op jit(solution)/shard_map/ppermute | solution.py:35
  15.2 55.8 %collective-permute-start.4 = (bf16[3,12,64,128]{3,2,1,0:T(8,128)(2,1)}, bf16[3,12,64,128]{3,2,1,0:T(8,128)(2,1)}, u32[]{:S(2)}, u32[]{:S(2)}) collective-permute-start(bf16[3,12,64,128]{3,2,1,0:T(8,128)(2,1)} %get-tuple-element.57), channel_id=1, source_target_pairs={{0,20},{4,16},{8,28},{12,24},{16,4},{20,0},{24,12},{28,8},{1,21},{... | collective-permute-start | bytes 1769480 | tf_op jit(solution)/shard_map/ppermute | solution.py:35
  22.4 26.4 %all-to-all-start.1 = ((bf16[8,96,128]{2,1,0:T(8,128)(2,1)}), bf16[8,96,128]{2,1,0:T(8,128)(2,1)S(1)}, u32[]{:S(2)}, u32[]{:S(2)}) async-start(bf16[8,96,128]{2,1,0:T(8,128)(2,1)} %copy.49), calls=%async_computation.1 | async-start | bytes 393216 | tf_op jit(solution)/shard_map/all_to_all | solution.py:682
  47.2 23.7 %collective-permute-start.5 = (bf16[3,12,64,128]{3,2,1,0:T(8,128)(2,1)}, bf16[3,12,64,128]{3,2,1,0:T(8,128)(2,1)}, u32[]{:S(2)}, u32[]{:S(2)}) collective-permute-start(bf16[3,12,64,128]{3,2,1,0:T(8,128)(2,1)} %get-tuple-element.59), channel_id=1, source_target_pairs={{0,24},{4,28},{8,16},{12,20},{16,8},{20,12},{24,0},{28,4},{1,25},{... | collective-permute-start | bytes 1769480 | tf_op jit(solution)/shard_map/ppermute | solution.py:35
  48.7 7.5 %copy-start.10 = (bf16[3,12,64,128]{3,2,1,0:T(8,128)(2,1)}, bf16[3,12,64,128]{3,2,1,0:T(8,128)(2,1)S(1)}, u32[]{:S(2)}) copy-start(bf16[3,12,64,128]{3,2,1,0:T(8,128)(2,1)S(1)} %collective-permute-done.1.refs_1_) | copy-start | bytes 1769476
  48.7 22.3 %collective-permute-start = (bf16[3,12,64,128]{3,2,1,0:T(8,128)(2,1)}, bf16[3,12,64,128]{3,2,1,0:T(8,128)(2,1)}, u32[]{:S(2)}, u32[]{:S(2)}) collective-permute-start(bf16[3,12,64,128]{3,2,1,0:T(8,128)(2,1)} %get-tuple-element.53), channel_id=1, source_target_pairs={{0,4},{4,0},{8,12},{12,8},{16,20},{20,16},{24,28},{28,24},{1,5},{5... | collective-permute-start | bytes 1769480 | tf_op jit(solution)/shard_map/ppermute | solution.py:35
  48.8 26.7 %collective-permute-start.6 = (bf16[3,12,64,128]{3,2,1,0:T(8,128)(2,1)}, bf16[3,12,64,128]{3,2,1,0:T(8,128)(2,1)}, u32[]{:S(2)}, u32[]{:S(2)}) collective-permute-start(bf16[3,12,64,128]{3,2,1,0:T(8,128)(2,1)} %get-tuple-element.61), channel_id=1, source_target_pairs={{0,28},{4,24},{8,20},{12,16},{16,12},{20,8},{24,4},{28,0},{1,29},{... | collective-permute-start | bytes 1769480 | tf_op jit(solution)/shard_map/ppermute | solution.py:35
  58.5 33.2 %all-to-all-start.2 = ((bf16[8,12,64,128]{3,2,1,0:T(8,128)(2,1)}), bf16[8,12,64,128]{3,2,1,0:T(8,128)(2,1)}, u32[]{:S(2)}, u32[]{:S(2)}) async-start(bf16[8,12,64,128]{3,2,1,0:T(8,128)(2,1)} %constant_dynamic-update-slice_fusion), calls=%async_computation.2 | async-start | bytes 3145728 | tf_op jit(solution)/shard_map/all_to_all | solution.py:719
  96.8 8.3 %collective-permute-start.7 = (bf16[32,1664]{1,0:T(8,128)(2,1)}, bf16[32,1664]{1,0:T(8,128)(2,1)}, u32[]{:S(2)}, u32[]{:S(2)}) collective-permute-start(bf16[32,1664]{1,0:T(8,128)(2,1)} %get-tuple-element.63), channel_id=1, source_target_pairs={{0,3},{1,2},{2,1},{3,0},{4,7},{5,6},{6,5},{7,4},{8,11},{9,10},{10,... | collective-permute-start | bytes 319496 | tf_op jit(solution)/shard_map/ppermute | solution.py:35
  99.3 9.9 %collective-permute-start.8 = (bf16[32,1664]{1,0:T(8,128)(2,1)}, bf16[32,1664]{1,0:T(8,128)(2,1)}, u32[]{:S(2)}, u32[]{:S(2)}) collective-permute-start(bf16[32,1664]{1,0:T(8,128)(2,1)} %get-tuple-element.64), channel_id=1, source_target_pairs={{0,2},{1,3},{2,0},{3,1},{4,6},{5,7},{6,4},{7,5},{8,10},{9,11},{10,... | collective-permute-start | bytes 319496 | tf_op jit(solution)/shard_map/ppermute | solution.py:35
  99.3 9.9 %collective-permute-start.9 = (bf16[32,1664]{1,0:T(8,128)(2,1)}, bf16[32,1664]{1,0:T(8,128)(2,1)}, u32[]{:S(2)}, u32[]{:S(2)}) collective-permute-start(bf16[32,1664]{1,0:T(8,128)(2,1)} %get-tuple-element.65), channel_id=1, source_target_pairs={{0,1},{1,0},{2,3},{3,2},{4,5},{5,4},{6,7},{7,6},{8,9},{9,8},{10,11... | collective-permute-start | bytes 319496 | tf_op jit(solution)/shard_map/ppermute | solution.py:35
  (1 other events, 7.4 us)
